TPU v7x, 256 devices: a whole 4x4x8 slice. The times are simulated.
256 devices in a mesh: tile: 64 (over z, y, core), group: 4 (over x).
Axes of the slice: x: 4, y: 4, z: 8, core: 2. Of those that a mesh axis runs over, the one named last changes fastest.
Arguments:
- features: bfloat16 [64, 8, 96, 16, 128], P('tile', 'group'), may hold values from -6 to 6
- tile_list: int32 [64], replicated, may hold values from 0 to 63, as said below
- neighbours: int32 [64, 8], replicated, may hold values from -1 to 63, as said below
- clip_frames: int32 [16], replicated, may hold values from 1 to 8, as said below
- gain_one: float32 [96], replicated, may hold values from 0.1 to 1.9
- weight_one: bfloat16 [3, 3, 3, 96, 96], replicated, may hold values from -0.125 to 0.125
- bias_one: float32 [96], replicated, may hold values from -3 to 3
- gain_two: float32 [96], replicated, may hold values from 0.1 to 1.9
- weight_two: bfloat16 [3, 3, 3, 96, 96], replicated, may hold values from -0.125 to 0.125
- bias_two: float32 [96], replicated, may hold values from -3 to 3
Outputs:
- decoded: bfloat16 [64, 8, 96, 16, 128], P('tile', 'group')
Inputs may be any that keep to these rules, and one draw needn't show every extreme that they name: `tile_list`: each tile number appears once. Tiles of clip k are numbers k * 4 to (k + 1) * 4 - 1, laid on a 2 x 2 grid in an order drawn from the seed; the table lists each tile's grid neighbours within its clip and -1 past the clip's border. `clip_frames`: some clip has all 8 frames.
All inputs are finite; a program needn't handle non-finite values.
Results may differ from a plain program's by a relative error of at most 0.0034.
Values may be sent and summed in bfloat16 or wider, within the bound.
No kernel may reach another device: no remote copies, remote signals or barrier semaphores. Data moves between devices by JAX's collectives and lax.ppermute only.
A program may use at most 64 MiB of HBM per device.

v0:
```python
import functools

import jax
import jax.numpy as jnp
from jax import lax
from jax.experimental import pallas as pl
from jax.experimental.pallas import tpu as pltpu
from jax.sharding import PartitionSpec as P

NZ, NY, NCORE, NX = 8, 4, 2, 4
TILES = NZ * NY * NCORE
TPC = 4
C, H, W, F = 96, 16, 128, 2
REC = 5
KF = 9 * C + 32
T_LIST = 2
T_NEAR = T_LIST + TILES
T_CLIP = T_NEAR + TILES * 8
BF, F32 = jnp.bfloat16, jnp.float32

SMEM = pl.BlockSpec(memory_space=pltpu.SMEM)
VMEM = pl.BlockSpec(memory_space=pltpu.VMEM)
ANY = pl.BlockSpec(memory_space=pl.ANY)


def params(mib):
    return pltpu.CompilerParams(vmem_limit_bytes=mib * 1024 * 1024)


def sides(table):
    tile = table[T_LIST + table[0]]
    up = table[T_NEAR + tile * 8 + 1] >= 0
    left = table[T_NEAR + tile * 8 + 3] >= 0
    return up, left


def norm_silu(values, gain):
    inverse = lax.rsqrt(jnp.mean(values * values, axis=0, keepdims=True) + 1e-06)
    scaled = values * inverse * gain
    return scaled / (1.0 + jnp.exp(-scaled))


def rotate(values, by):
    return pltpu.roll(values, by, 1)


def lanes(rows):
    return lax.broadcasted_iota(jnp.int32, (rows, W), 1)


def write_record(features, up, left, out, base):
    row = jnp.where(up, 0, H - 2)
    for f in range(F):
        for r in range(2):
            out[base + 2 * f + r] = features[f, row + r]
    turn = jnp.where(left, 0, 2)
    lane = lanes(C)
    columns = jnp.zeros((C, W), F32)
    for f in range(F):
        for y in range(H):
            at = f * 32 + 2 * y
            moved = rotate(features[f, y].astype(F32), at + turn)
            columns = jnp.where(lane // 2 == at // 2, moved, columns)
    out[base + 4] = jnp.where(lane < 64, columns, rotate(columns, 64)).astype(BF)


def record_kernel(table, features, out):
    up, left = sides(table)
    write_record(features, up, left, out, 0)


def weights_kernel(one, two, out):
    same = lax.broadcasted_iota(jnp.int32, (C, C), 0) == lax.broadcasted_iota(jnp.int32, (C, C), 1)
    same = same.astype(F32).astype(BF)
    for n, source in enumerate((one, two)):
        out[n, 0:C, 3 * KF :] = jnp.zeros((C, KF), BF)
        out[n, C:, 0:KF] = jnp.zeros((C, KF), BF)
        for t in range(3):
            flipped = lax.dot_general(same, source[t], (((1,), (1,)), ((), ())), preferred_element_type=F32)
            flipped = jnp.concatenate([flipped.astype(BF), jnp.zeros((C, KF - 9 * C), BF)], axis=1)
            out[n, 0:C, t * KF : (t + 1) * KF] = flipped
            out[n, C:, (t + 1) * KF : (t + 2) * KF] = flipped


def select_kernel(table, t0, t1, t2, t3, _, mine, other, inverse):
    held = (t0, t1, t2, t3)
    me = table[0]
    z, y, c = me // (NY * NCORE), (me // NCORE) % NY, me % NCORE

    def invert(i, _):
        inverse[table[T_LIST + i]] = i
        return 0

    lax.fori_loop(0, TILES, invert, 0)
    mine[...] = jnp.zeros_like(mine)
    other[...] = jnp.zeros_like(other)

    def place(tile):
        slot = inverse[jnp.maximum(tile, 0)]
        zs, ys, cs = slot // (NY * NCORE), (slot // NCORE) % NY, slot % NCORE
        away = jnp.where(c == 0, z - zs, zs - z)
        away = jnp.where(away < 0, away + NZ, away)
        label = jnp.where(cs == c, 0, 1)
        fits = (tile >= 0) & (ys == y) & ((away >= 1) & (away <= 3) | (label == 0) & ((away == 0) | (away == 4)))
        which = jnp.where(fits, jnp.minimum(away, 3), -1)
        return which, jnp.where(away == 4, 2, label)

    low = lanes(C) < 64
    for same, out in ((True, mine), (False, other)):
        core = c if same else 1 - c

        def dest(yd, _):
            near = T_NEAR + table[T_LIST + z * NY * NCORE + yd * NCORE + core] * 8
            vertical = place(jnp.maximum(table[near + 1], table[near + 6]))
            horizontal = place(jnp.maximum(table[near + 3], table[near + 4]))
            diagonal = place(
                jnp.maximum(
                    jnp.maximum(table[near], table[near + 2]), jnp.maximum(table[near + 5], table[near + 7])
                )
            )
            for k, ref in enumerate(held):

                @pl.when(vertical[0] == k)
                def _():
                    out[yd, 0:4] = ref[vertical[1], 0:4]

                @pl.when(horizontal[0] == k)
                def _():
                    out[yd, 4] = jnp.where(low, ref[horizontal[1], 4], out[yd, 4])

                @pl.when(diagonal[0] == k)
                def _():
                    out[yd, 4] = jnp.where(low, out[yd, 4], ref[diagonal[1], 4])

            return 0

        lax.fori_loop(0, NY, dest, 0)


def combine_kernel(table, mine, arrived, own, one, two, three):
    y = (table[0] // NCORE) % NY
    for by, out in enumerate((own, one, two, three)):
        to = (y + by) % NY
        out[...] = (mine[to].astype(F32) + arrived[to].astype(F32)).astype(BF)


def three_shifts(center, at_left, at_right):
    lane = lanes(C)
    before = jnp.where(lane == 0, at_left, rotate(center, 1))
    after = jnp.where(lane == W - 1, at_right, rotate(center, W - 1))
    return before.astype(BF), center.astype(BF), after.astype(BF)


def put_window(windows, place, values):
    for k, value in enumerate(values):
        windows[(*place, slice(k * C, (k + 1) * C))] = value


def stack(parts):
    full = []
    for part in parts:
        full += [part, jnp.zeros((KF - 9 * C, part.shape[1]), BF)]
    return jnp.concatenate(full, axis=0)


def row_parts(windows, base, oy, count):
    return [
        jnp.concatenate([windows[base + fr, pl.ds(oy + r, 3)].reshape(9 * C, W) for r in range(count)], axis=1)
        for fr in range(2 * F)
    ]


def product(weights, parts):
    return jnp.dot(weights[...], stack(parts), preferred_element_type=F32)


def inner_first_kernel(table, own, prev, weights, vectors, _, out, windows):
    up, left = sides(table)
    bias, gain_one, gain_two = vectors[:, 0:1], vectors[:, 1:2], vectors[:, 2:3]
    write_record(prev, up, left, out, F * H)
    zero_ends(windows)
    for fr in range(2 * F):
        source, f = (prev, fr) if fr < F else (own, fr - F)

        def row_step(y, _):
            center = norm_silu(source[f, y].astype(F32), gain_one)
            put_window(windows, (fr, y + 1), three_shifts(center, 0.0, 0.0))
            return 0

        lax.fori_loop(0, H, row_step, 0, unroll=4)

    border_row, border_lane = jnp.where(up, 0, H - 1), jnp.where(left, 0, W - 1)
    lane = lanes(C)

    def rows_step(n, _):
        acc = product(weights.at[0], row_parts(windows, 0, 2 * n, 2))
        for f in range(F):
            value = norm_silu(acc[f * C : (f + 1) * C] + bias, gain_two)
            for r in range(2):
                y = 2 * n + r
                border = (lane == border_lane) | (y == border_row)
                out[f * H + y] = jnp.where(border, 0.0, value[:, r * W : (r + 1) * W]).astype(BF)
        return 0

    lax.fori_loop(0, H // 2, rows_step, 0)


def inner_second_kernel(own, second_own, second_prev, weights, vectors, _, out, windows):
    bias = vectors[:, 3:4]
    zero_ends(windows)
    for fr in range(2 * F):
        source, f = (second_prev, fr) if fr < F else (second_own, fr - F)

        def row_step(y, _):
            center = source[f * H + y].astype(F32)
            put_window(windows, (fr, y + 1), three_shifts(center, 0.0, 0.0))
            return 0

        lax.fori_loop(0, H, row_step, 0, unroll=4)

    def rows_step(n, _):
        acc = product(weights.at[1], row_parts(windows, 0, 2 * n, 2))
        for f in range(F):
            value = acc[f * C : (f + 1) * C] + bias
            for r in range(2):
                y = 2 * n + r
                out[f, y] = own[f, y].astype(F32) + value[:, r * W : (r + 1) * W]
        return 0

    lax.fori_loop(0, H // 2, rows_step, 0)


def zero_ends(windows):
    for fr in range(2 * F):
        for yy in (0, H + 1):
            windows[fr, yy] = jnp.zeros((3 * C, W), BF)


def band_parts(band, columns, base):
    parts = row_parts(band, base, 0, 2)
    for fr in range(2 * F):
        beside = [
            jnp.concatenate([columns[base + fr, j + dx, dy] for dy in range(3) for dx in range(3)], axis=0)
            for j in range(2)
        ]
        parts[fr] = jnp.concatenate([parts[fr]] + beside, axis=1)
    return parts


def put_column(columns, fr, k, value):
    columns[fr, k, 0] = rotate(value, 1).astype(BF)
    columns[fr, k, 1] = value.astype(BF)
    columns[fr, k, 2] = rotate(value, W - 1).astype(BF)


def outer_kernel(
    table, inner, record0, second_own, second_prev, halo0, halo1, halo2, weights, vectors,
    out, band1, columns1, band2, columns2
):
    up, left = sides(table)
    bias1, gain1, gain2 = vectors[:, 0:1], vectors[:, 1:2], vectors[:, 2:3]
    sources = ((second_prev, F * H, halo2), (second_own, F * H, halo1), (record0, 0, halo0))
    lane = lanes(C)

    src = lax.broadcasted_iota(jnp.int32, (W, 2 * W), 0)
    dst2 = lax.broadcasted_iota(jnp.int32, (W, 2 * W), 1)
    dst, col = dst2 % W, dst2 // W
    none = -1000
    body = jnp.where((dst >= 2) & (dst < H + 2), 2 * (dst - 2), none)
    above = jnp.where(dst < 2, 64 + 2 * (H - 2 + dst), none)
    below = jnp.where((dst >= H + 2) & (dst < H + 4), 64 + 2 * (dst - H - 2), none)
    corner = jnp.where(up, above, below)
    past = jnp.where(up, 0, H + 2)
    first_col = jnp.where(left, 0, W - 2)
    for fr in range(3 * F):
        f = fr % F
        record, base, halo = sources[fr // F]
        pick = (src == jnp.maximum(body, corner) + f * 32 + col).astype(F32).astype(BF)
        theirs = norm_silu(jnp.dot(halo[4], pick, preferred_element_type=F32), gain1)
        picks = [(src == body + f * 32 + col).astype(F32).astype(BF)]
        for r in range(2):
            picks.append(((src == first_col + col) & (dst == past + r)).astype(F32).astype(BF))
        mine = jnp.concatenate([record[base + 4], halo[2 * f], halo[2 * f + 1]], axis=1)
        ours = norm_silu(jnp.dot(mine, jnp.concatenate(picks, axis=0), preferred_element_type=F32), gain1)
        low, high = jnp.where(left, theirs, ours), jnp.where(left, ours, theirs)
        for k in range(4):
            put_column(columns1, fr, k, (low if k < 2 else high)[:, (k % 2) * W : (k % 2 + 1) * W])
        near = jnp.where(left, theirs[:, W:], theirs[:, :W])
        for r in range(4):
            other, self = halo[2 * f + r % 2], record[base + 2 * f + r % 2]
            raw = jnp.where(up, other if r < 2 else self, self if r < 2 else other)
            at = jnp.where(up, r, H + r)
            moved = rotate(near, jnp.where(left, (W - at) % W, W - 1 - at))
            center = norm_silu(raw.astype(F32), gain1)
            put_window(
                band1, (fr, r), three_shifts(center, jnp.where(left, moved, 0.0), jnp.where(left, 0.0, moved))
            )

    inside = (lane >= jnp.where(up, 3, 2)) & (lane < jnp.where(up, H + 2, H + 1))
    row_at, col_at = jnp.where(up, 0, 2), jnp.where(left, 0, 2)
    for p in range(2):
        acc = product(weights.at[0], band_parts(band1, columns1, F * p))
        for f in range(F):
            s = F * p + f
            value = norm_silu(acc[f * C : (f + 1) * C] + bias1, gain2)
            if p == 0:
                value = jnp.where(table[1] > 0, value, 0.0)
            beside = [value[:, 2 * W : 3 * W], value[:, 3 * W :]]
            near = jnp.where(left, beside[0], beside[1])
            for j in range(2):
                at = jnp.where(up, 1 + j, H + 1 + j)
                moved = rotate(near, jnp.where(left, W - at, W - 1 - at))
                center = value[:, j * W : (j + 1) * W]
                put_window(
                    band2,
                    (s, row_at + j),
                    three_shifts(center, jnp.where(left, moved, 0.0), jnp.where(left, 0.0, moved)),
                )
                band2[s, 2 - row_at + j] = jnp.zeros((3 * C, W), BF)
                put_column(columns2, s, col_at + j, jnp.where(inside, beside[j], 0.0))
                columns2[s, 2 - col_at + j] = jnp.zeros((3, C, W), BF)

    length = table[T_CLIP + table[T_LIST + table[0]] // TPC]
    start = table[1] * F
    acc = product(weights.at[1], band_parts(band2, columns2, 0))
    for f in range(F):
        value = acc[f * C : (f + 1) * C]
        for y in range(H):
            total = inner[f, y]
            for j in range(2):
                at = first_col + j
                moved = rotate(value[:, (2 + j) * W : (3 + j) * W], (at + W - 2 - y) % W)
                total = total + jnp.where(lane == at, moved, 0.0)
            if y < 2:
                total = total + jnp.where(up, value[:, y * W : (y + 1) * W], 0.0)
            if y >= H - 2:
                j = y - (H - 2)
                total = total + jnp.where(up, 0.0, value[:, j * W : (j + 1) * W])
            out[f, y] = jnp.where(start + f < length, total, 0.0).astype(BF)


def call(kernel, outs, kinds, scratch=(), mib=8, flops=0):
    single = not isinstance(outs, (list, tuple))
    return pl.pallas_call(
        kernel,
        out_shape=outs,
        in_specs=[{"s": SMEM, "v": VMEM, "-": ANY}[kind] for kind in kinds],
        out_specs=VMEM if single else [VMEM] * len(outs),
        scratch_shapes=list(scratch),
        compiler_params=params(mib),
        cost_estimate=pl.CostEstimate(flops=flops, bytes_accessed=2**20, transcendentals=0),
    )


def shape(*extent):
    return jax.ShapeDtypeStruct(extent, BF)


def place_of(z, y, c):
    return (z % NZ) * NY * NCORE + (y % NY) * NCORE + c


def pairs(move):
    return [
        (place_of(z, y, c), place_of(*move(z, y, c))) for z in range(NZ) for y in range(NY) for c in range(NCORE)
    ]


def send(array, move):
    return lax.ppermute(array, "tile", pairs(move))


def later(array, by=1):
    return lax.ppermute(array, "group", [(i, i + by) for i in range(NX - by)])


def spread(record):
    along = lambda by: lambda z, y, c: (z + (by if c == 0 else -by), y, c)
    t0 = jnp.stack([record, send(record, swap)])
    t1 = send(t0, along(1))
    t2 = send(t0, along(2))
    t3 = send(jnp.concatenate([t1, t2[:1]], axis=0), along(2))
    return t0, t1, t2, t3


def swap(z, y, c):
    return z, y, 1 - c


def deliver(table, held, after):
    mine, other = call(
        select_kernel, [shape(NY, REC, C, W)] * 2, "svvvv-", [pltpu.SMEM((TILES,), jnp.int32)]
    )(table, *held, after)
    arrived = send(other, swap)
    own, one, two, three = call(combine_kernel, [shape(REC, C, W)] * 4, "svv")(table, mine, arrived)
    total = own.astype(F32)
    for by, part in ((2, two), (1, one), (3, three)):
        total = total + send(part, lambda z, y, c, by=by: (z, y + by, c)).astype(F32)
    return total.astype(BF)


def per_device(
    features, tile_list, neighbours, clip_frames, gain_one, weight_one, bias_one, gain_two, weight_two, bias_two
):
    table = jnp.concatenate(
        [
            jnp.stack([lax.axis_index("tile"), lax.axis_index("group")]).astype(jnp.int32),
            tile_list,
            neighbours.reshape(-1),
            clip_frames,
        ]
    )
    vectors = jnp.stack([bias_one, gain_one, gain_two, bias_two], axis=1)
    own = features[0].transpose(0, 2, 1, 3)
    prev = later(own)
    record = call(record_kernel, shape(REC, C, W), "sv")(table, own)
    weights = call(weights_kernel, shape(2, 2 * C, 4 * KF), "vv", mib=16)(
        weight_one.reshape(3, 9 * C, C), weight_two.reshape(3, 9 * C, C)
    )
    held = spread(record)
    window = pltpu.VMEM((2 * F, H + 2, 3 * C, W), BF)
    second = call(
        inner_first_kernel, shape(F * H + REC, C, W), "svvvv-", [window], 24, 8 * 10**9
    )(table, own, prev, weights, vectors, held[1])
    second_prev = later(second)
    halo = deliver(table, held, second)
    halo1, halo2 = later(halo), later(halo, 2)
    inner = call(
        inner_second_kernel, jax.ShapeDtypeStruct((F, H, C, W), F32), "vvvvv-", [window], 24, 8 * 10**9
    )(own, second, second_prev, weights, vectors, halo)
    out = call(
        outer_kernel,
        shape(F, H, C, W),
        "s" + "v" * 9,
        [
            pltpu.VMEM((3 * F, 4, 3 * C, W), BF),
            pltpu.VMEM((3 * F, 4, 3, C, W), BF),
            pltpu.VMEM((2 * F, 4, 3 * C, W), BF),
            pltpu.VMEM((2 * F, 4, 3, C, W), BF),
        ],
        24,
        4 * 10**9,
    )(table, inner, record, second, second_prev, halo, halo1, halo2, weights, vectors)
    return out.transpose(0, 2, 1, 3)[None]


def solution(mesh):
    placed = (P("tile", "group", None, None, None), P(), P(), P(), P(), P(), P(), P(), P(), P())
    return jax.shard_map(
        per_device,
        mesh=mesh,
        in_specs=placed,
        out_specs=P("tile", "group", None, None, None),
        check_vma=False,
    )
```

profile of v0, /device:TPU:44, one launch (start us, length us, event | category | flops | bytes accessed | tf_op | source)
XLA Modules:
  0.0 76.0 jit_solution(16339006231773648589)
XLA Ops:
  0.0 1.4 %copy.31 = bf16[1,2,96,16,128]{4,2,3,1,0:T(8,128)(2,1)S(1)} copy(bf16[1,2,96,16,128]{4,3,2,1,0:T(8,128)(2,1)} %param.10) | data formatting | bytes 1572864 | tf_op args[0]
  1.5 3.1 %collective-permute-start = (bf16[2,16,96,128]{3,2,1,0:T(8,128)(2,1)S(1)}, bf16[2,16,96,128]{3,2,1,0:T(8,128)(2,1)}, u32[]{:S(2)}, u32[]{:S(2)}) collective-permute-start(bf16[2,16,96,128]{3,2,1,0:T(8,128)(2,1)S(1)} %bitcast.18), channel_id=1, source_target_pairs={{0,1},{1,2},{2,3},{4,5},{5,6},{6,7},{8,9},{9,10},{10,11},{12,13},{... | collective-permute-start | bytes 2359304 | tf_op jit(solution)/shard_map/ppermute | solution.py:374
  4.6 0.8 %copy.24 = s32[64,8]{1,0:T(8,128)S(1)} copy(s32[64,8]{0,1:T(8,128)} %param.12) | data formatting | bytes 4096 | tf_op args[2]
  5.4 0.1 reshape.9
  5.5 0.8 concatenate.6.table
  6.2 0.9 %shard_map.101.record0 = bf16[5,96,128]{2,1,0:T(8,128)(2,1)S(1)} custom-call(s32[594]{0:T(1024)S(1)} %concatenate.6.table, bf16[2,16,96,128]{3,2,1,0:T(8,128)(2,1)S(1)} %bitcast.19), custom_call_target="tpu_custom_call" | custom-call | bytes 1048576 | tf_op jit(solution)/shard_map/pallas_call | solution.py:416
  7.1 0.1 collective-permute-start.1
  7.2 1.3 %collective-permute-done.1 = bf16[5,96,128]{2,1,0:T(8,128)(2,1)S(1)} collective-permute-done((bf16[5,96,128]{2,1,0:T(8,128)(2,1)S(1)}, bf16[5,96,128]{2,1,0:T(8,128)(2,1)S(1)}, u32[]{:S(2)}, u32[]{:S(2)}) %collective-permute-start.1) | collective-permute-done | bytes 122912 | tf_op jit(solution)/shard_map/ppermute | solution.py:370
  8.6 3.3 %collective-permute-start.4 = (bf16[2,5,96,128]{3,2,1,0:T(8,128)(2,1)S(1)}, bf16[2,5,96,128]{3,2,1,0:T(8,128)(2,1)S(1)}, u32[]{:S(2)}, u32[]{:S(2)}) collective-permute-start(bf16[2,5,96,128]{3,2,1,0:T(8,128)(2,1)S(1)} %pad_maximum_fusion.1.t0), channel_id=1, source_target_pairs={{0,64},{4,196},{8,72},{12,204},{16,80},{20,212},{24,88},{28,220},{... | collective-permute-start | bytes 737288 | tf_op jit(solution)/shard_map/ppermute | solution.py:370
  11.9 3.1 %collective-permute-start.2 = (bf16[2,5,96,128]{3,2,1,0:T(8,128)(2,1)S(1)}, bf16[2,5,96,128]{3,2,1,0:T(8,128)(2,1)S(1)}, u32[]{:S(2)}, u32[]{:S(2)}) collective-permute-start(bf16[2,5,96,128]{3,2,1,0:T(8,128)(2,1)S(1)} %pad_maximum_fusion.1.t0), channel_id=1, source_target_pairs={{0,32},{4,228},{8,40},{12,236},{16,48},{20,244},{24,56},{28,252},{... | collective-permute-start | bytes 737288 | tf_op jit(solution)/shard_map/ppermute | solution.py:370
  15.1 0.1 copy.26.vectors
  15.2 0.6 shard_map.100.weights
  15.8 5.2 %collective-permute-done.4.t2 = bf16[2,5,96,128]{3,2,1,0:T(8,128)(2,1)S(1)} collective-permute-done((bf16[2,5,96,128]{3,2,1,0:T(8,128)(2,1)S(1)}, bf16[2,5,96,128]{3,2,1,0:T(8,128)(2,1)S(1)}, u32[]{:S(2)}, u32[]{:S(2)}) %collective-permute-start.4) | collective-permute-done | bytes 245792 | tf_op jit(solution)/shard_map/ppermute | solution.py:370
  21.0 0.5 collective-permute-done.2._.t1
  21.5 4.5 %collective-permute-start.5 = (bf16[3,5,96,128]{3,2,1,0:T(8,128)(2,1)S(1)}, bf16[3,5,96,128]{3,2,1,0:T(8,128)(2,1)S(1)}, u32[]{:S(2)}, u32[]{:S(2)}) collective-permute-start(bf16[3,5,96,128]{3,2,1,0:T(8,128)(2,1)S(1)} %pad_maximum_fusion), channel_id=1, source_target_pairs={{0,64},{4,196},{8,72},{12,204},{16,80},{20,212},{24,88},{28,220},{... | collective-permute-start | bytes 1105928 | tf_op jit(solution)/shard_map/ppermute | solution.py:370
  26.0 9.9 %shard_map.102._.second_own = bf16[37,96,128]{2,1,0:T(8,128)(2,1)S(1)} custom-call(s32[594]{0:T(1024)S(1)} %concatenate.6.table, bf16[2,16,96,128]{3,2,1,0:T(8,128)(2,1)S(1)} %bitcast.20, bf16[2,16,96,128]{3,2,1,0:T(8,128)(2,1)} %collective-permute-done.prev, bf16[2,192,3584]{2,1,0:T(8,128)(2,1)S(1)} %shard_map.100.weights, f32[96,4]{1,0:T(8,128)S(1)} %copy.26.vectors, ...), custom_call_target="tpu_custom_call" | custom-call | flops 8000000000 | bytes 1048576 | tf_op jit(solution)/shard_map/pallas_call | solution.py:422
  35.9 1.9 %collective-permute-start.3 = (bf16[37,96,128]{2,1,0:T(8,128)(2,1)S(1)}, bf16[37,96,128]{2,1,0:T(8,128)(2,1)S(1)}, u32[]{:S(2)}, u32[]{:S(2)}) collective-permute-start(bf16[37,96,128]{2,1,0:T(8,128)(2,1)S(1)} %shard_map.102._.second_own), channel_id=1, source_target_pairs={{0,1},{1,2},{2,3},{4,5},{5,6},{6,7},{8,9},{9,10},{10,11},{12,13},{... | collective-permute-start | bytes 2727944 | tf_op jit(solution)/shard_map/ppermute | solution.py:374
  37.9 2.5 %shard_map.103 = (bf16[4,5,96,128]{3,2,1,0:T(8,128)(2,1)S(1)}, bf16[4,5,96,128]{3,2,1,0:T(8,128)(2,1)S(1)}) custom-call(s32[594]{0:T(1024)S(1)} %concatenate.6.table, bf16[2,5,96,128]{3,2,1,0:T(8,128)(2,1)S(1)} %pad_maximum_fusion.1.t0, bf16[2,5,96,128]{3,2,1,0:T(8,128)(2,1)S(1)} %collective-permute-done.2._.t1, ...), custom_call_target="tpu_custom_call" | custom-call | bytes 1048576 | tf_op jit(solution)/shard_map/pallas_call | solution.py:391
  40.4 0.1 collective-permute-start.6
  40.5 1.9 %collective-permute-done.6.arrived = bf16[4,5,96,128]{3,2,1,0:T(8,128)(2,1)S(1)} collective-permute-done((bf16[4,5,96,128]{3,2,1,0:T(8,128)(2,1)S(1)}, bf16[4,5,96,128]{3,2,1,0:T(8,128)(2,1)S(1)}, u32[]{:S(2)}, u32[]{:S(2)}) %collective-permute-start.6) | collective-permute-done | bytes 491552 | tf_op jit(solution)/shard_map/ppermute | solution.py:370
  42.3 0.7 shard_map.104
  43.0 2.4 %collective-permute-start.7 = (bf16[5,96,128]{2,1,0:T(8,128)(2,1)S(1)}, bf16[5,96,128]{2,1,0:T(8,128)(2,1)S(1)}, u32[]{:S(2)}, u32[]{:S(2)}) collective-permute-start(bf16[5,96,128]{2,1,0:T(8,128)(2,1)S(1)} %get-tuple-element.14), channel_id=1, source_target_pairs={{0,16},{4,20},{8,24},{12,28},{16,0},{20,4},{24,8},{28,12},{32,48},... | collective-permute-start | bytes 368648 | tf_op jit(solution)/shard_map/ppermute | solution.py:370
  45.4 2.0 %collective-permute-start.9 = (bf16[5,96,128]{2,1,0:T(8,128)(2,1)S(1)}, bf16[5,96,128]{2,1,0:T(8,128)(2,1)S(1)}, u32[]{:S(2)}, u32[]{:S(2)}) collective-permute-start(bf16[5,96,128]{2,1,0:T(8,128)(2,1)S(1)} %get-tuple-element.16), channel_id=1, source_target_pairs={{0,24},{4,28},{8,0},{12,4},{16,8},{20,12},{24,16},{28,20},{32,56},... | collective-permute-start | bytes 368648 | tf_op jit(solution)/shard_map/ppermute | solution.py:370
  47.5 3.2 %collective-permute-done.7 = bf16[5,96,128]{2,1,0:T(8,128)(2,1)S(1)} collective-permute-done((bf16[5,96,128]{2,1,0:T(8,128)(2,1)S(1)}, bf16[5,96,128]{2,1,0:T(8,128)(2,1)S(1)}, u32[]{:S(2)}, u32[]{:S(2)}) %collective-permute-start.7) | collective-permute-done | bytes 122912 | tf_op jit(solution)/shard_map/ppermute | solution.py:370
  50.7 2.1 %collective-permute-done.8 = bf16[5,96,128]{2,1,0:T(8,128)(2,1)S(1)} collective-permute-done((bf16[5,96,128]{2,1,0:T(8,128)(2,1)S(1)}, bf16[5,96,128]{2,1,0:T(8,128)(2,1)S(1)}, u32[]{:S(2)}, u32[]{:S(2)}) %collective-permute-start.8) | collective-permute-done | bytes 122912 | tf_op jit(solution)/shard_map/ppermute | solution.py:370
  52.8 0.1 add_convert_fusion._.halo0
  52.9 1.3 %collective-permute-start.11 = (bf16[5,96,128]{2,1,0:T(8,128)(2,1)S(1)}, bf16[5,96,128]{2,1,0:T(8,128)(2,1)S(1)}, u32[]{:S(2)}, u32[]{:S(2)}) collective-permute-start(bf16[5,96,128]{2,1,0:T(8,128)(2,1)S(1)} %add_convert_fusion._.halo0), channel_id=1, source_target_pairs={{0,2},{1,3},{4,6},{5,7},{8,10},{9,11},{12,14},{13,15},{16,18},{17,... | collective-permute-start | bytes 368648 | tf_op jit(solution)/shard_map/ppermute | solution.py:374
  54.2 2.1 %collective-permute-start.10 = (bf16[5,96,128]{2,1,0:T(8,128)(2,1)S(1)}, bf16[5,96,128]{2,1,0:T(8,128)(2,1)S(1)}, u32[]{:S(2)}, u32[]{:S(2)}) collective-permute-start(bf16[5,96,128]{2,1,0:T(8,128)(2,1)S(1)} %add_convert_fusion._.halo0), channel_id=1, source_target_pairs={{0,1},{1,2},{2,3},{4,5},{5,6},{6,7},{8,9},{9,10},{10,11},{12,13},{... | collective-permute-start | bytes 368648 | tf_op jit(solution)/shard_map/ppermute | solution.py:374
  56.3 7.0 %collective-permute-done.3.second_prev = bf16[37,96,128]{2,1,0:T(8,128)(2,1)S(1)} collective-permute-done((bf16[37,96,128]{2,1,0:T(8,128)(2,1)S(1)}, bf16[37,96,128]{2,1,0:T(8,128)(2,1)S(1)}, u32[]{:S(2)}, u32[]{:S(2)}) %collective-permute-start.3) | collective-permute-done | bytes 909344 | tf_op jit(solution)/shard_map/ppermute | solution.py:374
  63.2 6.4 %shard_map.105.inner = f32[2,16,96,128]{3,2,1,0:T(8,128)S(1)} custom-call(bf16[2,16,96,128]{3,2,1,0:T(8,128)(2,1)S(1)} %bitcast.21, bf16[37,96,128]{2,1,0:T(8,128)(2,1)S(1)} %shard_map.102._.second_own, bf16[37,96,128]{2,1,0:T(8,128)(2,1)S(1)} %collective-permute-done.3.second_prev, bf16[2,192,3584]{2,1,0:T(8,128)(2,1)S(1)} %shard_map.100.weights, ...), custom_call_target="tpu_custom_call" | custom-call | flops 8000000000 | bytes 1048576 | tf_op jit(solution)/shard_map/pallas_call | solution.py:428
  69.6 5.2 %shard_map.106 = bf16[2,16,96,128]{3,2,1,0:T(8,128)(2,1)S(1)} custom-call(s32[594]{0:T(1024)S(1)} %concatenate.6.table, f32[2,16,96,128]{3,2,1,0:T(8,128)S(1)} %shard_map.105.inner, bf16[5,96,128]{2,1,0:T(8,128)(2,1)S(1)} %shard_map.101.record0, bf16[37,96,128]{2,1,0:T(8,128)(2,1)S(1)} %shard_map.102._.second_own, ...), custom_call_target="tpu_custom_call" | custom-call | flops 4000000000 | bytes 1048576 | tf_op jit(solution)/shard_map/pallas_call | solution.py:431
  74.8 1.2 %copy.29 = bf16[1,2,96,16,128]{4,3,2,1,0:T(8,128)(2,1)} copy(bf16[1,2,96,16,128]{4,2,3,1,0:T(8,128)(2,1)S(1)} %bitcast.22) | data formatting | bytes 1572864 | tf_op jit(solution)/shard_map/broadcast_in_dim | solution.py:444
  (22 shorter events, 0.1 us)
Async XLA Ops:
  0.0 15.1 %copy-start.2 = (f32[96]{0:T(128)S(1)}, f32[96]{0:T(128)}, u32[]{:S(2)}) copy-start(f32[96]{0:T(128)} %param.19) | copy-start | bytes 1156
  0.0 15.1 %copy-start.3 = (f32[96]{0:T(128)S(1)}, f32[96]{0:T(128)}, u32[]{:S(2)}) copy-start(f32[96]{0:T(128)} %param.17) | copy-start | bytes 1156
  0.0 15.1 %copy-start.5 = (f32[96]{0:T(128)S(1)}, f32[96]{0:T(128)}, u32[]{:S(2)}) copy-start(f32[96]{0:T(128)} %param.16) | copy-start | bytes 1156
  0.0 15.1 %copy-start.4 = (f32[96]{0:T(128)S(1)}, f32[96]{0:T(128)}, u32[]{:S(2)}) copy-start(f32[96]{0:T(128)} %param.14) | copy-start | bytes 1156
  0.0 15.2 %copy-start.1 = (bf16[3,3,3,96,96]{4,3,2,1,0:T(8,128)(2,1)S(1)}, bf16[3,3,3,96,96]{4,3,2,1,0:T(8,128)(2,1)}, u32[]{:S(2)}) copy-start(bf16[3,3,3,96,96]{4,3,2,1,0:T(8,128)(2,1)} %param.18) | copy-start | bytes 1492996
  0.0 15.2 %copy-start = (bf16[3,3,3,96,96]{4,3,2,1,0:T(8,128)(2,1)S(1)}, bf16[3,3,3,96,96]{4,3,2,1,0:T(8,128)(2,1)}, u32[]{:S(2)}) copy-start(bf16[3,3,3,96,96]{4,3,2,1,0:T(8,128)(2,1)} %param.15) | copy-start | bytes 1492996
  1.5 24.5 %collective-permute-start = (bf16[2,16,96,128]{3,2,1,0:T(8,128)(2,1)S(1)}, bf16[2,16,96,128]{3,2,1,0:T(8,128)(2,1)}, u32[]{:S(2)}, u32[]{:S(2)}) collective-permute-start(bf16[2,16,96,128]{3,2,1,0:T(8,128)(2,1)S(1)} %bitcast.18), channel_id=1, source_target_pairs={{0,1},{1,2},{2,3},{4,5},{5,6},{6,7},{8,9},{9,10},{10,11},{12,13},{... | collective-permute-start | bytes 2359304 | tf_op jit(solution)/shard_map/ppermute | solution.py:374
  7.1 1.4 %collective-permute-start.1 = (bf16[5,96,128]{2,1,0:T(8,128)(2,1)S(1)}, bf16[5,96,128]{2,1,0:T(8,128)(2,1)S(1)}, u32[]{:S(2)}, u32[]{:S(2)}) collective-permute-start(bf16[5,96,128]{2,1,0:T(8,128)(2,1)S(1)} %shard_map.101.record0), channel_id=1, source_target_pairs={{0,4},{4,0},{8,12},{12,8},{16,20},{20,16},{24,28},{28,24},{32,36},... | collective-permute-start | bytes 368648 | tf_op jit(solution)/shard_map/ppermute | solution.py:370
  8.6 12.4 %collective-permute-start.4 = (bf16[2,5,96,128]{3,2,1,0:T(8,128)(2,1)S(1)}, bf16[2,5,96,128]{3,2,1,0:T(8,128)(2,1)S(1)}, u32[]{:S(2)}, u32[]{:S(2)}) collective-permute-start(bf16[2,5,96,128]{3,2,1,0:T(8,128)(2,1)S(1)} %pad_maximum_fusion.1.t0), channel_id=1, source_target_pairs={{0,64},{4,196},{8,72},{12,204},{16,80},{20,212},{24,88},{28,220},{... | collective-permute-start | bytes 737288 | tf_op jit(solution)/shard_map/ppermute | solution.py:370
  11.9 9.6 %collective-permute-start.2 = (bf16[2,5,96,128]{3,2,1,0:T(8,128)(2,1)S(1)}, bf16[2,5,96,128]{3,2,1,0:T(8,128)(2,1)S(1)}, u32[]{:S(2)}, u32[]{:S(2)}) collective-permute-start(bf16[2,5,96,128]{3,2,1,0:T(8,128)(2,1)S(1)} %pad_maximum_fusion.1.t0), channel_id=1, source_target_pairs={{0,32},{4,228},{8,40},{12,236},{16,48},{20,244},{24,56},{28,252},{... | collective-permute-start | bytes 737288 | tf_op jit(solution)/shard_map/ppermute | solution.py:370
  21.5 16.4 %collective-permute-start.5 = (bf16[3,5,96,128]{3,2,1,0:T(8,128)(2,1)S(1)}, bf16[3,5,96,128]{3,2,1,0:T(8,128)(2,1)S(1)}, u32[]{:S(2)}, u32[]{:S(2)}) collective-permute-start(bf16[3,5,96,128]{3,2,1,0:T(8,128)(2,1)S(1)} %pad_maximum_fusion), channel_id=1, source_target_pairs={{0,64},{4,196},{8,72},{12,204},{16,80},{20,212},{24,88},{28,220},{... | collective-permute-start | bytes 1105928 | tf_op jit(solution)/shard_map/ppermute | solution.py:370
  35.9 27.3 %collective-permute-start.3 = (bf16[37,96,128]{2,1,0:T(8,128)(2,1)S(1)}, bf16[37,96,128]{2,1,0:T(8,128)(2,1)S(1)}, u32[]{:S(2)}, u32[]{:S(2)}) collective-permute-start(bf16[37,96,128]{2,1,0:T(8,128)(2,1)S(1)} %shard_map.102._.second_own), channel_id=1, source_target_pairs={{0,1},{1,2},{2,3},{4,5},{5,6},{6,7},{8,9},{9,10},{10,11},{12,13},{... | collective-permute-start | bytes 2727944 | tf_op jit(solution)/shard_map/ppermute | solution.py:374
  40.4 2.0 %collective-permute-start.6 = (bf16[4,5,96,128]{3,2,1,0:T(8,128)(2,1)S(1)}, bf16[4,5,96,128]{3,2,1,0:T(8,128)(2,1)S(1)}, u32[]{:S(2)}, u32[]{:S(2)}) collective-permute-start(bf16[4,5,96,128]{3,2,1,0:T(8,128)(2,1)S(1)} %get-tuple-element.12), channel_id=1, source_target_pairs={{0,4},{4,0},{8,12},{12,8},{16,20},{20,16},{24,28},{28,24},{32,36},... | collective-permute-start | bytes 1474568 | tf_op jit(solution)/shard_map/ppermute | solution.py:370
  43.0 7.7 %collective-permute-start.7 = (bf16[5,96,128]{2,1,0:T(8,128)(2,1)S(1)}, bf16[5,96,128]{2,1,0:T(8,128)(2,1)S(1)}, u32[]{:S(2)}, u32[]{:S(2)}) collective-permute-start(bf16[5,96,128]{2,1,0:T(8,128)(2,1)S(1)} %get-tuple-element.14), channel_id=1, source_target_pairs={{0,16},{4,20},{8,24},{12,28},{16,0},{20,4},{24,8},{28,12},{32,48},... | collective-permute-start | bytes 368648 | tf_op jit(solution)/shard_map/ppermute | solution.py:370
  45.4 7.4 %collective-permute-start.8 = (bf16[5,96,128]{2,1,0:T(8,128)(2,1)S(1)}, bf16[5,96,128]{2,1,0:T(8,128)(2,1)S(1)}, u32[]{:S(2)}, u32[]{:S(2)}) collective-permute-start(bf16[5,96,128]{2,1,0:T(8,128)(2,1)S(1)} %get-tuple-element.15), channel_id=1, source_target_pairs={{0,8},{4,12},{8,16},{12,20},{16,24},{20,28},{24,0},{28,4},{32,40},... | collective-permute-start | bytes 368648 | tf_op jit(solution)/shard_map/ppermute | solution.py:370
  45.4 7.4 %collective-permute-start.9 = (bf16[5,96,128]{2,1,0:T(8,128)(2,1)S(1)}, bf16[5,96,128]{2,1,0:T(8,128)(2,1)S(1)}, u32[]{:S(2)}, u32[]{:S(2)}) collective-permute-start(bf16[5,96,128]{2,1,0:T(8,128)(2,1)S(1)} %get-tuple-element.16), channel_id=1, source_target_pairs={{0,24},{4,28},{8,0},{12,4},{16,8},{20,12},{24,16},{28,20},{32,56},... | collective-permute-start | bytes 368648 | tf_op jit(solution)/shard_map/ppermute | solution.py:370
  52.9 16.8 %collective-permute-start.11 = (bf16[5,96,128]{2,1,0:T(8,128)(2,1)S(1)}, bf16[5,96,128]{2,1,0:T(8,128)(2,1)S(1)}, u32[]{:S(2)}, u32[]{:S(2)}) collective-permute-start(bf16[5,96,128]{2,1,0:T(8,128)(2,1)S(1)} %add_convert_fusion._.halo0), channel_id=1, source_target_pairs={{0,2},{1,3},{4,6},{5,7},{8,10},{9,11},{12,14},{13,15},{16,18},{17,... | collective-permute-start | bytes 368648 | tf_op jit(solution)/shard_map/ppermute | solution.py:374
  54.2 15.5 %collective-permute-start.10 = (bf16[5,96,128]{2,1,0:T(8,128)(2,1)S(1)}, bf16[5,96,128]{2,1,0:T(8,128)(2,1)S(1)}, u32[]{:S(2)}, u32[]{:S(2)}) collective-permute-start(bf16[5,96,128]{2,1,0:T(8,128)(2,1)S(1)} %add_convert_fusion._.halo0), channel_id=1, source_target_pairs={{0,1},{1,2},{2,3},{4,5},{5,6},{6,7},{8,9},{9,10},{10,11},{12,13},{... | collective-permute-start | bytes 368648 | tf_op jit(solution)/shard_map/ppermute | solution.py:374
where the time goes:
time: 76.3 us; the launch traced here: 76 us
  Pallas kernels  26.1 us (34%)
  starting transfers between devices  24 us (31%)
  waiting for transfers between devices  21.2 us (28%)
  local copies, waits for them, and re-layouts  4.38 us (6%)
    ppermute x8, starting transfers between devices, send(): return lax.ppermute(array, 'tile', pairs(move))  15.6 us
    ppermute x8, waiting for transfers between devices, send(): return lax.ppermute(array, 'tile', pairs(move))  14.2 us
    pallas_call x1, Pallas kernels, per_device(): call(inner_first_kernel, shape(F * H + REC, C, W), 'svvvv-', [window], 24...  9.91 us
    ppermute x4, starting transfers between devices, later(): return lax.ppermute(array, 'group', [(i, i + by) for i in range(NX - by)])  8.42 us
    ppermute x4, waiting for transfers between devices, later(): return lax.ppermute(array, 'group', [(i, i + by) for i in range(NX - by)])  6.96 us
    pallas_call x1, Pallas kernels, per_device(): call(inner_second_kernel, jax.ShapeDtypeStruct((F, H, C, W), F32), 'vvvvv...  6.38 us
    pallas_call x1, Pallas kernels, per_device(): call(outer_kernel, shape(F, H, C, W), 's' + 'v' * 9, [pltpu.VMEM((3 * F,...  5.16 us
    pallas_call x1, Pallas kernels, deliver(): call(select_kernel, [shape(NY, REC, C, W)] * 2, 'svvvv-', [pltpu.SMEM((TI...  2.49 us
  transfers between devices with their start and end apart: 12, of which 7 were waited for; matrix products, arithmetic and copies ran while one was open for 2% of the time, Pallas kernels for 28%

commit v1 on v0

--- a/solution.py
+++ b/solution.py
@@ -64,12 +64,13 @@
     out[base + 4] = jnp.where(lane < 64, columns, rotate(columns, 64)).astype(BF)
 
 
-def record_kernel(table, features, out):
-    up, left = sides(table)
+def record_kernel(ids, tiles, near, features, out):
+    tile = tiles[ids[0]]
+    up, left = near[1, tile] >= 0, near[3, tile] >= 0
     write_record(features, up, left, out, 0)
 
 
-def weights_kernel(one, two, out):
+def weights_kernel(one, two, _, out):
     same = lax.broadcasted_iota(jnp.int32, (C, C), 0) == lax.broadcasted_iota(jnp.int32, (C, C), 1)
     same = same.astype(F32).astype(BF)
     for n, source in enumerate((one, two)):
@@ -82,8 +83,7 @@
             out[n, C:, (t + 1) * KF : (t + 2) * KF] = flipped
 
 
-def select_kernel(table, t0, t1, t2, t3, _, mine, other, inverse):
-    held = (t0, t1, t2, t3)
+def plan_kernel(table, _, out, inverse):
     me = table[0]
     z, y, c = me // (NY * NCORE), (me // NCORE) % NY, me % NCORE
 
@@ -92,8 +92,6 @@
         return 0
 
     lax.fori_loop(0, TILES, invert, 0)
-    mine[...] = jnp.zeros_like(mine)
-    other[...] = jnp.zeros_like(other)
 
     def place(tile):
         slot = inverse[jnp.maximum(tile, 0)]
@@ -102,39 +100,42 @@
         away = jnp.where(away < 0, away + NZ, away)
         label = jnp.where(cs == c, 0, 1)
         fits = (tile >= 0) & (ys == y) & ((away >= 1) & (away <= 3) | (label == 0) & ((away == 0) | (away == 4)))
-        which = jnp.where(fits, jnp.minimum(away, 3), -1)
-        return which, jnp.where(away == 4, 2, label)
-
+        return jnp.where(fits, jnp.minimum(away, 3), -1), jnp.where(away == 4, 0, jnp.where(away == 3, 1 + label, label))
+
+    for n in range(2 * NY):
+        core = c if n < NY else 1 - c
+        near = T_NEAR + table[T_LIST + z * NY * NCORE + (n % NY) * NCORE + core] * 8
+        vertical = jnp.maximum(table[near + 1], table[near + 6])
+        horizontal = jnp.maximum(table[near + 3], table[near + 4])
+        diagonal = jnp.maximum(
+            jnp.maximum(table[near], table[near + 2]), jnp.maximum(table[near + 5], table[near + 7])
+        )
+        for k, tile in enumerate((vertical, horizontal, diagonal)):
+            which, index = place(tile)
+            out[6 * n + 2 * k] = which
+            out[6 * n + 2 * k + 1] = index
+
+
+def select_kernel(plan, t0, t1, t2, t3, _, mine, other):
+    held = (t0, t1, t2, t3)
+    mine[...] = jnp.zeros_like(mine)
+    other[...] = jnp.zeros_like(other)
     low = lanes(C) < 64
-    for same, out in ((True, mine), (False, other)):
-        core = c if same else 1 - c
-
-        def dest(yd, _):
-            near = T_NEAR + table[T_LIST + z * NY * NCORE + yd * NCORE + core] * 8
-            vertical = place(jnp.maximum(table[near + 1], table[near + 6]))
-            horizontal = place(jnp.maximum(table[near + 3], table[near + 4]))
-            diagonal = place(
-                jnp.maximum(
-                    jnp.maximum(table[near], table[near + 2]), jnp.maximum(table[near + 5], table[near + 7])
-                )
-            )
-            for k, ref in enumerate(held):
-
-                @pl.when(vertical[0] == k)
-                def _():
-                    out[yd, 0:4] = ref[vertical[1], 0:4]
-
-                @pl.when(horizontal[0] == k)
-                def _():
-                    out[yd, 4] = jnp.where(low, ref[horizontal[1], 4], out[yd, 4])
-
-                @pl.when(diagonal[0] == k)
-                def _():
-                    out[yd, 4] = jnp.where(low, out[yd, 4], ref[diagonal[1], 4])
-
-            return 0
-
-        lax.fori_loop(0, NY, dest, 0)
+    for n in range(2 * NY):
+        out, yd = (mine, other)[n // NY], n % NY
+        for k, ref in enumerate(held):
+
+            @pl.when(plan[6 * n] == k)
+            def _():
+                out[yd, 0:4] = ref[plan[6 * n + 1], 0:4]
+
+            @pl.when(plan[6 * n + 2] == k)
+            def _():
+                out[yd, 4] = jnp.where(low, ref[plan[6 * n + 3], 4], out[yd, 4])
+
+            @pl.when(plan[6 * n + 4] == k)
+            def _():
+                out[yd, 4] = jnp.where(low, out[yd, 4], ref[plan[6 * n + 5], 4])
 
 
 def combine_kernel(table, mine, arrived, own, one, two, three):
@@ -163,37 +164,85 @@
     return jnp.concatenate(full, axis=0)
 
 
-def row_parts(windows, base, oy, count):
+def row_parts(frames, oy, count):
     return [
-        jnp.concatenate([windows[base + fr, pl.ds(oy + r, 3)].reshape(9 * C, W) for r in range(count)], axis=1)
-        for fr in range(2 * F)
+        jnp.concatenate([windows[f, pl.ds(oy + r, 3)].reshape(9 * C, W) for r in range(count)], axis=1)
+        for windows, f in frames
     ]
+
+
+def frames_of(*windows):
+    return [(ref, f) for ref in windows for f in range(F)]
 
 
 def product(weights, parts):
     return jnp.dot(weights[...], stack(parts), preferred_element_type=F32)
 
 
-def inner_first_kernel(table, own, prev, weights, vectors, _, out, windows):
+def half_product(weights, windows, half, oy):
+    return product(weights.at[:, pl.ds(half * F * KF, F * KF)], row_parts(frames_of(windows), oy, 2))
+
+
+def first_windows(source, gain, exists, windows):
+    zero_ends(windows)
+    for f in range(F):
+
+        def row_step(y, _):
+            center = jnp.where(exists, norm_silu(source[f, y].astype(F32), gain), 0.0)
+            put_window(windows, (f, y + 1), three_shifts(center, 0.0, 0.0))
+            return 0
+
+        lax.fori_loop(0, H, row_step, 0, unroll=4)
+
+
+def own_first_kernel(own, weights, vectors, out, windows):
+    first_windows(own, vectors[:, 1:2], True, windows)
+
+    def rows_step(n, _):
+        out[n] = half_product(weights.at[0], windows, 1, 2 * n)
+        return 0
+
+    lax.fori_loop(0, H // 2, rows_step, 0)
+
+
+def second_windows(source, exists, windows):
+    zero_ends(windows)
+    for f in range(F):
+
+        def row_step(y, _):
+            center = jnp.where(exists, source[f * H + y].astype(F32), 0.0)
+            put_window(windows, (f, y + 1), three_shifts(center, 0.0, 0.0))
+            return 0
+
+        lax.fori_loop(0, H, row_step, 0, unroll=4)
+
+
+def own_second_kernel(own, second, weights, vectors, out, windows):
+    bias = vectors[:, 3:4]
+    second_windows(second, True, windows)
+
+    def rows_step(n, _):
+        acc = half_product(weights.at[1], windows, 1, 2 * n)
+        for f in range(F):
+            value = acc[f * C : (f + 1) * C] + bias
+            for r in range(2):
+                y = 2 * n + r
+                out[f, y] = own[f, y].astype(F32) + value[:, r * W : (r + 1) * W]
+        return 0
+
+    lax.fori_loop(0, H // 2, rows_step, 0)
+
+
+def inner_first_kernel(table, prev, partial, weights, vectors, _, _plan, out, windows):
     up, left = sides(table)
     bias, gain_one, gain_two = vectors[:, 0:1], vectors[:, 1:2], vectors[:, 2:3]
     write_record(prev, up, left, out, F * H)
-    zero_ends(windows)
-    for fr in range(2 * F):
-        source, f = (prev, fr) if fr < F else (own, fr - F)
-
-        def row_step(y, _):
-            center = norm_silu(source[f, y].astype(F32), gain_one)
-            put_window(windows, (fr, y + 1), three_shifts(center, 0.0, 0.0))
-            return 0
-
-        lax.fori_loop(0, H, row_step, 0, unroll=4)
-
+    first_windows(prev, gain_one, table[1] > 0, windows)
     border_row, border_lane = jnp.where(up, 0, H - 1), jnp.where(left, 0, W - 1)
     lane = lanes(C)
 
     def rows_step(n, _):
-        acc = product(weights.at[0], row_parts(windows, 0, 2 * n, 2))
+        acc = partial[n] + half_product(weights.at[0], windows, 0, 2 * n)
         for f in range(F):
             value = norm_silu(acc[f * C : (f + 1) * C] + bias, gain_two)
             for r in range(2):
@@ -205,39 +254,28 @@
     lax.fori_loop(0, H // 2, rows_step, 0)
 
 
-def inner_second_kernel(own, second_own, second_prev, weights, vectors, _, out, windows):
-    bias = vectors[:, 3:4]
-    zero_ends(windows)
-    for fr in range(2 * F):
-        source, f = (second_prev, fr) if fr < F else (second_own, fr - F)
-
-        def row_step(y, _):
-            center = source[f * H + y].astype(F32)
-            put_window(windows, (fr, y + 1), three_shifts(center, 0.0, 0.0))
-            return 0
-
-        lax.fori_loop(0, H, row_step, 0, unroll=4)
+def inner_second_kernel(table, partial, second_prev, weights, _, out, windows):
+    second_windows(second_prev, table[1] > 0, windows)
 
     def rows_step(n, _):
-        acc = product(weights.at[1], row_parts(windows, 0, 2 * n, 2))
+        acc = half_product(weights.at[1], windows, 0, 2 * n)
         for f in range(F):
-            value = acc[f * C : (f + 1) * C] + bias
             for r in range(2):
                 y = 2 * n + r
-                out[f, y] = own[f, y].astype(F32) + value[:, r * W : (r + 1) * W]
+                out[f, y] = partial[f, y] + acc[f * C : (f + 1) * C, r * W : (r + 1) * W]
         return 0
 
     lax.fori_loop(0, H // 2, rows_step, 0)
 
 
 def zero_ends(windows):
-    for fr in range(2 * F):
+    for fr in range(F):
         for yy in (0, H + 1):
             windows[fr, yy] = jnp.zeros((3 * C, W), BF)
 
 
 def band_parts(band, columns, base):
-    parts = row_parts(band, base, 0, 2)
+    parts = row_parts([(band, base + fr) for fr in range(2 * F)], 0, 2)
     for fr in range(2 * F):
         beside = [
             jnp.concatenate([columns[base + fr, j + dx, dy] for dy in range(3) for dx in range(3)], axis=0)
@@ -275,13 +313,16 @@
     for fr in range(3 * F):
         f = fr % F
         record, base, halo = sources[fr // F]
+        exists = table[1] >= 2 - fr // F
         pick = (src == jnp.maximum(body, corner) + f * 32 + col).astype(F32).astype(BF)
-        theirs = norm_silu(jnp.dot(halo[4], pick, preferred_element_type=F32), gain1)
+        theirs = jnp.dot(halo[4], pick, preferred_element_type=F32)
+        theirs = norm_silu(jnp.where(exists, theirs, 0.0), gain1)
         picks = [(src == body + f * 32 + col).astype(F32).astype(BF)]
         for r in range(2):
             picks.append(((src == first_col + col) & (dst == past + r)).astype(F32).astype(BF))
         mine = jnp.concatenate([record[base + 4], halo[2 * f], halo[2 * f + 1]], axis=1)
-        ours = norm_silu(jnp.dot(mine, jnp.concatenate(picks, axis=0), preferred_element_type=F32), gain1)
+        ours = jnp.dot(mine, jnp.concatenate(picks, axis=0), preferred_element_type=F32)
+        ours = norm_silu(jnp.where(exists, ours, 0.0), gain1)
         low, high = jnp.where(left, theirs, ours), jnp.where(left, ours, theirs)
         for k in range(4):
             put_column(columns1, fr, k, (low if k < 2 else high)[:, (k % 2) * W : (k % 2 + 1) * W])
@@ -291,7 +332,7 @@
             raw = jnp.where(up, other if r < 2 else self, self if r < 2 else other)
             at = jnp.where(up, r, H + r)
             moved = rotate(near, jnp.where(left, (W - at) % W, W - 1 - at))
-            center = norm_silu(raw.astype(F32), gain1)
+            center = norm_silu(jnp.where(exists, raw.astype(F32), 0.0), gain1)
             put_window(
                 band1, (fr, r), three_shifts(center, jnp.where(left, moved, 0.0), jnp.where(left, 0.0, moved))
             )
@@ -371,7 +412,7 @@
 
 
 def later(array, by=1):
-    return lax.ppermute(array, "group", [(i, i + by) for i in range(NX - by)])
+    return lax.ppermute(array, "group", [(i, (i + by) % NX) for i in range(NX)])
 
 
 def spread(record):
@@ -379,7 +420,7 @@
     t0 = jnp.stack([record, send(record, swap)])
     t1 = send(t0, along(1))
     t2 = send(t0, along(2))
-    t3 = send(jnp.concatenate([t1, t2[:1]], axis=0), along(2))
+    t3 = send(jnp.concatenate([t2[:1], t1], axis=0), along(2))
     return t0, t1, t2, t3
 
 
@@ -387,10 +428,8 @@
     return z, y, 1 - c
 
 
-def deliver(table, held, after):
-    mine, other = call(
-        select_kernel, [shape(NY, REC, C, W)] * 2, "svvvv-", [pltpu.SMEM((TILES,), jnp.int32)]
-    )(table, *held, after)
+def deliver(table, plan, held, after):
+    mine, other = call(select_kernel, [shape(NY, REC, C, W)] * 2, "svvvv-")(plan, *held, after)
     arrived = send(other, swap)
     own, one, two, three = call(combine_kernel, [shape(REC, C, W)] * 4, "svv")(table, mine, arrived)
     total = own.astype(F32)
@@ -402,9 +441,10 @@
 def per_device(
     features, tile_list, neighbours, clip_frames, gain_one, weight_one, bias_one, gain_two, weight_two, bias_two
 ):
+    ids = jnp.stack([lax.axis_index("tile"), lax.axis_index("group")]).astype(jnp.int32)
     table = jnp.concatenate(
         [
-            jnp.stack([lax.axis_index("tile"), lax.axis_index("group")]).astype(jnp.int32),
+            ids,
             tile_list,
             neighbours.reshape(-1),
             clip_frames,
@@ -413,21 +453,33 @@
     vectors = jnp.stack([bias_one, gain_one, gain_two, bias_two], axis=1)
     own = features[0].transpose(0, 2, 1, 3)
     prev = later(own)
-    record = call(record_kernel, shape(REC, C, W), "sv")(table, own)
-    weights = call(weights_kernel, shape(2, 2 * C, 4 * KF), "vv", mib=16)(
-        weight_one.reshape(3, 9 * C, C), weight_two.reshape(3, 9 * C, C)
+    record = call(record_kernel, shape(REC, C, W), "sssv")(ids, tile_list, neighbours.T, own)
+    held = spread(record)
+    weights = call(weights_kernel, shape(2, 2 * C, 4 * KF), "vv-", mib=16)(
+        weight_one.reshape(3, 9 * C, C), weight_two.reshape(3, 9 * C, C), held[0]
     )
-    held = spread(record)
-    window = pltpu.VMEM((2 * F, H + 2, 3 * C, W), BF)
+    plan = pl.pallas_call(
+        plan_kernel,
+        out_shape=jax.ShapeDtypeStruct((12 * NY,), jnp.int32),
+        in_specs=[SMEM, ANY],
+        out_specs=SMEM,
+        scratch_shapes=[pltpu.SMEM((TILES,), jnp.int32)],
+    )(table, held[0])
+    scratch = [pltpu.VMEM((F, H + 2, 3 * C, W), BF)]
+    own_one = call(
+        own_first_kernel, jax.ShapeDtypeStruct((H // 2, 2 * C, 2 * W), F32), "vvv", scratch, 16, 3 * 10**9
+    )(own, weights, vectors)
     second = call(
-        inner_first_kernel, shape(F * H + REC, C, W), "svvvv-", [window], 24, 8 * 10**9
-    )(table, own, prev, weights, vectors, held[1])
+        inner_first_kernel, shape(F * H + REC, C, W), "svvvv-s", scratch, 16, 8 * 10**9
+    )(table, prev, own_one, weights, vectors, held[1], plan)
+    whole = jax.ShapeDtypeStruct((F, H, C, W), F32)
+    own_two = call(own_second_kernel, whole, "vvvv", scratch, 16, 10**9)(own, second, weights, vectors)
     second_prev = later(second)
-    halo = deliver(table, held, second)
+    halo = deliver(table, plan, held, second)
     halo1, halo2 = later(halo), later(halo, 2)
-    inner = call(
-        inner_second_kernel, jax.ShapeDtypeStruct((F, H, C, W), F32), "vvvvv-", [window], 24, 8 * 10**9
-    )(own, second, second_prev, weights, vectors, halo)
+    inner = call(inner_second_kernel, whole, "svvv-", scratch, 16, 12 * 10**9)(
+        table, own_two, second_prev, weights, halo
+    )
     out = call(
         outer_kernel,
         shape(F, H, C, W),

time: 76.3 us -> 67 us (0.88)
  the two profiles are of different devices: /device:TPU:44 before, /device:TPU:1 now
where the time goes in v1:
time: 67 us; the launch traced here: 66.8 us
  Pallas kernels  31.6 us (47%)
  starting transfers between devices  22.3 us (33%)
  waiting for transfers between devices  7.78 us (12%)
  local copies, waits for them, and re-layouts  4.58 us (7%)
    ppermute x8, starting transfers between devices, send(): return lax.ppermute(array, 'tile', pairs(move))  16.2 us
    pallas_call x1, Pallas kernels, per_device(): call(inner_first_kernel, shape(F * H + REC, C, W), 'svvvv-s', scratch, 16...  6.97 us
    ppermute x4, starting transfers between devices, later(): return lax.ppermute(array, 'group', [(i, (i + by) % NX) for i in range(NX)])  6.11 us
    ppermute x4, waiting for transfers between devices, later(): return lax.ppermute(array, 'group', [(i, (i + by) % NX) for i in range(NX)])  5.49 us
    pallas_call x1, Pallas kernels, per_device(): call(outer_kernel, shape(F, H, C, W), 's' + 'v' * 9, [pltpu.VMEM((3 * F,...  5.26 us
    pallas_call x1, Pallas kernels, per_device(): call(own_first_kernel, jax.ShapeDtypeStruct((H // 2, 2 * C, 2 * W), F32),...  4.71 us
    pallas_call x1, Pallas kernels, per_device(): call(inner_second_kernel, whole, 'svvv-', scratch, 16, 12 * 10 ** 9)  4.54 us
    pallas_call x1, Pallas kernels, per_device(): call(own_second_kernel, whole, 'vvvv', scratch, 16, 10 ** 9)  3.98 us
  transfers between devices with their start and end apart: 12, of which 4 were waited for; matrix products, arithmetic and copies ran while one was open for 2% of the time, Pallas kernels for 39%

profile of v1, /device:TPU:1, one launch (start us, length us, event | category | flops | bytes accessed | tf_op | source)
XLA Modules:
  0.0 66.8 jit_solution(11865354529262717096)
XLA Ops:
  0.1 1.4 %copy.32 = bf16[1,2,96,16,128]{4,2,3,1,0:T(8,128)(2,1)S(1)} copy(bf16[1,2,96,16,128]{4,3,2,1,0:T(8,128)(2,1)} %param.10) | data formatting | bytes 1572864 | tf_op args[0]
  1.5 2.1 %collective-permute-start = (bf16[2,16,96,128]{3,2,1,0:T(8,128)(2,1)S(1)}, bf16[2,16,96,128]{3,2,1,0:T(8,128)(2,1)}, u32[]{:S(2)}, u32[]{:S(2)}) collective-permute-start(bf16[2,16,96,128]{3,2,1,0:T(8,128)(2,1)S(1)} %bitcast.19), channel_id=1, source_target_pairs={{0,1},{1,2},{2,3},{3,0},{4,5},{5,6},{6,7},{7,4},{8,9},{9,10},{10,1... | collective-permute-start | bytes 2359304 | tf_op jit(solution)/shard_map/ppermute | solution.py:415
  3.7 1.0 %shard_map.100.record0 = bf16[5,96,128]{2,1,0:T(8,128)(2,1)S(1)} custom-call(s32[2]{0:T(128)S(1)} %pad_add_fusion.ids, s32[64]{0:T(128)S(1)} %copy-done.7, s32[8,64]{1,0:T(8,128)S(1)} %bitcast.27, bf16[2,16,96,128]{3,2,1,0:T(8,128)(2,1)S(1)} %bitcast.20), custom_call_target="tpu_custom_call" | custom-call | bytes 1048576 | tf_op jit(solution)/shard_map/pallas_call | solution.py:456
  4.7 1.3 %collective-permute-start.1 = (bf16[5,96,128]{2,1,0:T(8,128)(2,1)S(1)}, bf16[5,96,128]{2,1,0:T(8,128)(2,1)S(1)}, u32[]{:S(2)}, u32[]{:S(2)}) collective-permute-start(bf16[5,96,128]{2,1,0:T(8,128)(2,1)S(1)} %shard_map.100.record0), channel_id=1, source_target_pairs={{0,4},{4,0},{8,12},{12,8},{16,20},{20,16},{24,28},{28,24},{32,36},... | collective-permute-start | bytes 368648 | tf_op jit(solution)/shard_map/ppermute | solution.py:411
  6.1 0.1 copy.26.vectors
  6.2 0.1 reshape.9
  6.3 0.7 %concatenate.7.table = s32[594]{0:T(1024)} concatenate(s32[1]{0:T(128)} %bitcast, s32[1]{0:T(128)} %bitcast.1, s32[64]{0:T(128)S(1)} %copy-done.7, s32[512]{0:T(512)S(1)} %reshape.9, s32[16]{0:T(128)S(1)} %copy-done.8), dimensions={0} | concatenate | bytes 4752 | tf_op jit(solution)/shard_map/concatenate | solution.py:445
  7.0 5.4 %collective-permute-start.2 = (bf16[2,5,96,128]{3,2,1,0:T(8,128)(2,1)S(1)}, bf16[2,5,96,128]{3,2,1,0:T(8,128)(2,1)S(1)}, u32[]{:S(2)}, u32[]{:S(2)}) collective-permute-start(bf16[2,5,96,128]{3,2,1,0:T(8,128)(2,1)S(1)} %pad_maximum_fusion.1._.t0), channel_id=1, source_target_pairs={{0,32},{4,228},{8,40},{12,236},{16,48},{20,244},{24,56},{28,252},{... | collective-permute-start | bytes 737288 | tf_op jit(solution)/shard_map/ppermute | solution.py:411
  12.4 1.2 %collective-permute-start.4 = (bf16[2,5,96,128]{3,2,1,0:T(8,128)(2,1)S(1)}, bf16[2,5,96,128]{3,2,1,0:T(8,128)(2,1)S(1)}, u32[]{:S(2)}, u32[]{:S(2)}) collective-permute-start(bf16[2,5,96,128]{3,2,1,0:T(8,128)(2,1)S(1)} %pad_maximum_fusion.1._.t0), channel_id=1, source_target_pairs={{0,64},{4,196},{8,72},{12,204},{16,80},{20,212},{24,88},{28,220},{... | collective-permute-start | bytes 737288 | tf_op jit(solution)/shard_map/ppermute | solution.py:411
  13.6 2.4 %shard_map.103._plan.plan = s32[48]{0:T(128)} custom-call(s32[594]{0:T(1024)} %concatenate.7.table, bf16[2,5,96,128]{3,2,1,0:T(8,128)(2,1)} %copy-done), custom_call_target="tpu_custom_call" | custom-call | tf_op jit(solution)/shard_map/pallas_call | solution.py:461
  16.1 0.9 %copy-done.1 = bf16[2,5,96,128]{3,2,1,0:T(8,128)(2,1)S(1)} copy-done((bf16[2,5,96,128]{3,2,1,0:T(8,128)(2,1)S(1)}, bf16[2,5,96,128]{3,2,1,0:T(8,128)(2,1)}, u32[]{:S(2)}) %copy-start.1) | copy-done | bytes 245784
  17.0 0.6 shard_map.101.weights
  17.6 4.7 %shard_map.102.partial = f32[8,192,256]{2,1,0:T(8,128)S(1)} custom-call(bf16[2,16,96,128]{3,2,1,0:T(8,128)(2,1)S(1)} %bitcast.21, bf16[2,192,3584]{2,1,0:T(8,128)(2,1)S(1)} %shard_map.101.weights, f32[96,4]{1,0:T(8,128)S(1)} %copy.26.vectors), custom_call_target="tpu_custom_call" | custom-call | flops 3000000000 | bytes 1048576 | tf_op jit(solution)/shard_map/pallas_call | solution.py:469
  22.4 2.6 %collective-permute-start.5 = (bf16[3,5,96,128]{3,2,1,0:T(8,128)(2,1)S(1)}, bf16[3,5,96,128]{3,2,1,0:T(8,128)(2,1)S(1)}, u32[]{:S(2)}, u32[]{:S(2)}) collective-permute-start(bf16[3,5,96,128]{3,2,1,0:T(8,128)(2,1)S(1)} %pad_maximum_fusion), channel_id=1, source_target_pairs={{0,64},{4,196},{8,72},{12,204},{16,80},{20,212},{24,88},{28,220},{... | collective-permute-start | bytes 1105928 | tf_op jit(solution)/shard_map/ppermute | solution.py:411
  25.0 7.0 %shard_map.104.second._.second_own = bf16[37,96,128]{2,1,0:T(8,128)(2,1)S(1)} custom-call(s32[594]{0:T(1024)S(1)} %copy-done.4, bf16[2,16,96,128]{3,2,1,0:T(8,128)(2,1)} %collective-permute-done.prev, f32[8,192,256]{2,1,0:T(8,128)S(1)} %shard_map.102.partial, bf16[2,192,3584]{2,1,0:T(8,128)(2,1)S(1)} %shard_map.101.weights, f32[96,4]{1,0:T(8,128)S(1)} %copy.26.vectors, ...), custom_call_target="tpu_custom_call" | custom-call | flops 8000000000 | bytes 1048576 | tf_op jit(solution)/shard_map/pallas_call | solution.py:472
  32.0 1.3 %collective-permute-start.3 = (bf16[37,96,128]{2,1,0:T(8,128)(2,1)S(1)}, bf16[37,96,128]{2,1,0:T(8,128)(2,1)S(1)}, u32[]{:S(2)}, u32[]{:S(2)}) collective-permute-start(bf16[37,96,128]{2,1,0:T(8,128)(2,1)S(1)} %shard_map.104.second._.second_own), channel_id=1, source_target_pairs={{0,1},{1,2},{2,3},{3,0},{4,5},{5,6},{6,7},{7,4},{8,9},{9,10},{10,1... | collective-permute-start | bytes 2727944 | tf_op jit(solution)/shard_map/ppermute | solution.py:415
  33.3 0.4 collective-permute-done.5.t3
  33.7 1.5 %shard_map.106 = (bf16[4,5,96,128]{3,2,1,0:T(8,128)(2,1)S(1)}, bf16[4,5,96,128]{3,2,1,0:T(8,128)(2,1)S(1)}) custom-call(s32[48]{0:T(128)S(1)} %copy-done.6, bf16[2,5,96,128]{3,2,1,0:T(8,128)(2,1)S(1)} %copy-done.1, bf16[2,5,96,128]{3,2,1,0:T(8,128)(2,1)S(1)} %collective-permute-done.2._.t1, bf16[2,5,96,128]{3,2,1,0:T(8,128)(2,1)S(1)} %collective-permute-done.4.t2, ...), custom_call_target="tpu_custom_call" | custom-call | bytes 1048576 | tf_op jit(solution)/shard_map/pallas_call | solution.py:432
  35.2 0.1 collective-permute-start.6
  35.3 1.9 %collective-permute-done.6.arrived = bf16[4,5,96,128]{3,2,1,0:T(8,128)(2,1)S(1)} collective-permute-done((bf16[4,5,96,128]{3,2,1,0:T(8,128)(2,1)S(1)}, bf16[4,5,96,128]{3,2,1,0:T(8,128)(2,1)S(1)}, u32[]{:S(2)}, u32[]{:S(2)}) %collective-permute-start.6) | collective-permute-done | bytes 491552 | tf_op jit(solution)/shard_map/ppermute | solution.py:411
  37.1 0.7 %shard_map.107 = (bf16[5,96,128]{2,1,0:T(8,128)(2,1)S(1)}, bf16[5,96,128]{2,1,0:T(8,128)(2,1)S(1)}, bf16[5,96,128]{2,1,0:T(8,128)(2,1)S(1)}, bf16[5,96,128]{2,1,0:T(8,128)(2,1)S(1)}) custom-call(s32[594]{0:T(1024)S(1)} %copy-done.4, bf16[4,5,96,128]{3,2,1,0:T(8,128)(2,1)S(1)} %get-tuple-element.11.mine, ...), custom_call_target="tpu_custom_call" | custom-call | bytes 1048576 | tf_op jit(solution)/shard_map/pallas_call | solution.py:434
  37.9 3.0 %collective-permute-start.7 = (bf16[5,96,128]{2,1,0:T(8,128)(2,1)S(1)}, bf16[5,96,128]{2,1,0:T(8,128)(2,1)S(1)}, u32[]{:S(2)}, u32[]{:S(2)}) collective-permute-start(bf16[5,96,128]{2,1,0:T(8,128)(2,1)S(1)} %get-tuple-element.14), channel_id=1, source_target_pairs={{0,16},{4,20},{8,24},{12,28},{16,0},{20,4},{24,8},{28,12},{32,48},... | collective-permute-start | bytes 368648 | tf_op jit(solution)/shard_map/ppermute | solution.py:411
  40.9 0.4 collective-permute-start.8
  41.3 2.3 %collective-permute-start.9 = (bf16[5,96,128]{2,1,0:T(8,128)(2,1)S(1)}, bf16[5,96,128]{2,1,0:T(8,128)(2,1)S(1)}, u32[]{:S(2)}, u32[]{:S(2)}) collective-permute-start(bf16[5,96,128]{2,1,0:T(8,128)(2,1)S(1)} %get-tuple-element.16), channel_id=1, source_target_pairs={{0,24},{4,28},{8,0},{12,4},{16,8},{20,12},{24,16},{28,20},{32,56},... | collective-permute-start | bytes 368648 | tf_op jit(solution)/shard_map/ppermute | solution.py:411
  43.5 4.0 %shard_map.105.partial = f32[2,16,96,128]{3,2,1,0:T(8,128)S(1)} custom-call(bf16[2,16,96,128]{3,2,1,0:T(8,128)(2,1)S(1)} %bitcast.22, bf16[37,96,128]{2,1,0:T(8,128)(2,1)S(1)} %shard_map.104.second._.second_own, bf16[2,192,3584]{2,1,0:T(8,128)(2,1)S(1)} %shard_map.101.weights, f32[96,4]{1,0:T(8,128)S(1)} %copy.26.vectors), custom_call_target="tpu_custom_call" | custom-call | flops 1000000000 | bytes 1048576 | tf_op jit(solution)/shard_map/pallas_call | solution.py:476
  47.6 1.3 %collective-permute-start.10 = (bf16[5,96,128]{2,1,0:T(8,128)(2,1)S(1)}, bf16[5,96,128]{2,1,0:T(8,128)(2,1)S(1)}, u32[]{:S(2)}, u32[]{:S(2)}) collective-permute-start(bf16[5,96,128]{2,1,0:T(8,128)(2,1)S(1)} %add_convert_fusion._.halo0), channel_id=1, source_target_pairs={{0,1},{1,2},{2,3},{3,0},{4,5},{5,6},{6,7},{7,4},{8,9},{9,10},{10,1... | collective-permute-start | bytes 368648 | tf_op jit(solution)/shard_map/ppermute | solution.py:415
  48.9 1.4 %collective-permute-start.11 = (bf16[5,96,128]{2,1,0:T(8,128)(2,1)S(1)}, bf16[5,96,128]{2,1,0:T(8,128)(2,1)S(1)}, u32[]{:S(2)}, u32[]{:S(2)}) collective-permute-start(bf16[5,96,128]{2,1,0:T(8,128)(2,1)S(1)} %add_convert_fusion._.halo0), channel_id=1, source_target_pairs={{0,2},{1,3},{2,0},{3,1},{4,6},{5,7},{6,4},{7,5},{8,10},{9,11},{10,... | collective-permute-start | bytes 368648 | tf_op jit(solution)/shard_map/ppermute | solution.py:415
  50.3 4.8 %collective-permute-done.3.second_prev = bf16[37,96,128]{2,1,0:T(8,128)(2,1)S(1)} collective-permute-done((bf16[37,96,128]{2,1,0:T(8,128)(2,1)S(1)}, bf16[37,96,128]{2,1,0:T(8,128)(2,1)S(1)}, u32[]{:S(2)}, u32[]{:S(2)}) %collective-permute-start.3) | collective-permute-done | bytes 909344 | tf_op jit(solution)/shard_map/ppermute | solution.py:415
  55.2 4.5 %shard_map.108.inner = f32[2,16,96,128]{3,2,1,0:T(8,128)S(1)} custom-call(s32[594]{0:T(1024)S(1)} %copy-done.4, f32[2,16,96,128]{3,2,1,0:T(8,128)S(1)} %shard_map.105.partial, bf16[37,96,128]{2,1,0:T(8,128)(2,1)S(1)} %collective-permute-done.3.second_prev, bf16[2,192,3584]{2,1,0:T(8,128)(2,1)S(1)} %shard_map.101.weights, ...), custom_call_target="tpu_custom_call" | custom-call | flops 12000000000 | bytes 1048576 | tf_op jit(solution)/shard_map/pallas_call | solution.py:480
  59.7 0.6 collective-permute-done.11.halo2
  60.4 5.3 %shard_map.109 = bf16[2,16,96,128]{3,2,1,0:T(8,128)(2,1)S(1)} custom-call(s32[594]{0:T(1024)S(1)} %copy-done.4, f32[2,16,96,128]{3,2,1,0:T(8,128)S(1)} %shard_map.108.inner, bf16[5,96,128]{2,1,0:T(8,128)(2,1)S(1)} %shard_map.100.record0, bf16[37,96,128]{2,1,0:T(8,128)(2,1)S(1)} %shard_map.104.second._.second_own, ...), custom_call_target="tpu_custom_call" | custom-call | flops 4000000000 | bytes 1048576 | tf_op jit(solution)/shard_map/pallas_call | solution.py:483
  65.7 1.2 %copy.30 = bf16[1,2,96,16,128]{4,3,2,1,0:T(8,128)(2,1)} copy(bf16[1,2,96,16,128]{4,2,3,1,0:T(8,128)(2,1)S(1)} %bitcast.23) | data formatting | bytes 1572864 | tf_op jit(solution)/shard_map/broadcast_in_dim | solution.py:496
  (40 shorter events, 0.4 us)
Async XLA Ops:
  0.0 3.7 %copy-start.5 = (s32[64,8]{0,1:T(8,128)S(1)}, s32[64,8]{0,1:T(8,128)}, u32[]{:S(2)}) copy-start(s32[64,8]{0,1:T(8,128)} %param.12) | copy-start | bytes 6148
  0.0 3.7 %copy-start.7 = (s32[64]{0:T(128)S(1)}, s32[64]{0:T(128)}, u32[]{:S(2)}) copy-start(s32[64]{0:T(128)} %tiles.1) | copy-start | bytes 772
  0.0 6.1 %copy-start.12 = (f32[96]{0:T(128)S(1)}, f32[96]{0:T(128)}, u32[]{:S(2)}) copy-start(f32[96]{0:T(128)} %param.16) | copy-start | bytes 1156
  0.0 6.0 %copy-start.11 = (f32[96]{0:T(128)S(1)}, f32[96]{0:T(128)}, u32[]{:S(2)}) copy-start(f32[96]{0:T(128)} %param.14) | copy-start | bytes 1156
  0.0 6.0 %copy-start.10 = (f32[96]{0:T(128)S(1)}, f32[96]{0:T(128)}, u32[]{:S(2)}) copy-start(f32[96]{0:T(128)} %param.17) | copy-start | bytes 1156
  0.0 6.0 %copy-start.9 = (f32[96]{0:T(128)S(1)}, f32[96]{0:T(128)}, u32[]{:S(2)}) copy-start(f32[96]{0:T(128)} %param.19) | copy-start | bytes 1156
  0.0 6.3 %copy-start.8 = (s32[16]{0:T(128)S(1)}, s32[16]{0:T(128)}, u32[]{:S(2)}) copy-start(s32[16]{0:T(128)} %param.13) | copy-start | bytes 196
  0.0 16.0 %copy-start.2 = (bf16[3,3,3,96,96]{4,3,2,1,0:T(8,128)(2,1)S(1)}, bf16[3,3,3,96,96]{4,3,2,1,0:T(8,128)(2,1)}, u32[]{:S(2)}) copy-start(bf16[3,3,3,96,96]{4,3,2,1,0:T(8,128)(2,1)} %param.15) | copy-start | bytes 1492996
  0.1 16.0 %copy-start.3 = (bf16[3,3,3,96,96]{4,3,2,1,0:T(8,128)(2,1)S(1)}, bf16[3,3,3,96,96]{4,3,2,1,0:T(8,128)(2,1)}, u32[]{:S(2)}) copy-start(bf16[3,3,3,96,96]{4,3,2,1,0:T(8,128)(2,1)} %param.18) | copy-start | bytes 1492996
  1.5 23.5 %collective-permute-start = (bf16[2,16,96,128]{3,2,1,0:T(8,128)(2,1)S(1)}, bf16[2,16,96,128]{3,2,1,0:T(8,128)(2,1)}, u32[]{:S(2)}, u32[]{:S(2)}) collective-permute-start(bf16[2,16,96,128]{3,2,1,0:T(8,128)(2,1)S(1)} %bitcast.19), channel_id=1, source_target_pairs={{0,1},{1,2},{2,3},{3,0},{4,5},{5,6},{6,7},{7,4},{8,9},{9,10},{10,1... | collective-permute-start | bytes 2359304 | tf_op jit(solution)/shard_map/ppermute | solution.py:415
  4.7 2.3 %collective-permute-start.1 = (bf16[5,96,128]{2,1,0:T(8,128)(2,1)S(1)}, bf16[5,96,128]{2,1,0:T(8,128)(2,1)S(1)}, u32[]{:S(2)}, u32[]{:S(2)}) collective-permute-start(bf16[5,96,128]{2,1,0:T(8,128)(2,1)S(1)} %shard_map.100.record0), channel_id=1, source_target_pairs={{0,4},{4,0},{8,12},{12,8},{16,20},{20,16},{24,28},{28,24},{32,36},... | collective-permute-start | bytes 368648 | tf_op jit(solution)/shard_map/ppermute | solution.py:411
  7.0 6.6 %copy-start = (bf16[2,5,96,128]{3,2,1,0:T(8,128)(2,1)}, bf16[2,5,96,128]{3,2,1,0:T(8,128)(2,1)S(1)}, u32[]{:S(2)}) copy-start(bf16[2,5,96,128]{3,2,1,0:T(8,128)(2,1)S(1)} %pad_maximum_fusion.1._.t0) | copy-start | bytes 737284
  7.0 15.3 %collective-permute-start.2 = (bf16[2,5,96,128]{3,2,1,0:T(8,128)(2,1)S(1)}, bf16[2,5,96,128]{3,2,1,0:T(8,128)(2,1)S(1)}, u32[]{:S(2)}, u32[]{:S(2)}) collective-permute-start(bf16[2,5,96,128]{3,2,1,0:T(8,128)(2,1)S(1)} %pad_maximum_fusion.1._.t0), channel_id=1, source_target_pairs={{0,32},{4,228},{8,40},{12,236},{16,48},{20,244},{24,56},{28,252},{... | collective-permute-start | bytes 737288 | tf_op jit(solution)/shard_map/ppermute | solution.py:411
  12.4 9.9 %collective-permute-start.4 = (bf16[2,5,96,128]{3,2,1,0:T(8,128)(2,1)S(1)}, bf16[2,5,96,128]{3,2,1,0:T(8,128)(2,1)S(1)}, u32[]{:S(2)}, u32[]{:S(2)}) collective-permute-start(bf16[2,5,96,128]{3,2,1,0:T(8,128)(2,1)S(1)} %pad_maximum_fusion.1._.t0), channel_id=1, source_target_pairs={{0,64},{4,196},{8,72},{12,204},{16,80},{20,212},{24,88},{28,220},{... | collective-permute-start | bytes 737288 | tf_op jit(solution)/shard_map/ppermute | solution.py:411
  16.1 0.9 %copy-start.1 = (bf16[2,5,96,128]{3,2,1,0:T(8,128)(2,1)S(1)}, bf16[2,5,96,128]{3,2,1,0:T(8,128)(2,1)}, u32[]{:S(2)}) copy-start(bf16[2,5,96,128]{3,2,1,0:T(8,128)(2,1)} %copy-done) | copy-start | bytes 737284
  17.6 7.4 %copy-start.4 = (s32[594]{0:T(1024)S(1)}, s32[594]{0:T(1024)}, u32[]{:S(2)}) copy-start(s32[594]{0:T(1024)} %concatenate.7.table) | copy-start | bytes 7132
  17.6 7.4 %copy-start.6 = (s32[48]{0:T(128)S(1)}, s32[48]{0:T(128)}, u32[]{:S(2)}) copy-start(s32[48]{0:T(128)} %shard_map.103._plan.plan) | copy-start | bytes 580
  22.4 11.3 %collective-permute-start.5 = (bf16[3,5,96,128]{3,2,1,0:T(8,128)(2,1)S(1)}, bf16[3,5,96,128]{3,2,1,0:T(8,128)(2,1)S(1)}, u32[]{:S(2)}, u32[]{:S(2)}) collective-permute-start(bf16[3,5,96,128]{3,2,1,0:T(8,128)(2,1)S(1)} %pad_maximum_fusion), channel_id=1, source_target_pairs={{0,64},{4,196},{8,72},{12,204},{16,80},{20,212},{24,88},{28,220},{... | collective-permute-start | bytes 1105928 | tf_op jit(solution)/shard_map/ppermute | solution.py:411
  32.0 23.2 %collective-permute-start.3 = (bf16[37,96,128]{2,1,0:T(8,128)(2,1)S(1)}, bf16[37,96,128]{2,1,0:T(8,128)(2,1)S(1)}, u32[]{:S(2)}, u32[]{:S(2)}) collective-permute-start(bf16[37,96,128]{2,1,0:T(8,128)(2,1)S(1)} %shard_map.104.second._.second_own), channel_id=1, source_target_pairs={{0,1},{1,2},{2,3},{3,0},{4,5},{5,6},{6,7},{7,4},{8,9},{9,10},{10,1... | collective-permute-start | bytes 2727944 | tf_op jit(solution)/shard_map/ppermute | solution.py:415
  35.2 2.0 %collective-permute-start.6 = (bf16[4,5,96,128]{3,2,1,0:T(8,128)(2,1)S(1)}, bf16[4,5,96,128]{3,2,1,0:T(8,128)(2,1)S(1)}, u32[]{:S(2)}, u32[]{:S(2)}) collective-permute-start(bf16[4,5,96,128]{3,2,1,0:T(8,128)(2,1)S(1)} %get-tuple-element.12), channel_id=1, source_target_pairs={{0,4},{4,0},{8,12},{12,8},{16,20},{20,16},{24,28},{28,24},{32,36},... | collective-permute-start | bytes 1474568 | tf_op jit(solution)/shard_map/ppermute | solution.py:411
  37.9 9.7 %collective-permute-start.7 = (bf16[5,96,128]{2,1,0:T(8,128)(2,1)S(1)}, bf16[5,96,128]{2,1,0:T(8,128)(2,1)S(1)}, u32[]{:S(2)}, u32[]{:S(2)}) collective-permute-start(bf16[5,96,128]{2,1,0:T(8,128)(2,1)S(1)} %get-tuple-element.14), channel_id=1, source_target_pairs={{0,16},{4,20},{8,24},{12,28},{16,0},{20,4},{24,8},{28,12},{32,48},... | collective-permute-start | bytes 368648 | tf_op jit(solution)/shard_map/ppermute | solution.py:411
  40.9 6.7 %collective-permute-start.8 = (bf16[5,96,128]{2,1,0:T(8,128)(2,1)S(1)}, bf16[5,96,128]{2,1,0:T(8,128)(2,1)S(1)}, u32[]{:S(2)}, u32[]{:S(2)}) collective-permute-start(bf16[5,96,128]{2,1,0:T(8,128)(2,1)S(1)} %get-tuple-element.15), channel_id=1, source_target_pairs={{0,8},{4,12},{8,16},{12,20},{16,24},{20,28},{24,0},{28,4},{32,40},... | collective-permute-start | bytes 368648 | tf_op jit(solution)/shard_map/ppermute | solution.py:411
  41.3 6.3 %collective-permute-start.9 = (bf16[5,96,128]{2,1,0:T(8,128)(2,1)S(1)}, bf16[5,96,128]{2,1,0:T(8,128)(2,1)S(1)}, u32[]{:S(2)}, u32[]{:S(2)}) collective-permute-start(bf16[5,96,128]{2,1,0:T(8,128)(2,1)S(1)} %get-tuple-element.16), channel_id=1, source_target_pairs={{0,24},{4,28},{8,0},{12,4},{16,8},{20,12},{24,16},{28,20},{32,56},... | collective-permute-start | bytes 368648 | tf_op jit(solution)/shard_map/ppermute | solution.py:411
  47.6 12.1 %collective-permute-start.10 = (bf16[5,96,128]{2,1,0:T(8,128)(2,1)S(1)}, bf16[5,96,128]{2,1,0:T(8,128)(2,1)S(1)}, u32[]{:S(2)}, u32[]{:S(2)}) collective-permute-start(bf16[5,96,128]{2,1,0:T(8,128)(2,1)S(1)} %add_convert_fusion._.halo0), channel_id=1, source_target_pairs={{0,1},{1,2},{2,3},{3,0},{4,5},{5,6},{6,7},{7,4},{8,9},{9,10},{10,1... | collective-permute-start | bytes 368648 | tf_op jit(solution)/shard_map/ppermute | solution.py:415
  48.9 11.5 %collective-permute-start.11 = (bf16[5,96,128]{2,1,0:T(8,128)(2,1)S(1)}, bf16[5,96,128]{2,1,0:T(8,128)(2,1)S(1)}, u32[]{:S(2)}, u32[]{:S(2)}) collective-permute-start(bf16[5,96,128]{2,1,0:T(8,128)(2,1)S(1)} %add_convert_fusion._.halo0), channel_id=1, source_target_pairs={{0,2},{1,3},{2,0},{3,1},{4,6},{5,7},{6,4},{7,5},{8,10},{9,11},{10,... | collective-permute-start | bytes 368648 | tf_op jit(solution)/shard_map/ppermute | solution.py:415

commit v2 on v1

--- a/solution.py
+++ b/solution.py
@@ -192,7 +192,8 @@
             put_window(windows, (f, y + 1), three_shifts(center, 0.0, 0.0))
             return 0
 
-        lax.fori_loop(0, H, row_step, 0, unroll=4)
+        for y in range(H):
+            row_step(y, 0)
 
 
 def own_first_kernel(own, weights, vectors, out, windows):
@@ -202,7 +203,8 @@
         out[n] = half_product(weights.at[0], windows, 1, 2 * n)
         return 0
 
-    lax.fori_loop(0, H // 2, rows_step, 0)
+    for n in range(H // 2):
+        rows_step(n, 0)
 
 
 def second_windows(source, exists, windows):
@@ -214,7 +216,8 @@
             put_window(windows, (f, y + 1), three_shifts(center, 0.0, 0.0))
             return 0
 
-        lax.fori_loop(0, H, row_step, 0, unroll=4)
+        for y in range(H):
+            row_step(y, 0)
 
 
 def own_second_kernel(own, second, weights, vectors, out, windows):
@@ -230,7 +233,8 @@
                 out[f, y] = own[f, y].astype(F32) + value[:, r * W : (r + 1) * W]
         return 0
 
-    lax.fori_loop(0, H // 2, rows_step, 0)
+    for n in range(H // 2):
+        rows_step(n, 0)
 
 
 def inner_first_kernel(table, prev, partial, weights, vectors, _, _plan, out, windows):
@@ -251,7 +255,8 @@
                 out[f * H + y] = jnp.where(border, 0.0, value[:, r * W : (r + 1) * W]).astype(BF)
         return 0
 
-    lax.fori_loop(0, H // 2, rows_step, 0)
+    for n in range(H // 2):
+        rows_step(n, 0)
 
 
 def inner_second_kernel(table, partial, second_prev, weights, _, out, windows):
@@ -265,7 +270,8 @@
                 out[f, y] = partial[f, y] + acc[f * C : (f + 1) * C, r * W : (r + 1) * W]
         return 0
 
-    lax.fori_loop(0, H // 2, rows_step, 0)
+    for n in range(H // 2):
+        rows_step(n, 0)
 
 
 def zero_ends(windows):

time: 67 us -> 63.4 us (0.946)
  Pallas kernels: 31.6 us -> 22.4 us
  waiting for transfers between devices: 7.78 us -> 11.8 us
  starting transfers between devices: 22.3 us -> 23.8 us
    ppermute x8, waiting for transfers between devices: 2.29 us -> 5.88 us  [send(): return lax.ppermute(array, 'tile', pairs(move))]
    pallas_call x1, Pallas kernels: 6.97 us -> 4.29 us  [per_device(): call(inner_first_kernel, shape(F * H + REC, C, W), 'svvvv-s', scratch, 16...]
    pallas_call x1, Pallas kernels: 4.71 us -> 2.37 us  [per_device(): call(own_first_kernel, jax.ShapeDtypeStruct((H // 2, 2 * C, 2 * W), F32),...]
    pallas_call x1, Pallas kernels: 3.98 us -> 1.79 us  [per_device(): call(own_second_kernel, whole, 'vvvv', scratch, 16, 10 ** 9)]
    pallas_call x1, Pallas kernels: 4.54 us -> 2.37 us  [per_device(): call(inner_second_kernel, whole, 'svvv-', scratch, 16, 12 * 10 ** 9)]
    ppermute x8, starting transfers between devices: 16.2 us -> 17.7 us  [send(): return lax.ppermute(array, 'tile', pairs(move))]
  transfers between devices with their start and end apart: 12 -> 12, of which waited for: 4 -> 8; matrix products, arithmetic and copies ran while one was open for 2% -> 2% of each run, Pallas kernels for 39% -> 27%
where the time goes in v2:
time: 63.4 us; the launch traced here: 63.2 us
  starting transfers between devices  23.8 us (38%)
  Pallas kernels  22.4 us (35%)
  waiting for transfers between devices  11.8 us (19%)
  local copies, waits for them, and re-layouts  4.58 us (7%)
    ppermute x8, starting transfers between devices, send(): return lax.ppermute(array, 'tile', pairs(move))  17.7 us
    ppermute x4, starting transfers between devices, later(): return lax.ppermute(array, 'group', [(i, (i + by) % NX) for i in range(NX)])  6.13 us
    ppermute x4, waiting for transfers between devices, later(): return lax.ppermute(array, 'group', [(i, (i + by) % NX) for i in range(NX)])  5.95 us
    ppermute x8, waiting for transfers between devices, send(): return lax.ppermute(array, 'tile', pairs(move))  5.88 us
    pallas_call x1, Pallas kernels, per_device(): call(outer_kernel, shape(F, H, C, W), 's' + 'v' * 9, [pltpu.VMEM((3 * F,...  5.26 us
    pallas_call x1, Pallas kernels, per_device(): call(inner_first_kernel, shape(F * H + REC, C, W), 'svvvv-s', scratch, 16...  4.29 us
    unnamed x28, local copies, waits for them, and re-layouts  2.52 us
    pallas_call x1, Pallas kernels, per_device(): pl.pallas_call(plan_kernel, out_shape=jax.ShapeDtypeStruct((12 * NY,), jn...  2.44 us
  transfers between devices with their start and end apart: 12, of which 8 were waited for; matrix products, arithmetic and copies ran while one was open for 2% of the time, Pallas kernels for 27%

profile of v2, /device:TPU:1, one launch (start us, length us, event | category | flops | bytes accessed | tf_op | source)
XLA Modules:
  0.0 63.2 jit_solution(5907169906523538668)
XLA Ops:
  0.1 1.4 %copy.32 = bf16[1,2,96,16,128]{4,2,3,1,0:T(8,128)(2,1)S(1)} copy(bf16[1,2,96,16,128]{4,3,2,1,0:T(8,128)(2,1)} %param.10) | data formatting | bytes 1572864 | tf_op args[0]
  1.5 2.1 %collective-permute-start = (bf16[2,16,96,128]{3,2,1,0:T(8,128)(2,1)S(1)}, bf16[2,16,96,128]{3,2,1,0:T(8,128)(2,1)}, u32[]{:S(2)}, u32[]{:S(2)}) collective-permute-start(bf16[2,16,96,128]{3,2,1,0:T(8,128)(2,1)S(1)} %bitcast.19), channel_id=1, source_target_pairs={{0,1},{1,2},{2,3},{3,0},{4,5},{5,6},{6,7},{7,4},{8,9},{9,10},{10,1... | collective-permute-start | bytes 2359304 | tf_op jit(solution)/shard_map/ppermute | solution.py:421
  3.7 1.0 %shard_map.100.record0 = bf16[5,96,128]{2,1,0:T(8,128)(2,1)S(1)} custom-call(s32[2]{0:T(128)S(1)} %pad_add_fusion.ids, s32[64]{0:T(128)S(1)} %copy-done.7, s32[8,64]{1,0:T(8,128)S(1)} %bitcast.27, bf16[2,16,96,128]{3,2,1,0:T(8,128)(2,1)S(1)} %bitcast.20), custom_call_target="tpu_custom_call" | custom-call | bytes 1048576 | tf_op jit(solution)/shard_map/pallas_call | solution.py:462
  4.7 1.3 %collective-permute-start.1 = (bf16[5,96,128]{2,1,0:T(8,128)(2,1)S(1)}, bf16[5,96,128]{2,1,0:T(8,128)(2,1)S(1)}, u32[]{:S(2)}, u32[]{:S(2)}) collective-permute-start(bf16[5,96,128]{2,1,0:T(8,128)(2,1)S(1)} %shard_map.100.record0), channel_id=1, source_target_pairs={{0,4},{4,0},{8,12},{12,8},{16,20},{20,16},{24,28},{28,24},{32,36},... | collective-permute-start | bytes 368648 | tf_op jit(solution)/shard_map/ppermute | solution.py:417
  6.3 0.7 %concatenate.7.table = s32[594]{0:T(1024)} concatenate(s32[1]{0:T(128)} %bitcast, s32[1]{0:T(128)} %bitcast.1, s32[64]{0:T(128)S(1)} %copy-done.7, s32[512]{0:T(512)S(1)} %reshape.9, s32[16]{0:T(128)S(1)} %copy-done.8), dimensions={0} | concatenate | bytes 4752 | tf_op jit(solution)/shard_map/concatenate | solution.py:451
  7.0 5.4 %collective-permute-start.2 = (bf16[2,5,96,128]{3,2,1,0:T(8,128)(2,1)S(1)}, bf16[2,5,96,128]{3,2,1,0:T(8,128)(2,1)S(1)}, u32[]{:S(2)}, u32[]{:S(2)}) collective-permute-start(bf16[2,5,96,128]{3,2,1,0:T(8,128)(2,1)S(1)} %pad_maximum_fusion.1._.t0), channel_id=1, source_target_pairs={{0,32},{4,228},{8,40},{12,236},{16,48},{20,244},{24,56},{28,252},{... | collective-permute-start | bytes 737288 | tf_op jit(solution)/shard_map/ppermute | solution.py:417
  12.4 1.2 %collective-permute-start.4 = (bf16[2,5,96,128]{3,2,1,0:T(8,128)(2,1)S(1)}, bf16[2,5,96,128]{3,2,1,0:T(8,128)(2,1)S(1)}, u32[]{:S(2)}, u32[]{:S(2)}) collective-permute-start(bf16[2,5,96,128]{3,2,1,0:T(8,128)(2,1)S(1)} %pad_maximum_fusion.1._.t0), channel_id=1, source_target_pairs={{0,64},{4,196},{8,72},{12,204},{16,80},{20,212},{24,88},{28,220},{... | collective-permute-start | bytes 737288 | tf_op jit(solution)/shard_map/ppermute | solution.py:417
  13.6 2.4 %shard_map.103._plan.plan = s32[48]{0:T(128)} custom-call(s32[594]{0:T(1024)} %concatenate.7.table, bf16[2,5,96,128]{3,2,1,0:T(8,128)(2,1)} %copy-done), custom_call_target="tpu_custom_call" | custom-call | tf_op jit(solution)/shard_map/pallas_call | solution.py:467
  16.1 0.9 %copy-done.1 = bf16[2,5,96,128]{3,2,1,0:T(8,128)(2,1)S(1)} copy-done((bf16[2,5,96,128]{3,2,1,0:T(8,128)(2,1)S(1)}, bf16[2,5,96,128]{3,2,1,0:T(8,128)(2,1)}, u32[]{:S(2)}) %copy-start.1) | copy-done | bytes 245784
  17.0 0.6 shard_map.101.weights
  17.6 2.4 %shard_map.102.partial = f32[8,192,256]{2,1,0:T(8,128)S(1)} custom-call(bf16[2,16,96,128]{3,2,1,0:T(8,128)(2,1)S(1)} %bitcast.21, bf16[2,192,3584]{2,1,0:T(8,128)(2,1)S(1)} %shard_map.101.weights, f32[96,4]{1,0:T(8,128)S(1)} %copy.26.vectors), custom_call_target="tpu_custom_call" | custom-call | flops 3000000000 | bytes 1048576 | tf_op jit(solution)/shard_map/pallas_call | solution.py:475
  20.0 0.8 %collective-permute-done.4.t2 = bf16[2,5,96,128]{3,2,1,0:T(8,128)(2,1)S(1)} collective-permute-done((bf16[2,5,96,128]{3,2,1,0:T(8,128)(2,1)S(1)}, bf16[2,5,96,128]{3,2,1,0:T(8,128)(2,1)S(1)}, u32[]{:S(2)}, u32[]{:S(2)}) %collective-permute-start.4) | collective-permute-done | bytes 245792 | tf_op jit(solution)/shard_map/ppermute | solution.py:417
  20.9 4.1 %collective-permute-start.5 = (bf16[3,5,96,128]{3,2,1,0:T(8,128)(2,1)S(1)}, bf16[3,5,96,128]{3,2,1,0:T(8,128)(2,1)S(1)}, u32[]{:S(2)}, u32[]{:S(2)}) collective-permute-start(bf16[3,5,96,128]{3,2,1,0:T(8,128)(2,1)S(1)} %pad_maximum_fusion), channel_id=1, source_target_pairs={{0,64},{4,196},{8,72},{12,204},{16,80},{20,212},{24,88},{28,220},{... | collective-permute-start | bytes 1105928 | tf_op jit(solution)/shard_map/ppermute | solution.py:417
  25.0 4.3 %shard_map.104.second._.second_own = bf16[37,96,128]{2,1,0:T(8,128)(2,1)S(1)} custom-call(s32[594]{0:T(1024)S(1)} %copy-done.4, bf16[2,16,96,128]{3,2,1,0:T(8,128)(2,1)} %collective-permute-done.prev, f32[8,192,256]{2,1,0:T(8,128)S(1)} %shard_map.102.partial, bf16[2,192,3584]{2,1,0:T(8,128)(2,1)S(1)} %shard_map.101.weights, f32[96,4]{1,0:T(8,128)S(1)} %copy.26.vectors, ...), custom_call_target="tpu_custom_call" | custom-call | flops 8000000000 | bytes 1048576 | tf_op jit(solution)/shard_map/pallas_call | solution.py:478
  29.3 1.3 %collective-permute-start.3 = (bf16[37,96,128]{2,1,0:T(8,128)(2,1)S(1)}, bf16[37,96,128]{2,1,0:T(8,128)(2,1)S(1)}, u32[]{:S(2)}, u32[]{:S(2)}) collective-permute-start(bf16[37,96,128]{2,1,0:T(8,128)(2,1)S(1)} %shard_map.104.second._.second_own), channel_id=1, source_target_pairs={{0,1},{1,2},{2,3},{3,0},{4,5},{5,6},{6,7},{7,4},{8,9},{9,10},{10,1... | collective-permute-start | bytes 2727944 | tf_op jit(solution)/shard_map/ppermute | solution.py:421
  30.6 1.3 %collective-permute-done.5.t3 = bf16[3,5,96,128]{3,2,1,0:T(8,128)(2,1)S(1)} collective-permute-done((bf16[3,5,96,128]{3,2,1,0:T(8,128)(2,1)S(1)}, bf16[3,5,96,128]{3,2,1,0:T(8,128)(2,1)S(1)}, u32[]{:S(2)}, u32[]{:S(2)}) %collective-permute-start.5) | collective-permute-done | bytes 368672 | tf_op jit(solution)/shard_map/ppermute | solution.py:417
  31.9 1.7 %shard_map.106 = (bf16[4,5,96,128]{3,2,1,0:T(8,128)(2,1)S(1)}, bf16[4,5,96,128]{3,2,1,0:T(8,128)(2,1)S(1)}) custom-call(s32[48]{0:T(128)S(1)} %copy-done.6, bf16[2,5,96,128]{3,2,1,0:T(8,128)(2,1)S(1)} %copy-done.1, bf16[2,5,96,128]{3,2,1,0:T(8,128)(2,1)S(1)} %collective-permute-done.2._.t1, bf16[2,5,96,128]{3,2,1,0:T(8,128)(2,1)S(1)} %collective-permute-done.4.t2, ...), custom_call_target="tpu_custom_call" | custom-call | bytes 1048576 | tf_op jit(solution)/shard_map/pallas_call | solution.py:438
  33.7 1.9 %collective-permute-done.6.arrived = bf16[4,5,96,128]{3,2,1,0:T(8,128)(2,1)S(1)} collective-permute-done((bf16[4,5,96,128]{3,2,1,0:T(8,128)(2,1)S(1)}, bf16[4,5,96,128]{3,2,1,0:T(8,128)(2,1)S(1)}, u32[]{:S(2)}, u32[]{:S(2)}) %collective-permute-start.6) | collective-permute-done | bytes 491552 | tf_op jit(solution)/shard_map/ppermute | solution.py:417
  35.5 0.7 %shard_map.107 = (bf16[5,96,128]{2,1,0:T(8,128)(2,1)S(1)}, bf16[5,96,128]{2,1,0:T(8,128)(2,1)S(1)}, bf16[5,96,128]{2,1,0:T(8,128)(2,1)S(1)}, bf16[5,96,128]{2,1,0:T(8,128)(2,1)S(1)}) custom-call(s32[594]{0:T(1024)S(1)} %copy-done.4, bf16[4,5,96,128]{3,2,1,0:T(8,128)(2,1)S(1)} %get-tuple-element.11.mine, ...), custom_call_target="tpu_custom_call" | custom-call | bytes 1048576 | tf_op jit(solution)/shard_map/pallas_call | solution.py:440
  36.3 3.0 %collective-permute-start.7 = (bf16[5,96,128]{2,1,0:T(8,128)(2,1)S(1)}, bf16[5,96,128]{2,1,0:T(8,128)(2,1)S(1)}, u32[]{:S(2)}, u32[]{:S(2)}) collective-permute-start(bf16[5,96,128]{2,1,0:T(8,128)(2,1)S(1)} %get-tuple-element.14), channel_id=1, source_target_pairs={{0,16},{4,20},{8,24},{12,28},{16,0},{20,4},{24,8},{28,12},{32,48},... | collective-permute-start | bytes 368648 | tf_op jit(solution)/shard_map/ppermute | solution.py:417
  39.2 0.4 collective-permute-start.8
  39.6 2.3 %collective-permute-start.9 = (bf16[5,96,128]{2,1,0:T(8,128)(2,1)S(1)}, bf16[5,96,128]{2,1,0:T(8,128)(2,1)S(1)}, u32[]{:S(2)}, u32[]{:S(2)}) collective-permute-start(bf16[5,96,128]{2,1,0:T(8,128)(2,1)S(1)} %get-tuple-element.16), channel_id=1, source_target_pairs={{0,24},{4,28},{8,0},{12,4},{16,8},{20,12},{24,16},{28,20},{32,56},... | collective-permute-start | bytes 368648 | tf_op jit(solution)/shard_map/ppermute | solution.py:417
  41.9 1.8 %shard_map.105.partial = f32[2,16,96,128]{3,2,1,0:T(8,128)S(1)} custom-call(bf16[2,16,96,128]{3,2,1,0:T(8,128)(2,1)S(1)} %bitcast.22, bf16[37,96,128]{2,1,0:T(8,128)(2,1)S(1)} %shard_map.104.second._.second_own, bf16[2,192,3584]{2,1,0:T(8,128)(2,1)S(1)} %shard_map.101.weights, f32[96,4]{1,0:T(8,128)S(1)} %copy.26.vectors), custom_call_target="tpu_custom_call" | custom-call | flops 1000000000 | bytes 1048576 | tf_op jit(solution)/shard_map/pallas_call | solution.py:482
  43.7 1.8 %collective-permute-done.8 = bf16[5,96,128]{2,1,0:T(8,128)(2,1)S(1)} collective-permute-done((bf16[5,96,128]{2,1,0:T(8,128)(2,1)S(1)}, bf16[5,96,128]{2,1,0:T(8,128)(2,1)S(1)}, u32[]{:S(2)}, u32[]{:S(2)}) %collective-permute-start.8) | collective-permute-done | bytes 122912 | tf_op jit(solution)/shard_map/ppermute | solution.py:417
  45.7 1.3 %collective-permute-start.10 = (bf16[5,96,128]{2,1,0:T(8,128)(2,1)S(1)}, bf16[5,96,128]{2,1,0:T(8,128)(2,1)S(1)}, u32[]{:S(2)}, u32[]{:S(2)}) collective-permute-start(bf16[5,96,128]{2,1,0:T(8,128)(2,1)S(1)} %add_convert_fusion._.halo0), channel_id=1, source_target_pairs={{0,1},{1,2},{2,3},{3,0},{4,5},{5,6},{6,7},{7,4},{8,9},{9,10},{10,1... | collective-permute-start | bytes 368648 | tf_op jit(solution)/shard_map/ppermute | solution.py:421
  47.0 1.4 %collective-permute-start.11 = (bf16[5,96,128]{2,1,0:T(8,128)(2,1)S(1)}, bf16[5,96,128]{2,1,0:T(8,128)(2,1)S(1)}, u32[]{:S(2)}, u32[]{:S(2)}) collective-permute-start(bf16[5,96,128]{2,1,0:T(8,128)(2,1)S(1)} %add_convert_fusion._.halo0), channel_id=1, source_target_pairs={{0,2},{1,3},{2,0},{3,1},{4,6},{5,7},{6,4},{7,5},{8,10},{9,11},{10,... | collective-permute-start | bytes 368648 | tf_op jit(solution)/shard_map/ppermute | solution.py:421
  48.4 3.9 %collective-permute-done.3.second_prev = bf16[37,96,128]{2,1,0:T(8,128)(2,1)S(1)} collective-permute-done((bf16[37,96,128]{2,1,0:T(8,128)(2,1)S(1)}, bf16[37,96,128]{2,1,0:T(8,128)(2,1)S(1)}, u32[]{:S(2)}, u32[]{:S(2)}) %collective-permute-start.3) | collective-permute-done | bytes 909344 | tf_op jit(solution)/shard_map/ppermute | solution.py:421
  52.3 2.4 %shard_map.108.inner = f32[2,16,96,128]{3,2,1,0:T(8,128)S(1)} custom-call(s32[594]{0:T(1024)S(1)} %copy-done.4, f32[2,16,96,128]{3,2,1,0:T(8,128)S(1)} %shard_map.105.partial, bf16[37,96,128]{2,1,0:T(8,128)(2,1)S(1)} %collective-permute-done.3.second_prev, bf16[2,192,3584]{2,1,0:T(8,128)(2,1)S(1)} %shard_map.101.weights, ...), custom_call_target="tpu_custom_call" | custom-call | flops 12000000000 | bytes 1048576 | tf_op jit(solution)/shard_map/pallas_call | solution.py:486
  54.7 0.3 collective-permute-done.10.halo1
  55.0 1.7 %collective-permute-done.11.halo2 = bf16[5,96,128]{2,1,0:T(8,128)(2,1)S(1)} collective-permute-done((bf16[5,96,128]{2,1,0:T(8,128)(2,1)S(1)}, bf16[5,96,128]{2,1,0:T(8,128)(2,1)S(1)}, u32[]{:S(2)}, u32[]{:S(2)}) %collective-permute-start.11) | collective-permute-done | bytes 122912 | tf_op jit(solution)/shard_map/ppermute | solution.py:421
  56.7 5.3 %shard_map.109 = bf16[2,16,96,128]{3,2,1,0:T(8,128)(2,1)S(1)} custom-call(s32[594]{0:T(1024)S(1)} %copy-done.4, f32[2,16,96,128]{3,2,1,0:T(8,128)S(1)} %shard_map.108.inner, bf16[5,96,128]{2,1,0:T(8,128)(2,1)S(1)} %shard_map.100.record0, bf16[37,96,128]{2,1,0:T(8,128)(2,1)S(1)} %shard_map.104.second._.second_own, ...), custom_call_target="tpu_custom_call" | custom-call | flops 4000000000 | bytes 1048576 | tf_op jit(solution)/shard_map/pallas_call | solution.py:489
  62.0 1.2 %copy.30 = bf16[1,2,96,16,128]{4,3,2,1,0:T(8,128)(2,1)} copy(bf16[1,2,96,16,128]{4,2,3,1,0:T(8,128)(2,1)S(1)} %bitcast.23) | data formatting | bytes 1572864 | tf_op jit(solution)/shard_map/broadcast_in_dim | solution.py:502
  (40 shorter events, 0.8 us)
Async XLA Ops:
  0.0 3.7 %copy-start.5 = (s32[64,8]{0,1:T(8,128)S(1)}, s32[64,8]{0,1:T(8,128)}, u32[]{:S(2)}) copy-start(s32[64,8]{0,1:T(8,128)} %param.12) | copy-start | bytes 6148
  0.0 3.7 %copy-start.7 = (s32[64]{0:T(128)S(1)}, s32[64]{0:T(128)}, u32[]{:S(2)}) copy-start(s32[64]{0:T(128)} %tiles.1) | copy-start | bytes 772
  0.0 6.1 %copy-start.12 = (f32[96]{0:T(128)S(1)}, f32[96]{0:T(128)}, u32[]{:S(2)}) copy-start(f32[96]{0:T(128)} %param.16) | copy-start | bytes 1156
  0.0 6.0 %copy-start.11 = (f32[96]{0:T(128)S(1)}, f32[96]{0:T(128)}, u32[]{:S(2)}) copy-start(f32[96]{0:T(128)} %param.14) | copy-start | bytes 1156
  0.0 6.0 %copy-start.10 = (f32[96]{0:T(128)S(1)}, f32[96]{0:T(128)}, u32[]{:S(2)}) copy-start(f32[96]{0:T(128)} %param.17) | copy-start | bytes 1156
  0.0 6.0 %copy-start.9 = (f32[96]{0:T(128)S(1)}, f32[96]{0:T(128)}, u32[]{:S(2)}) copy-start(f32[96]{0:T(128)} %param.19) | copy-start | bytes 1156
  0.0 6.3 %copy-start.8 = (s32[16]{0:T(128)S(1)}, s32[16]{0:T(128)}, u32[]{:S(2)}) copy-start(s32[16]{0:T(128)} %param.13) | copy-start | bytes 196
  0.0 16.0 %copy-start.2 = (bf16[3,3,3,96,96]{4,3,2,1,0:T(8,128)(2,1)S(1)}, bf16[3,3,3,96,96]{4,3,2,1,0:T(8,128)(2,1)}, u32[]{:S(2)}) copy-start(bf16[3,3,3,96,96]{4,3,2,1,0:T(8,128)(2,1)} %param.15) | copy-start | bytes 1492996
  0.1 16.0 %copy-start.3 = (bf16[3,3,3,96,96]{4,3,2,1,0:T(8,128)(2,1)S(1)}, bf16[3,3,3,96,96]{4,3,2,1,0:T(8,128)(2,1)}, u32[]{:S(2)}) copy-start(bf16[3,3,3,96,96]{4,3,2,1,0:T(8,128)(2,1)} %param.18) | copy-start | bytes 1492996
  1.5 23.5 %collective-permute-start = (bf16[2,16,96,128]{3,2,1,0:T(8,128)(2,1)S(1)}, bf16[2,16,96,128]{3,2,1,0:T(8,128)(2,1)}, u32[]{:S(2)}, u32[]{:S(2)}) collective-permute-start(bf16[2,16,96,128]{3,2,1,0:T(8,128)(2,1)S(1)} %bitcast.19), channel_id=1, source_target_pairs={{0,1},{1,2},{2,3},{3,0},{4,5},{5,6},{6,7},{7,4},{8,9},{9,10},{10,1... | collective-permute-start | bytes 2359304 | tf_op jit(solution)/shard_map/ppermute | solution.py:421
  4.7 2.3 %collective-permute-start.1 = (bf16[5,96,128]{2,1,0:T(8,128)(2,1)S(1)}, bf16[5,96,128]{2,1,0:T(8,128)(2,1)S(1)}, u32[]{:S(2)}, u32[]{:S(2)}) collective-permute-start(bf16[5,96,128]{2,1,0:T(8,128)(2,1)S(1)} %shard_map.100.record0), channel_id=1, source_target_pairs={{0,4},{4,0},{8,12},{12,8},{16,20},{20,16},{24,28},{28,24},{32,36},... | collective-permute-start | bytes 368648 | tf_op jit(solution)/shard_map/ppermute | solution.py:417
  7.0 6.6 %copy-start = (bf16[2,5,96,128]{3,2,1,0:T(8,128)(2,1)}, bf16[2,5,96,128]{3,2,1,0:T(8,128)(2,1)S(1)}, u32[]{:S(2)}) copy-start(bf16[2,5,96,128]{3,2,1,0:T(8,128)(2,1)S(1)} %pad_maximum_fusion.1._.t0) | copy-start | bytes 737284
  7.0 13.8 %collective-permute-start.2 = (bf16[2,5,96,128]{3,2,1,0:T(8,128)(2,1)S(1)}, bf16[2,5,96,128]{3,2,1,0:T(8,128)(2,1)S(1)}, u32[]{:S(2)}, u32[]{:S(2)}) collective-permute-start(bf16[2,5,96,128]{3,2,1,0:T(8,128)(2,1)S(1)} %pad_maximum_fusion.1._.t0), channel_id=1, source_target_pairs={{0,32},{4,228},{8,40},{12,236},{16,48},{20,244},{24,56},{28,252},{... | collective-permute-start | bytes 737288 | tf_op jit(solution)/shard_map/ppermute | solution.py:417
  12.4 8.4 %collective-permute-start.4 = (bf16[2,5,96,128]{3,2,1,0:T(8,128)(2,1)S(1)}, bf16[2,5,96,128]{3,2,1,0:T(8,128)(2,1)S(1)}, u32[]{:S(2)}, u32[]{:S(2)}) collective-permute-start(bf16[2,5,96,128]{3,2,1,0:T(8,128)(2,1)S(1)} %pad_maximum_fusion.1._.t0), channel_id=1, source_target_pairs={{0,64},{4,196},{8,72},{12,204},{16,80},{20,212},{24,88},{28,220},{... | collective-permute-start | bytes 737288 | tf_op jit(solution)/shard_map/ppermute | solution.py:417
  16.1 0.9 %copy-start.1 = (bf16[2,5,96,128]{3,2,1,0:T(8,128)(2,1)S(1)}, bf16[2,5,96,128]{3,2,1,0:T(8,128)(2,1)}, u32[]{:S(2)}) copy-start(bf16[2,5,96,128]{3,2,1,0:T(8,128)(2,1)} %copy-done) | copy-start | bytes 737284
  17.6 7.4 %copy-start.4 = (s32[594]{0:T(1024)S(1)}, s32[594]{0:T(1024)}, u32[]{:S(2)}) copy-start(s32[594]{0:T(1024)} %concatenate.7.table) | copy-start | bytes 7132
  17.6 7.4 %copy-start.6 = (s32[48]{0:T(128)S(1)}, s32[48]{0:T(128)}, u32[]{:S(2)}) copy-start(s32[48]{0:T(128)} %shard_map.103._plan.plan) | copy-start | bytes 580
  20.9 11.0 %collective-permute-start.5 = (bf16[3,5,96,128]{3,2,1,0:T(8,128)(2,1)S(1)}, bf16[3,5,96,128]{3,2,1,0:T(8,128)(2,1)S(1)}, u32[]{:S(2)}, u32[]{:S(2)}) collective-permute-start(bf16[3,5,96,128]{3,2,1,0:T(8,128)(2,1)S(1)} %pad_maximum_fusion), channel_id=1, source_target_pairs={{0,64},{4,196},{8,72},{12,204},{16,80},{20,212},{24,88},{28,220},{... | collective-permute-start | bytes 1105928 | tf_op jit(solution)/shard_map/ppermute | solution.py:417
  29.3 23.0 %collective-permute-start.3 = (bf16[37,96,128]{2,1,0:T(8,128)(2,1)S(1)}, bf16[37,96,128]{2,1,0:T(8,128)(2,1)S(1)}, u32[]{:S(2)}, u32[]{:S(2)}) collective-permute-start(bf16[37,96,128]{2,1,0:T(8,128)(2,1)S(1)} %shard_map.104.second._.second_own), channel_id=1, source_target_pairs={{0,1},{1,2},{2,3},{3,0},{4,5},{5,6},{6,7},{7,4},{8,9},{9,10},{10,1... | collective-permute-start | bytes 2727944 | tf_op jit(solution)/shard_map/ppermute | solution.py:421
  33.6 2.0 %collective-permute-start.6 = (bf16[4,5,96,128]{3,2,1,0:T(8,128)(2,1)S(1)}, bf16[4,5,96,128]{3,2,1,0:T(8,128)(2,1)S(1)}, u32[]{:S(2)}, u32[]{:S(2)}) collective-permute-start(bf16[4,5,96,128]{3,2,1,0:T(8,128)(2,1)S(1)} %get-tuple-element.12), channel_id=1, source_target_pairs={{0,4},{4,0},{8,12},{12,8},{16,20},{20,16},{24,28},{28,24},{32,36},... | collective-permute-start | bytes 1474568 | tf_op jit(solution)/shard_map/ppermute | solution.py:417
  36.3 7.5 %collective-permute-start.7 = (bf16[5,96,128]{2,1,0:T(8,128)(2,1)S(1)}, bf16[5,96,128]{2,1,0:T(8,128)(2,1)S(1)}, u32[]{:S(2)}, u32[]{:S(2)}) collective-permute-start(bf16[5,96,128]{2,1,0:T(8,128)(2,1)S(1)} %get-tuple-element.14), channel_id=1, source_target_pairs={{0,16},{4,20},{8,24},{12,28},{16,0},{20,4},{24,8},{28,12},{32,48},... | collective-permute-start | bytes 368648 | tf_op jit(solution)/shard_map/ppermute | solution.py:417
  39.2 6.3 %collective-permute-start.8 = (bf16[5,96,128]{2,1,0:T(8,128)(2,1)S(1)}, bf16[5,96,128]{2,1,0:T(8,128)(2,1)S(1)}, u32[]{:S(2)}, u32[]{:S(2)}) collective-permute-start(bf16[5,96,128]{2,1,0:T(8,128)(2,1)S(1)} %get-tuple-element.15), channel_id=1, source_target_pairs={{0,8},{4,12},{8,16},{12,20},{16,24},{20,28},{24,0},{28,4},{32,40},... | collective-permute-start | bytes 368648 | tf_op jit(solution)/shard_map/ppermute | solution.py:417
  39.6 5.9 %collective-permute-start.9 = (bf16[5,96,128]{2,1,0:T(8,128)(2,1)S(1)}, bf16[5,96,128]{2,1,0:T(8,128)(2,1)S(1)}, u32[]{:S(2)}, u32[]{:S(2)}) collective-permute-start(bf16[5,96,128]{2,1,0:T(8,128)(2,1)S(1)} %get-tuple-element.16), channel_id=1, source_target_pairs={{0,24},{4,28},{8,0},{12,4},{16,8},{20,12},{24,16},{28,20},{32,56},... | collective-permute-start | bytes 368648 | tf_op jit(solution)/shard_map/ppermute | solution.py:417
  45.7 9.3 %collective-permute-start.10 = (bf16[5,96,128]{2,1,0:T(8,128)(2,1)S(1)}, bf16[5,96,128]{2,1,0:T(8,128)(2,1)S(1)}, u32[]{:S(2)}, u32[]{:S(2)}) collective-permute-start(bf16[5,96,128]{2,1,0:T(8,128)(2,1)S(1)} %add_convert_fusion._.halo0), channel_id=1, source_target_pairs={{0,1},{1,2},{2,3},{3,0},{4,5},{5,6},{6,7},{7,4},{8,9},{9,10},{10,1... | collective-permute-start | bytes 368648 | tf_op jit(solution)/shard_map/ppermute | solution.py:421
  47.0 9.8 %collective-permute-start.11 = (bf16[5,96,128]{2,1,0:T(8,128)(2,1)S(1)}, bf16[5,96,128]{2,1,0:T(8,128)(2,1)S(1)}, u32[]{:S(2)}, u32[]{:S(2)}) collective-permute-start(bf16[5,96,128]{2,1,0:T(8,128)(2,1)S(1)} %add_convert_fusion._.halo0), channel_id=1, source_target_pairs={{0,2},{1,3},{2,0},{3,1},{4,6},{5,7},{6,4},{7,5},{8,10},{9,11},{10,... | collective-permute-start | bytes 368648 | tf_op jit(solution)/shard_map/ppermute | solution.py:421

commit v3 on v2

--- a/solution.py
+++ b/solution.py
@@ -280,32 +280,26 @@
             windows[fr, yy] = jnp.zeros((3 * C, W), BF)
 
 
-def band_parts(band, columns, base):
-    parts = row_parts([(band, base + fr) for fr in range(2 * F)], 0, 2)
-    for fr in range(2 * F):
-        beside = [
-            jnp.concatenate([columns[base + fr, j + dx, dy] for dy in range(3) for dx in range(3)], axis=0)
-            for j in range(2)
-        ]
-        parts[fr] = jnp.concatenate([parts[fr]] + beside, axis=1)
+def band_parts(frames):
+    parts = row_parts([(band, f) for band, _, f in frames], 0, 2)
+    for n, (_, columns, f) in enumerate(frames):
+        beside = jnp.concatenate([columns[f, dx, dy] for dy in range(3) for dx in range(3)], axis=0)
+        parts[n] = jnp.concatenate([parts[n], beside], axis=1)
     return parts
 
 
-def put_column(columns, fr, k, value):
-    columns[fr, k, 0] = rotate(value, 1).astype(BF)
-    columns[fr, k, 1] = value.astype(BF)
-    columns[fr, k, 2] = rotate(value, W - 1).astype(BF)
-
-
-def outer_kernel(
-    table, inner, record0, second_own, second_prev, halo0, halo1, halo2, weights, vectors,
-    out, band1, columns1, band2, columns2
-):
+def put_columns(columns, f, values):
+    low = lanes(C) < 64
+    for k in range(3):
+        value = jnp.where(low, values[k], rotate(values[k + 1], 64))
+        columns[f, k, 0] = rotate(value, 1).astype(BF)
+        columns[f, k, 1] = value.astype(BF)
+        columns[f, k, 2] = rotate(value, W - 1).astype(BF)
+
+
+def border_windows(table, vectors, record, base, halo, exists, band, columns):
     up, left = sides(table)
-    bias1, gain1, gain2 = vectors[:, 0:1], vectors[:, 1:2], vectors[:, 2:3]
-    sources = ((second_prev, F * H, halo2), (second_own, F * H, halo1), (record0, 0, halo0))
-    lane = lanes(C)
-
+    gain = vectors[:, 1:2]
     src = lax.broadcasted_iota(jnp.int32, (W, 2 * W), 0)
     dst2 = lax.broadcasted_iota(jnp.int32, (W, 2 * W), 1)
     dst, col = dst2 % W, dst2 // W
@@ -316,67 +310,81 @@
     corner = jnp.where(up, above, below)
     past = jnp.where(up, 0, H + 2)
     first_col = jnp.where(left, 0, W - 2)
-    for fr in range(3 * F):
-        f = fr % F
-        record, base, halo = sources[fr // F]
-        exists = table[1] >= 2 - fr // F
+    for f in range(F):
         pick = (src == jnp.maximum(body, corner) + f * 32 + col).astype(F32).astype(BF)
         theirs = jnp.dot(halo[4], pick, preferred_element_type=F32)
-        theirs = norm_silu(jnp.where(exists, theirs, 0.0), gain1)
+        theirs = norm_silu(jnp.where(exists, theirs, 0.0), gain)
         picks = [(src == body + f * 32 + col).astype(F32).astype(BF)]
         for r in range(2):
             picks.append(((src == first_col + col) & (dst == past + r)).astype(F32).astype(BF))
         mine = jnp.concatenate([record[base + 4], halo[2 * f], halo[2 * f + 1]], axis=1)
         ours = jnp.dot(mine, jnp.concatenate(picks, axis=0), preferred_element_type=F32)
-        ours = norm_silu(jnp.where(exists, ours, 0.0), gain1)
+        ours = norm_silu(jnp.where(exists, ours, 0.0), gain)
         low, high = jnp.where(left, theirs, ours), jnp.where(left, ours, theirs)
-        for k in range(4):
-            put_column(columns1, fr, k, (low if k < 2 else high)[:, (k % 2) * W : (k % 2 + 1) * W])
+        put_columns(columns, f, [low[:, :W], low[:, W:], high[:, :W], high[:, W:]])
         near = jnp.where(left, theirs[:, W:], theirs[:, :W])
         for r in range(4):
             other, self = halo[2 * f + r % 2], record[base + 2 * f + r % 2]
             raw = jnp.where(up, other if r < 2 else self, self if r < 2 else other)
             at = jnp.where(up, r, H + r)
             moved = rotate(near, jnp.where(left, (W - at) % W, W - 1 - at))
-            center = norm_silu(jnp.where(exists, raw.astype(F32), 0.0), gain1)
+            center = norm_silu(jnp.where(exists, raw.astype(F32), 0.0), gain)
             put_window(
-                band1, (fr, r), three_shifts(center, jnp.where(left, moved, 0.0), jnp.where(left, 0.0, moved))
+                band, (f, r), three_shifts(center, jnp.where(left, moved, 0.0), jnp.where(left, 0.0, moved))
             )
 
+
+def own_border_kernel(table, record, halo, vectors, _, band, columns):
+    border_windows(table, vectors, record, 0, halo, True, band, columns)
+
+
+def outer_kernel(
+    table, inner, band0, columns0, second_own, second_prev, halo1, halo2, weights, vectors,
+    out, band1, columns1, band2, columns2, band, columns
+):
+    up, left = sides(table)
+    bias1, gain2 = vectors[:, 0:1], vectors[:, 2:3]
+    lane = lanes(C)
+    first_col = jnp.where(left, 0, W - 2)
+    border_windows(table, vectors, second_own, F * H, halo1, table[1] >= 1, band1, columns1)
+    border_windows(table, vectors, second_prev, F * H, halo2, table[1] >= 2, band2, columns2)
+    frames = [(b, c, f) for b, c in ((band2, columns2), (band1, columns1), (band0, columns0)) for f in range(F)]
+
     inside = (lane >= jnp.where(up, 3, 2)) & (lane < jnp.where(up, H + 2, H + 1))
-    row_at, col_at = jnp.where(up, 0, 2), jnp.where(left, 0, 2)
+    row_at = jnp.where(up, 0, 2)
     for p in range(2):
-        acc = product(weights.at[0], band_parts(band1, columns1, F * p))
+        acc = product(weights.at[0], band_parts(frames[F * p : F * p + 2 * F]))
         for f in range(F):
             s = F * p + f
             value = norm_silu(acc[f * C : (f + 1) * C] + bias1, gain2)
             if p == 0:
                 value = jnp.where(table[1] > 0, value, 0.0)
-            beside = [value[:, 2 * W : 3 * W], value[:, 3 * W :]]
+            beside = [value[:, 2 * W :], rotate(value[:, 2 * W :], 64)]
             near = jnp.where(left, beside[0], beside[1])
             for j in range(2):
                 at = jnp.where(up, 1 + j, H + 1 + j)
                 moved = rotate(near, jnp.where(left, W - at, W - 1 - at))
                 center = value[:, j * W : (j + 1) * W]
                 put_window(
-                    band2,
+                    band,
                     (s, row_at + j),
                     three_shifts(center, jnp.where(left, moved, 0.0), jnp.where(left, 0.0, moved)),
                 )
-                band2[s, 2 - row_at + j] = jnp.zeros((3 * C, W), BF)
-                put_column(columns2, s, col_at + j, jnp.where(inside, beside[j], 0.0))
-                columns2[s, 2 - col_at + j] = jnp.zeros((3, C, W), BF)
+                band[s, 2 - row_at + j] = jnp.zeros((3 * C, W), BF)
+            kept = [jnp.where(inside, b, 0.0) for b in beside]
+            low, high = [jnp.where(left, k, 0.0) for k in kept], [jnp.where(left, 0.0, k) for k in kept]
+            put_columns(columns, s, low + high)
 
     length = table[T_CLIP + table[T_LIST + table[0]] // TPC]
     start = table[1] * F
-    acc = product(weights.at[1], band_parts(band2, columns2, 0))
+    acc = product(weights.at[1], band_parts([(band, columns, s) for s in range(2 * F)]))
     for f in range(F):
         value = acc[f * C : (f + 1) * C]
         for y in range(H):
             total = inner[f, y]
             for j in range(2):
                 at = first_col + j
-                moved = rotate(value[:, (2 + j) * W : (3 + j) * W], (at + W - 2 - y) % W)
+                moved = rotate(value[:, 2 * W :], (at + 2 * W - 64 * j - 2 - y) % W)
                 total = total + jnp.where(lane == at, moved, 0.0)
             if y < 2:
                 total = total + jnp.where(up, value[:, y * W : (y + 1) * W], 0.0)
@@ -486,19 +494,23 @@
     inner = call(inner_second_kernel, whole, "svvv-", scratch, 16, 12 * 10**9)(
         table, own_two, second_prev, weights, halo
     )
+    edges = [shape(F, 4, 3 * C, W), shape(F, 3, 3, C, W)]
+    border0 = call(own_border_kernel, edges, "svvv-")(table, record, halo, vectors, inner)
     out = call(
         outer_kernel,
         shape(F, H, C, W),
         "s" + "v" * 9,
         [
-            pltpu.VMEM((3 * F, 4, 3 * C, W), BF),
-            pltpu.VMEM((3 * F, 4, 3, C, W), BF),
+            pltpu.VMEM((F, 4, 3 * C, W), BF),
+            pltpu.VMEM((F, 3, 3, C, W), BF),
+            pltpu.VMEM((F, 4, 3 * C, W), BF),
+            pltpu.VMEM((F, 3, 3, C, W), BF),
             pltpu.VMEM((2 * F, 4, 3 * C, W), BF),
-            pltpu.VMEM((2 * F, 4, 3, C, W), BF),
+            pltpu.VMEM((2 * F, 3, 3, C, W), BF),
         ],
         24,
         4 * 10**9,
-    )(table, inner, record, second, second_prev, halo, halo1, halo2, weights, vectors)
+    )(table, inner, *border0, second, second_prev, halo1, halo2, weights, vectors)
     return out.transpose(0, 2, 1, 3)[None]
 
 

time: 63.4 us -> 64.5 us (1.017)
  waiting for transfers between devices: 11.8 us -> 9.25 us
  starting transfers between devices: 23.8 us -> 26.1 us
  Pallas kernels: 22.4 us -> 23.6 us
    ppermute x4, waiting for transfers between devices: 5.95 us -> 2.8 us  [later(): return lax.ppermute(array, 'group', [(i, (i + by) % NX) for i in range(NX)])]
    ppermute x8, starting transfers between devices: 17.7 us -> 20.2 us  [send(): return lax.ppermute(array, 'tile', pairs(move))]
    pallas_call x1 -> x2, Pallas kernels: 5.26 us -> 6.43 us  [the longest x1 5.14 us: per_device(): call(outer_kernel, shape(F, H, C, W), 's' + 'v' * 9, [pltpu.VMEM((F, 4, 3...]
  transfers between devices with their start and end apart: 12 -> 12, of which waited for: 8 -> 6; matrix products, arithmetic and copies ran while one was open for 2% -> 2% of each run, Pallas kernels for 27% -> 29%
where the time goes in v3:
time: 64.5 us; the launch traced here: 64 us
  starting transfers between devices  26.1 us (40%)
  Pallas kernels  23.6 us (37%)
  waiting for transfers between devices  9.25 us (14%)
  local copies, waits for them, and re-layouts  4.59 us (7%)
    ppermute x8, starting transfers between devices, send(): return lax.ppermute(array, 'tile', pairs(move))  20.2 us
    ppermute x8, waiting for transfers between devices, send(): return lax.ppermute(array, 'tile', pairs(move))  6.46 us
    ppermute x4, starting transfers between devices, later(): return lax.ppermute(array, 'group', [(i, (i + by) % NX) for i in range(NX)])  5.94 us
    pallas_call x1, Pallas kernels, per_device(): call(outer_kernel, shape(F, H, C, W), 's' + 'v' * 9, [pltpu.VMEM((F, 4, 3...  5.14 us
    pallas_call x1, Pallas kernels, per_device(): call(inner_first_kernel, shape(F * H + REC, C, W), 'svvvv-s', scratch, 16...  4.3 us
    ppermute x4, waiting for transfers between devices, later(): return lax.ppermute(array, 'group', [(i, (i + by) % NX) for i in range(NX)])  2.8 us
    unnamed x28, local copies, waits for them, and re-layouts  2.52 us
    pallas_call x1, Pallas kernels, per_device(): pl.pallas_call(plan_kernel, out_shape=jax.ShapeDtypeStruct((12 * NY,), jn...  2.44 us
  transfers between devices with their start and end apart: 12, of which 6 were waited for; matrix products, arithmetic and copies ran while one was open for 2% of the time, Pallas kernels for 29%

profile of v3, /device:TPU:1, one launch (start us, length us, event | category | flops | bytes accessed | tf_op | source)
XLA Modules:
  0.0 64.0 jit_solution(16266764622742460770)
XLA Ops:
  0.1 1.4 %copy.33 = bf16[1,2,96,16,128]{4,2,3,1,0:T(8,128)(2,1)S(1)} copy(bf16[1,2,96,16,128]{4,3,2,1,0:T(8,128)(2,1)} %param.10) | data formatting | bytes 1572864 | tf_op args[0]
  1.5 2.1 %collective-permute-start = (bf16[2,16,96,128]{3,2,1,0:T(8,128)(2,1)S(1)}, bf16[2,16,96,128]{3,2,1,0:T(8,128)(2,1)}, u32[]{:S(2)}, u32[]{:S(2)}) collective-permute-start(bf16[2,16,96,128]{3,2,1,0:T(8,128)(2,1)S(1)} %bitcast.19), channel_id=1, source_target_pairs={{0,1},{1,2},{2,3},{3,0},{4,5},{5,6},{6,7},{7,4},{8,9},{9,10},{10,1... | collective-permute-start | bytes 2359304 | tf_op jit(solution)/shard_map/ppermute | solution.py:429
  3.7 1.0 %shard_map.100.record = bf16[5,96,128]{2,1,0:T(8,128)(2,1)S(1)} custom-call(s32[2]{0:T(128)S(1)} %pad_add_fusion.ids, s32[64]{0:T(128)S(1)} %copy-done.7, s32[8,64]{1,0:T(8,128)S(1)} %bitcast.27, bf16[2,16,96,128]{3,2,1,0:T(8,128)(2,1)S(1)} %bitcast.20), custom_call_target="tpu_custom_call" | custom-call | bytes 1048576 | tf_op jit(solution)/shard_map/pallas_call | solution.py:470
  4.7 1.3 %collective-permute-start.1 = (bf16[5,96,128]{2,1,0:T(8,128)(2,1)S(1)}, bf16[5,96,128]{2,1,0:T(8,128)(2,1)S(1)}, u32[]{:S(2)}, u32[]{:S(2)}) collective-permute-start(bf16[5,96,128]{2,1,0:T(8,128)(2,1)S(1)} %shard_map.100.record), channel_id=1, source_target_pairs={{0,4},{4,0},{8,12},{12,8},{16,20},{20,16},{24,28},{28,24},{32,36},... | collective-permute-start | bytes 368648 | tf_op jit(solution)/shard_map/ppermute | solution.py:425
  6.3 0.7 %concatenate.7.table = s32[594]{0:T(1024)} concatenate(s32[1]{0:T(128)} %bitcast, s32[1]{0:T(128)} %bitcast.1, s32[64]{0:T(128)S(1)} %copy-done.7, s32[512]{0:T(512)S(1)} %reshape.9, s32[16]{0:T(128)S(1)} %copy-done.8), dimensions={0} | concatenate | bytes 4752 | tf_op jit(solution)/shard_map/concatenate | solution.py:459
  7.0 5.8 %collective-permute-start.4 = (bf16[2,5,96,128]{3,2,1,0:T(8,128)(2,1)S(1)}, bf16[2,5,96,128]{3,2,1,0:T(8,128)(2,1)S(1)}, u32[]{:S(2)}, u32[]{:S(2)}) collective-permute-start(bf16[2,5,96,128]{3,2,1,0:T(8,128)(2,1)S(1)} %pad_maximum_fusion.1._.t0), channel_id=1, source_target_pairs={{0,64},{4,196},{8,72},{12,204},{16,80},{20,212},{24,88},{28,220},{... | collective-permute-start | bytes 737288 | tf_op jit(solution)/shard_map/ppermute | solution.py:425
  12.9 0.7 %collective-permute-start.2 = (bf16[2,5,96,128]{3,2,1,0:T(8,128)(2,1)S(1)}, bf16[2,5,96,128]{3,2,1,0:T(8,128)(2,1)S(1)}, u32[]{:S(2)}, u32[]{:S(2)}) collective-permute-start(bf16[2,5,96,128]{3,2,1,0:T(8,128)(2,1)S(1)} %pad_maximum_fusion.1._.t0), channel_id=1, source_target_pairs={{0,32},{4,228},{8,40},{12,236},{16,48},{20,244},{24,56},{28,252},{... | collective-permute-start | bytes 737288 | tf_op jit(solution)/shard_map/ppermute | solution.py:425
  13.6 2.4 %shard_map.103._plan.plan = s32[48]{0:T(128)} custom-call(s32[594]{0:T(1024)} %concatenate.7.table, bf16[2,5,96,128]{3,2,1,0:T(8,128)(2,1)} %copy-done), custom_call_target="tpu_custom_call" | custom-call | tf_op jit(solution)/shard_map/pallas_call | solution.py:475
  16.1 0.9 %copy-done.1 = bf16[2,5,96,128]{3,2,1,0:T(8,128)(2,1)S(1)} copy-done((bf16[2,5,96,128]{3,2,1,0:T(8,128)(2,1)S(1)}, bf16[2,5,96,128]{3,2,1,0:T(8,128)(2,1)}, u32[]{:S(2)}) %copy-start.1) | copy-done | bytes 245784
  17.0 0.6 shard_map.101.weights
  17.6 2.4 %shard_map.102.partial = f32[8,192,256]{2,1,0:T(8,128)S(1)} custom-call(bf16[2,16,96,128]{3,2,1,0:T(8,128)(2,1)S(1)} %bitcast.21, bf16[2,192,3584]{2,1,0:T(8,128)(2,1)S(1)} %shard_map.101.weights, f32[96,4]{1,0:T(8,128)S(1)} %copy.26.vectors), custom_call_target="tpu_custom_call" | custom-call | flops 3000000000 | bytes 1048576 | tf_op jit(solution)/shard_map/pallas_call | solution.py:483
  20.0 1.4 %collective-permute-done.2._.t1 = bf16[2,5,96,128]{3,2,1,0:T(8,128)(2,1)S(1)} collective-permute-done((bf16[2,5,96,128]{3,2,1,0:T(8,128)(2,1)S(1)}, bf16[2,5,96,128]{3,2,1,0:T(8,128)(2,1)S(1)}, u32[]{:S(2)}, u32[]{:S(2)}) %collective-permute-start.2) | collective-permute-done | bytes 245792 | tf_op jit(solution)/shard_map/ppermute | solution.py:425
  21.5 2.7 %collective-permute-start.5 = (bf16[3,5,96,128]{3,2,1,0:T(8,128)(2,1)S(1)}, bf16[3,5,96,128]{3,2,1,0:T(8,128)(2,1)S(1)}, u32[]{:S(2)}, u32[]{:S(2)}) collective-permute-start(bf16[3,5,96,128]{3,2,1,0:T(8,128)(2,1)S(1)} %pad_maximum_fusion), channel_id=1, source_target_pairs={{0,64},{4,196},{8,72},{12,204},{16,80},{20,212},{24,88},{28,220},{... | collective-permute-start | bytes 1105928 | tf_op jit(solution)/shard_map/ppermute | solution.py:425
  24.2 4.3 %shard_map.104.second._.second_own = bf16[37,96,128]{2,1,0:T(8,128)(2,1)S(1)} custom-call(s32[594]{0:T(1024)S(1)} %copy-done.4, bf16[2,16,96,128]{3,2,1,0:T(8,128)(2,1)} %collective-permute-done.prev, f32[8,192,256]{2,1,0:T(8,128)S(1)} %shard_map.102.partial, bf16[2,192,3584]{2,1,0:T(8,128)(2,1)S(1)} %shard_map.101.weights, f32[96,4]{1,0:T(8,128)S(1)} %copy.26.vectors, ...), custom_call_target="tpu_custom_call" | custom-call | flops 8000000000 | bytes 1048576 | tf_op jit(solution)/shard_map/pallas_call | solution.py:486
  28.5 1.3 %collective-permute-start.3 = (bf16[37,96,128]{2,1,0:T(8,128)(2,1)S(1)}, bf16[37,96,128]{2,1,0:T(8,128)(2,1)S(1)}, u32[]{:S(2)}, u32[]{:S(2)}) collective-permute-start(bf16[37,96,128]{2,1,0:T(8,128)(2,1)S(1)} %shard_map.104.second._.second_own), channel_id=1, source_target_pairs={{0,1},{1,2},{2,3},{3,0},{4,5},{5,6},{6,7},{7,4},{8,9},{9,10},{10,1... | collective-permute-start | bytes 2727944 | tf_op jit(solution)/shard_map/ppermute | solution.py:429
  29.8 1.8 %collective-permute-done.5.t3 = bf16[3,5,96,128]{3,2,1,0:T(8,128)(2,1)S(1)} collective-permute-done((bf16[3,5,96,128]{3,2,1,0:T(8,128)(2,1)S(1)}, bf16[3,5,96,128]{3,2,1,0:T(8,128)(2,1)S(1)}, u32[]{:S(2)}, u32[]{:S(2)}) %collective-permute-start.5) | collective-permute-done | bytes 368672 | tf_op jit(solution)/shard_map/ppermute | solution.py:425
  31.6 1.6 %shard_map.106 = (bf16[4,5,96,128]{3,2,1,0:T(8,128)(2,1)S(1)}, bf16[4,5,96,128]{3,2,1,0:T(8,128)(2,1)S(1)}) custom-call(s32[48]{0:T(128)S(1)} %copy-done.6, bf16[2,5,96,128]{3,2,1,0:T(8,128)(2,1)S(1)} %copy-done.1, bf16[2,5,96,128]{3,2,1,0:T(8,128)(2,1)S(1)} %collective-permute-done.2._.t1, bf16[2,5,96,128]{3,2,1,0:T(8,128)(2,1)S(1)} %collective-permute-done.4.t2, ...), custom_call_target="tpu_custom_call" | custom-call | bytes 1048576 | tf_op jit(solution)/shard_map/pallas_call | solution.py:446
  33.3 3.9 %collective-permute-start.6 = (bf16[4,5,96,128]{3,2,1,0:T(8,128)(2,1)S(1)}, bf16[4,5,96,128]{3,2,1,0:T(8,128)(2,1)S(1)}, u32[]{:S(2)}, u32[]{:S(2)}) collective-permute-start(bf16[4,5,96,128]{3,2,1,0:T(8,128)(2,1)S(1)} %get-tuple-element.14), channel_id=1, source_target_pairs={{0,4},{4,0},{8,12},{12,8},{16,20},{20,16},{24,28},{28,24},{32,36},... | collective-permute-start | bytes 1474568 | tf_op jit(solution)/shard_map/ppermute | solution.py:425
  37.2 1.5 %collective-permute-done.6.arrived = bf16[4,5,96,128]{3,2,1,0:T(8,128)(2,1)S(1)} collective-permute-done((bf16[4,5,96,128]{3,2,1,0:T(8,128)(2,1)S(1)}, bf16[4,5,96,128]{3,2,1,0:T(8,128)(2,1)S(1)}, u32[]{:S(2)}, u32[]{:S(2)}) %collective-permute-start.6) | collective-permute-done | bytes 491552 | tf_op jit(solution)/shard_map/ppermute | solution.py:425
  38.7 0.7 %shard_map.107 = (bf16[5,96,128]{2,1,0:T(8,128)(2,1)S(1)}, bf16[5,96,128]{2,1,0:T(8,128)(2,1)S(1)}, bf16[5,96,128]{2,1,0:T(8,128)(2,1)S(1)}, bf16[5,96,128]{2,1,0:T(8,128)(2,1)S(1)}) custom-call(s32[594]{0:T(1024)S(1)} %copy-done.4, bf16[4,5,96,128]{3,2,1,0:T(8,128)(2,1)S(1)} %get-tuple-element.13.mine, ...), custom_call_target="tpu_custom_call" | custom-call | bytes 1048576 | tf_op jit(solution)/shard_map/pallas_call | solution.py:448
  39.4 3.0 %collective-permute-start.7 = (bf16[5,96,128]{2,1,0:T(8,128)(2,1)S(1)}, bf16[5,96,128]{2,1,0:T(8,128)(2,1)S(1)}, u32[]{:S(2)}, u32[]{:S(2)}) collective-permute-start(bf16[5,96,128]{2,1,0:T(8,128)(2,1)S(1)} %get-tuple-element.16), channel_id=1, source_target_pairs={{0,16},{4,20},{8,24},{12,28},{16,0},{20,4},{24,8},{28,12},{32,48},... | collective-permute-start | bytes 368648 | tf_op jit(solution)/shard_map/ppermute | solution.py:425
  42.4 0.4 collective-permute-start.8
  42.8 2.3 %collective-permute-start.9 = (bf16[5,96,128]{2,1,0:T(8,128)(2,1)S(1)}, bf16[5,96,128]{2,1,0:T(8,128)(2,1)S(1)}, u32[]{:S(2)}, u32[]{:S(2)}) collective-permute-start(bf16[5,96,128]{2,1,0:T(8,128)(2,1)S(1)} %get-tuple-element.18), channel_id=1, source_target_pairs={{0,24},{4,28},{8,0},{12,4},{16,8},{20,12},{24,16},{28,20},{32,56},... | collective-permute-start | bytes 368648 | tf_op jit(solution)/shard_map/ppermute | solution.py:425
  45.1 1.8 %shard_map.105.partial = f32[2,16,96,128]{3,2,1,0:T(8,128)S(1)} custom-call(bf16[2,16,96,128]{3,2,1,0:T(8,128)(2,1)S(1)} %bitcast.22, bf16[37,96,128]{2,1,0:T(8,128)(2,1)S(1)} %shard_map.104.second._.second_own, bf16[2,192,3584]{2,1,0:T(8,128)(2,1)S(1)} %shard_map.101.weights, f32[96,4]{1,0:T(8,128)S(1)} %copy.26.vectors), custom_call_target="tpu_custom_call" | custom-call | flops 1000000000 | bytes 1048576 | tf_op jit(solution)/shard_map/pallas_call | solution.py:490
  46.9 1.7 %collective-permute-done.8 = bf16[5,96,128]{2,1,0:T(8,128)(2,1)S(1)} collective-permute-done((bf16[5,96,128]{2,1,0:T(8,128)(2,1)S(1)}, bf16[5,96,128]{2,1,0:T(8,128)(2,1)S(1)}, u32[]{:S(2)}, u32[]{:S(2)}) %collective-permute-start.8) | collective-permute-done | bytes 122912 | tf_op jit(solution)/shard_map/ppermute | solution.py:425
  48.7 2.5 %collective-permute-start.11 = (bf16[5,96,128]{2,1,0:T(8,128)(2,1)S(1)}, bf16[5,96,128]{2,1,0:T(8,128)(2,1)S(1)}, u32[]{:S(2)}, u32[]{:S(2)}) collective-permute-start(bf16[5,96,128]{2,1,0:T(8,128)(2,1)S(1)} %add_convert_fusion._.halo), channel_id=1, source_target_pairs={{0,2},{1,3},{2,0},{3,1},{4,6},{5,7},{6,4},{7,5},{8,10},{9,11},{10,... | collective-permute-start | bytes 368648 | tf_op jit(solution)/shard_map/ppermute | solution.py:429
  51.2 0.6 collective-permute-done.3.second_prev
  51.8 2.4 %shard_map.108._.inner = f32[2,16,96,128]{3,2,1,0:T(8,128)S(1)} custom-call(s32[594]{0:T(1024)S(1)} %copy-done.4, f32[2,16,96,128]{3,2,1,0:T(8,128)S(1)} %shard_map.105.partial, bf16[37,96,128]{2,1,0:T(8,128)(2,1)S(1)} %collective-permute-done.3.second_prev, bf16[2,192,3584]{2,1,0:T(8,128)(2,1)S(1)} %shard_map.101.weights, ...), custom_call_target="tpu_custom_call" | custom-call | flops 12000000000 | bytes 1048576 | tf_op jit(solution)/shard_map/pallas_call | solution.py:494
  54.2 1.3 %shard_map.109 = (bf16[2,4,288,128]{3,2,1,0:T(8,128)(2,1)S(1)}, bf16[2,3,3,96,128]{4,3,2,1,0:T(8,128)(2,1)S(1)}) custom-call(s32[594]{0:T(1024)S(1)} %copy-done.4, bf16[5,96,128]{2,1,0:T(8,128)(2,1)S(1)} %shard_map.100.record, bf16[5,96,128]{2,1,0:T(8,128)(2,1)S(1)} %add_convert_fusion._.halo, f32[96,4]{1,0:T(8,128)S(1)} %copy.26.vectors, ...), custom_call_target="tpu_custom_call" | custom-call | bytes 1048576 | tf_op jit(solution)/shard_map/pallas_call | solution.py:498
  55.5 2.2 %collective-permute-done.10.halo1 = bf16[5,96,128]{2,1,0:T(8,128)(2,1)S(1)} collective-permute-done((bf16[5,96,128]{2,1,0:T(8,128)(2,1)S(1)}, bf16[5,96,128]{2,1,0:T(8,128)(2,1)S(1)}, u32[]{:S(2)}, u32[]{:S(2)}) %collective-permute-start.10) | collective-permute-done | bytes 122912 | tf_op jit(solution)/shard_map/ppermute | solution.py:429
  57.7 5.1 %shard_map.110 = bf16[2,16,96,128]{3,2,1,0:T(8,128)(2,1)S(1)} custom-call(s32[594]{0:T(1024)S(1)} %copy-done.4, f32[2,16,96,128]{3,2,1,0:T(8,128)S(1)} %shard_map.108._.inner, bf16[2,4,288,128]{3,2,1,0:T(8,128)(2,1)S(1)} %get-tuple-element.19.band0, bf16[2,3,3,96,128]{4,3,2,1,0:T(8,128)(2,1)S(1)} %get-tuple-element.20.columns0, ...), custom_call_target="tpu_custom_call" | custom-call | flops 4000000000 | bytes 1048576 | tf_op jit(solution)/shard_map/pallas_call | solution.py:499
  62.8 1.2 %copy.31 = bf16[1,2,96,16,128]{4,3,2,1,0:T(8,128)(2,1)} copy(bf16[1,2,96,16,128]{4,2,3,1,0:T(8,128)(2,1)S(1)} %bitcast.24) | data formatting | bytes 1572864 | tf_op jit(solution)/shard_map/broadcast_in_dim | solution.py:514
  (41 shorter events, 0.6 us)
Async XLA Ops:
  0.0 3.7 %copy-start.7 = (s32[64]{0:T(128)S(1)}, s32[64]{0:T(128)}, u32[]{:S(2)}) copy-start(s32[64]{0:T(128)} %tiles.1) | copy-start | bytes 772
  0.0 3.7 %copy-start.5 = (s32[64,8]{0,1:T(8,128)S(1)}, s32[64,8]{0,1:T(8,128)}, u32[]{:S(2)}) copy-start(s32[64,8]{0,1:T(8,128)} %param.12) | copy-start | bytes 6148
  0.0 6.1 %copy-start.9 = (f32[96]{0:T(128)S(1)}, f32[96]{0:T(128)}, u32[]{:S(2)}) copy-start(f32[96]{0:T(128)} %param.19) | copy-start | bytes 1156
  0.0 6.1 %copy-start.10 = (f32[96]{0:T(128)S(1)}, f32[96]{0:T(128)}, u32[]{:S(2)}) copy-start(f32[96]{0:T(128)} %param.17) | copy-start | bytes 1156
  0.0 6.1 %copy-start.12 = (f32[96]{0:T(128)S(1)}, f32[96]{0:T(128)}, u32[]{:S(2)}) copy-start(f32[96]{0:T(128)} %param.16) | copy-start | bytes 1156
  0.0 6.1 %copy-start.11 = (f32[96]{0:T(128)S(1)}, f32[96]{0:T(128)}, u32[]{:S(2)}) copy-start(f32[96]{0:T(128)} %param.14) | copy-start | bytes 1156
  0.0 6.3 %copy-start.8 = (s32[16]{0:T(128)S(1)}, s32[16]{0:T(128)}, u32[]{:S(2)}) copy-start(s32[16]{0:T(128)} %param.13) | copy-start | bytes 196
  0.0 16.0 %copy-start.3 = (bf16[3,3,3,96,96]{4,3,2,1,0:T(8,128)(2,1)S(1)}, bf16[3,3,3,96,96]{4,3,2,1,0:T(8,128)(2,1)}, u32[]{:S(2)}) copy-start(bf16[3,3,3,96,96]{4,3,2,1,0:T(8,128)(2,1)} %param.18) | copy-start | bytes 1492996
  0.1 16.0 %copy-start.2 = (bf16[3,3,3,96,96]{4,3,2,1,0:T(8,128)(2,1)S(1)}, bf16[3,3,3,96,96]{4,3,2,1,0:T(8,128)(2,1)}, u32[]{:S(2)}) copy-start(bf16[3,3,3,96,96]{4,3,2,1,0:T(8,128)(2,1)} %param.15) | copy-start | bytes 1492996
  1.5 22.7 %collective-permute-start = (bf16[2,16,96,128]{3,2,1,0:T(8,128)(2,1)S(1)}, bf16[2,16,96,128]{3,2,1,0:T(8,128)(2,1)}, u32[]{:S(2)}, u32[]{:S(2)}) collective-permute-start(bf16[2,16,96,128]{3,2,1,0:T(8,128)(2,1)S(1)} %bitcast.19), channel_id=1, source_target_pairs={{0,1},{1,2},{2,3},{3,0},{4,5},{5,6},{6,7},{7,4},{8,9},{9,10},{10,1... | collective-permute-start | bytes 2359304 | tf_op jit(solution)/shard_map/ppermute | solution.py:429
  4.7 2.3 %collective-permute-start.1 = (bf16[5,96,128]{2,1,0:T(8,128)(2,1)S(1)}, bf16[5,96,128]{2,1,0:T(8,128)(2,1)S(1)}, u32[]{:S(2)}, u32[]{:S(2)}) collective-permute-start(bf16[5,96,128]{2,1,0:T(8,128)(2,1)S(1)} %shard_map.100.record), channel_id=1, source_target_pairs={{0,4},{4,0},{8,12},{12,8},{16,20},{20,16},{24,28},{28,24},{32,36},... | collective-permute-start | bytes 368648 | tf_op jit(solution)/shard_map/ppermute | solution.py:425
  7.0 6.6 %copy-start = (bf16[2,5,96,128]{3,2,1,0:T(8,128)(2,1)}, bf16[2,5,96,128]{3,2,1,0:T(8,128)(2,1)S(1)}, u32[]{:S(2)}) copy-start(bf16[2,5,96,128]{3,2,1,0:T(8,128)(2,1)S(1)} %pad_maximum_fusion.1._.t0) | copy-start | bytes 737284
  7.0 13.0 %collective-permute-start.4 = (bf16[2,5,96,128]{3,2,1,0:T(8,128)(2,1)S(1)}, bf16[2,5,96,128]{3,2,1,0:T(8,128)(2,1)S(1)}, u32[]{:S(2)}, u32[]{:S(2)}) collective-permute-start(bf16[2,5,96,128]{3,2,1,0:T(8,128)(2,1)S(1)} %pad_maximum_fusion.1._.t0), channel_id=1, source_target_pairs={{0,64},{4,196},{8,72},{12,204},{16,80},{20,212},{24,88},{28,220},{... | collective-permute-start | bytes 737288 | tf_op jit(solution)/shard_map/ppermute | solution.py:425
  12.9 8.6 %collective-permute-start.2 = (bf16[2,5,96,128]{3,2,1,0:T(8,128)(2,1)S(1)}, bf16[2,5,96,128]{3,2,1,0:T(8,128)(2,1)S(1)}, u32[]{:S(2)}, u32[]{:S(2)}) collective-permute-start(bf16[2,5,96,128]{3,2,1,0:T(8,128)(2,1)S(1)} %pad_maximum_fusion.1._.t0), channel_id=1, source_target_pairs={{0,32},{4,228},{8,40},{12,236},{16,48},{20,244},{24,56},{28,252},{... | collective-permute-start | bytes 737288 | tf_op jit(solution)/shard_map/ppermute | solution.py:425
  16.1 0.9 %copy-start.1 = (bf16[2,5,96,128]{3,2,1,0:T(8,128)(2,1)S(1)}, bf16[2,5,96,128]{3,2,1,0:T(8,128)(2,1)}, u32[]{:S(2)}) copy-start(bf16[2,5,96,128]{3,2,1,0:T(8,128)(2,1)} %copy-done) | copy-start | bytes 737284
  17.6 6.6 %copy-start.4 = (s32[594]{0:T(1024)S(1)}, s32[594]{0:T(1024)}, u32[]{:S(2)}) copy-start(s32[594]{0:T(1024)} %concatenate.7.table) | copy-start | bytes 7132
  17.6 6.6 %copy-start.6 = (s32[48]{0:T(128)S(1)}, s32[48]{0:T(128)}, u32[]{:S(2)}) copy-start(s32[48]{0:T(128)} %shard_map.103._plan.plan) | copy-start | bytes 580
  21.5 10.2 %collective-permute-start.5 = (bf16[3,5,96,128]{3,2,1,0:T(8,128)(2,1)S(1)}, bf16[3,5,96,128]{3,2,1,0:T(8,128)(2,1)S(1)}, u32[]{:S(2)}, u32[]{:S(2)}) collective-permute-start(bf16[3,5,96,128]{3,2,1,0:T(8,128)(2,1)S(1)} %pad_maximum_fusion), channel_id=1, source_target_pairs={{0,64},{4,196},{8,72},{12,204},{16,80},{20,212},{24,88},{28,220},{... | collective-permute-start | bytes 1105928 | tf_op jit(solution)/shard_map/ppermute | solution.py:425
  28.5 23.3 %collective-permute-start.3 = (bf16[37,96,128]{2,1,0:T(8,128)(2,1)S(1)}, bf16[37,96,128]{2,1,0:T(8,128)(2,1)S(1)}, u32[]{:S(2)}, u32[]{:S(2)}) collective-permute-start(bf16[37,96,128]{2,1,0:T(8,128)(2,1)S(1)} %shard_map.104.second._.second_own), channel_id=1, source_target_pairs={{0,1},{1,2},{2,3},{3,0},{4,5},{5,6},{6,7},{7,4},{8,9},{9,10},{10,1... | collective-permute-start | bytes 2727944 | tf_op jit(solution)/shard_map/ppermute | solution.py:429
  33.3 5.4 %collective-permute-start.6 = (bf16[4,5,96,128]{3,2,1,0:T(8,128)(2,1)S(1)}, bf16[4,5,96,128]{3,2,1,0:T(8,128)(2,1)S(1)}, u32[]{:S(2)}, u32[]{:S(2)}) collective-permute-start(bf16[4,5,96,128]{3,2,1,0:T(8,128)(2,1)S(1)} %get-tuple-element.14), channel_id=1, source_target_pairs={{0,4},{4,0},{8,12},{12,8},{16,20},{20,16},{24,28},{28,24},{32,36},... | collective-permute-start | bytes 1474568 | tf_op jit(solution)/shard_map/ppermute | solution.py:425
  39.4 7.5 %collective-permute-start.7 = (bf16[5,96,128]{2,1,0:T(8,128)(2,1)S(1)}, bf16[5,96,128]{2,1,0:T(8,128)(2,1)S(1)}, u32[]{:S(2)}, u32[]{:S(2)}) collective-permute-start(bf16[5,96,128]{2,1,0:T(8,128)(2,1)S(1)} %get-tuple-element.16), channel_id=1, source_target_pairs={{0,16},{4,20},{8,24},{12,28},{16,0},{20,4},{24,8},{28,12},{32,48},... | collective-permute-start | bytes 368648 | tf_op jit(solution)/shard_map/ppermute | solution.py:425
  42.4 6.2 %collective-permute-start.8 = (bf16[5,96,128]{2,1,0:T(8,128)(2,1)S(1)}, bf16[5,96,128]{2,1,0:T(8,128)(2,1)S(1)}, u32[]{:S(2)}, u32[]{:S(2)}) collective-permute-start(bf16[5,96,128]{2,1,0:T(8,128)(2,1)S(1)} %get-tuple-element.17), channel_id=1, source_target_pairs={{0,8},{4,12},{8,16},{12,20},{16,24},{20,28},{24,0},{28,4},{32,40},... | collective-permute-start | bytes 368648 | tf_op jit(solution)/shard_map/ppermute | solution.py:425
  42.8 5.8 %collective-permute-start.9 = (bf16[5,96,128]{2,1,0:T(8,128)(2,1)S(1)}, bf16[5,96,128]{2,1,0:T(8,128)(2,1)S(1)}, u32[]{:S(2)}, u32[]{:S(2)}) collective-permute-start(bf16[5,96,128]{2,1,0:T(8,128)(2,1)S(1)} %get-tuple-element.18), channel_id=1, source_target_pairs={{0,24},{4,28},{8,0},{12,4},{16,8},{20,12},{24,16},{28,20},{32,56},... | collective-permute-start | bytes 368648 | tf_op jit(solution)/shard_map/ppermute | solution.py:425
  48.7 6.8 %collective-permute-start.11 = (bf16[5,96,128]{2,1,0:T(8,128)(2,1)S(1)}, bf16[5,96,128]{2,1,0:T(8,128)(2,1)S(1)}, u32[]{:S(2)}, u32[]{:S(2)}) collective-permute-start(bf16[5,96,128]{2,1,0:T(8,128)(2,1)S(1)} %add_convert_fusion._.halo), channel_id=1, source_target_pairs={{0,2},{1,3},{2,0},{3,1},{4,6},{5,7},{6,4},{7,5},{8,10},{9,11},{10,... | collective-permute-start | bytes 368648 | tf_op jit(solution)/shard_map/ppermute | solution.py:429
  51.2 6.5 %collective-permute-start.10 = (bf16[5,96,128]{2,1,0:T(8,128)(2,1)S(1)}, bf16[5,96,128]{2,1,0:T(8,128)(2,1)S(1)}, u32[]{:S(2)}, u32[]{:S(2)}) collective-permute-start(bf16[5,96,128]{2,1,0:T(8,128)(2,1)S(1)} %add_convert_fusion._.halo), channel_id=1, source_target_pairs={{0,1},{1,2},{2,3},{3,0},{4,5},{5,6},{6,7},{7,4},{8,9},{9,10},{10,1... | collective-permute-start | bytes 368648 | tf_op jit(solution)/shard_map/ppermute | solution.py:429

commit v4 on v2

--- a/solution.py
+++ b/solution.py
@@ -62,12 +62,17 @@
             moved = rotate(features[f, y].astype(F32), at + turn)
             columns = jnp.where(lane // 2 == at // 2, moved, columns)
     out[base + 4] = jnp.where(lane < 64, columns, rotate(columns, 64)).astype(BF)
-
-
-def record_kernel(ids, tiles, near, features, out):
+    return columns
+
+
+def record_kernel(ids, tiles, near, features, out, packed):
     tile = tiles[ids[0]]
     up, left = near[1, tile] >= 0, near[3, tile] >= 0
-    write_record(features, up, left, out, 0)
+    columns = write_record(features, up, left, out, 0)
+    for n in range(2 * F):
+        packed[2 * n] = out[n, 0 : C // 2]
+        packed[2 * n + 1] = out[n, C // 2 :]
+    packed[4 * F] = jnp.where(lanes(C // 2) < 64, columns[: C // 2], rotate(columns[C // 2 :], 64)).astype(BF)
 
 
 def weights_kernel(one, two, _, out):
@@ -116,6 +121,13 @@
             out[6 * n + 2 * k + 1] = index
 
 
+def unpack_columns(block):
+    values = block.astype(F32)
+    turned, low = rotate(values, 64), lanes(C // 2) < 64
+    both = [jnp.where(low, values, turned), jnp.where(low, turned, values)]
+    return jnp.concatenate(both, axis=0).astype(BF)
+
+
 def select_kernel(plan, t0, t1, t2, t3, _, mine, other):
     held = (t0, t1, t2, t3)
     mine[...] = jnp.zeros_like(mine)
@@ -127,15 +139,17 @@
 
             @pl.when(plan[6 * n] == k)
             def _():
-                out[yd, 0:4] = ref[plan[6 * n + 1], 0:4]
+                for b in range(2 * F):
+                    out[yd, b, 0 : C // 2] = ref[plan[6 * n + 1], 2 * b]
+                    out[yd, b, C // 2 :] = ref[plan[6 * n + 1], 2 * b + 1]
 
             @pl.when(plan[6 * n + 2] == k)
             def _():
-                out[yd, 4] = jnp.where(low, ref[plan[6 * n + 3], 4], out[yd, 4])
+                out[yd, 4] = jnp.where(low, unpack_columns(ref[plan[6 * n + 3], 4 * F]), out[yd, 4])
 
             @pl.when(plan[6 * n + 4] == k)
             def _():
-                out[yd, 4] = jnp.where(low, out[yd, 4], ref[plan[6 * n + 5], 4])
+                out[yd, 4] = jnp.where(low, out[yd, 4], unpack_columns(ref[plan[6 * n + 5], 4 * F]))
 
 
 def combine_kernel(table, mine, arrived, own, one, two, three):
@@ -459,8 +473,8 @@
     vectors = jnp.stack([bias_one, gain_one, gain_two, bias_two], axis=1)
     own = features[0].transpose(0, 2, 1, 3)
     prev = later(own)
-    record = call(record_kernel, shape(REC, C, W), "sssv")(ids, tile_list, neighbours.T, own)
-    held = spread(record)
+    record, packed = call(record_kernel, [shape(REC, C, W), shape(4 * F + 1, C // 2, W)], "sssv")(ids, tile_list, neighbours.T, own)
+    held = spread(packed)
     weights = call(weights_kernel, shape(2, 2 * C, 4 * KF), "vv-", mib=16)(
         weight_one.reshape(3, 9 * C, C), weight_two.reshape(3, 9 * C, C), held[0]
     )

time: 63.4 us -> 63.3 us (level)
    ppermute x8, waiting for transfers between devices: 5.88 us -> 5.15 us  [send(): return lax.ppermute(array, 'tile', pairs(move))]
where the time goes in v4:
time: 63.3 us; the launch traced here: 63.1 us
  starting transfers between devices  24 us (38%)
  Pallas kernels  22.4 us (35%)
  waiting for transfers between devices  11.6 us (18%)
  local copies, waits for them, and re-layouts  4.57 us (7%)
    ppermute x8, starting transfers between devices, send(): return lax.ppermute(array, 'tile', pairs(move))  17.8 us
    ppermute x4, waiting for transfers between devices, later(): return lax.ppermute(array, 'group', [(i, (i + by) % NX) for i in range(NX)])  6.5 us
    ppermute x4, starting transfers between devices, later(): return lax.ppermute(array, 'group', [(i, (i + by) % NX) for i in range(NX)])  6.25 us
    pallas_call x1, Pallas kernels, per_device(): call(outer_kernel, shape(F, H, C, W), 's' + 'v' * 9, [pltpu.VMEM((3 * F,...  5.25 us
    ppermute x8, waiting for transfers between devices, send(): return lax.ppermute(array, 'tile', pairs(move))  5.15 us
    pallas_call x1, Pallas kernels, per_device(): call(inner_first_kernel, shape(F * H + REC, C, W), 'svvvv-s', scratch, 16...  4.26 us
    unnamed x28, local copies, waits for them, and re-layouts  2.51 us
    pallas_call x1, Pallas kernels, per_device(): pl.pallas_call(plan_kernel, out_shape=jax.ShapeDtypeStruct((12 * NY,), jn...  2.44 us
  transfers between devices with their start and end apart: 12, of which 8 were waited for; matrix products, arithmetic and copies ran while one was open for 2% of the time, Pallas kernels for 27%

profile of v4, /device:TPU:1, one launch (start us, length us, event | category | flops | bytes accessed | tf_op | source)
XLA Modules:
  0.0 63.1 jit_solution(12750547522321412194)
XLA Ops:
  0.1 1.4 %copy.32 = bf16[1,2,96,16,128]{4,2,3,1,0:T(8,128)(2,1)S(1)} copy(bf16[1,2,96,16,128]{4,3,2,1,0:T(8,128)(2,1)} %param.10) | data formatting | bytes 1572864 | tf_op args[0]
  1.5 2.1 %collective-permute-start = (bf16[2,16,96,128]{3,2,1,0:T(8,128)(2,1)S(1)}, bf16[2,16,96,128]{3,2,1,0:T(8,128)(2,1)}, u32[]{:S(2)}, u32[]{:S(2)}) collective-permute-start(bf16[2,16,96,128]{3,2,1,0:T(8,128)(2,1)S(1)} %bitcast.19), channel_id=1, source_target_pairs={{0,1},{1,2},{2,3},{3,0},{4,5},{5,6},{6,7},{7,4},{8,9},{9,10},{10,1... | collective-permute-start | bytes 2359304 | tf_op jit(solution)/shard_map/ppermute | solution.py:435
  3.7 1.0 %shard_map.100 = (bf16[5,96,128]{2,1,0:T(8,128)(2,1)S(1)}, bf16[9,48,128]{2,1,0:T(8,128)(2,1)S(1)}) custom-call(s32[2]{0:T(128)S(1)} %pad_add_fusion.ids, s32[64]{0:T(128)S(1)} %copy-done.7, s32[8,64]{1,0:T(8,128)S(1)} %bitcast.27, bf16[2,16,96,128]{3,2,1,0:T(8,128)(2,1)S(1)} %bitcast.20), custom_call_target="tpu_custom_call" | custom-call | bytes 1048576 | tf_op jit(solution)/shard_map/pallas_call | solution.py:476
  4.7 1.3 %collective-permute-start.1 = (bf16[9,48,128]{2,1,0:T(8,128)(2,1)S(1)}, bf16[9,48,128]{2,1,0:T(8,128)(2,1)S(1)}, u32[]{:S(2)}, u32[]{:S(2)}) collective-permute-start(bf16[9,48,128]{2,1,0:T(8,128)(2,1)S(1)} %get-tuple-element.13), channel_id=1, source_target_pairs={{0,4},{4,0},{8,12},{12,8},{16,20},{20,16},{24,28},{28,24},{32,36},... | collective-permute-start | bytes 331784 | tf_op jit(solution)/shard_map/ppermute | solution.py:431
  6.3 0.7 %concatenate.7.table = s32[594]{0:T(1024)} concatenate(s32[1]{0:T(128)} %bitcast, s32[1]{0:T(128)} %bitcast.1, s32[64]{0:T(128)S(1)} %copy-done.7, s32[512]{0:T(512)S(1)} %reshape.9, s32[16]{0:T(128)S(1)} %copy-done.8), dimensions={0} | concatenate | bytes 4752 | tf_op jit(solution)/shard_map/concatenate | solution.py:465
  7.0 5.4 %collective-permute-start.2 = (bf16[2,9,48,128]{3,2,1,0:T(8,128)(2,1)S(1)}, bf16[2,9,48,128]{3,2,1,0:T(8,128)(2,1)S(1)}, u32[]{:S(2)}, u32[]{:S(2)}) collective-permute-start(bf16[2,9,48,128]{3,2,1,0:T(8,128)(2,1)S(1)} %pad_maximum_fusion.1._.t0), channel_id=1, source_target_pairs={{0,32},{4,228},{8,40},{12,236},{16,48},{20,244},{24,56},{28,252},{... | collective-permute-start | bytes 663560 | tf_op jit(solution)/shard_map/ppermute | solution.py:431
  12.4 1.2 %collective-permute-start.4 = (bf16[2,9,48,128]{3,2,1,0:T(8,128)(2,1)S(1)}, bf16[2,9,48,128]{3,2,1,0:T(8,128)(2,1)S(1)}, u32[]{:S(2)}, u32[]{:S(2)}) collective-permute-start(bf16[2,9,48,128]{3,2,1,0:T(8,128)(2,1)S(1)} %pad_maximum_fusion.1._.t0), channel_id=1, source_target_pairs={{0,64},{4,196},{8,72},{12,204},{16,80},{20,212},{24,88},{28,220},{... | collective-permute-start | bytes 663560 | tf_op jit(solution)/shard_map/ppermute | solution.py:431
  13.6 2.4 %shard_map.103._plan.plan = s32[48]{0:T(128)} custom-call(s32[594]{0:T(1024)} %concatenate.7.table, bf16[2,9,48,128]{3,2,1,0:T(8,128)(2,1)} %copy-done), custom_call_target="tpu_custom_call" | custom-call | tf_op jit(solution)/shard_map/pallas_call | solution.py:481
  16.1 0.9 %copy-done.1 = bf16[2,9,48,128]{3,2,1,0:T(8,128)(2,1)S(1)} copy-done((bf16[2,9,48,128]{3,2,1,0:T(8,128)(2,1)S(1)}, bf16[2,9,48,128]{3,2,1,0:T(8,128)(2,1)}, u32[]{:S(2)}) %copy-start.1) | copy-done | bytes 221208
  17.0 0.6 shard_map.101.weights
  17.6 2.4 %shard_map.102.partial = f32[8,192,256]{2,1,0:T(8,128)S(1)} custom-call(bf16[2,16,96,128]{3,2,1,0:T(8,128)(2,1)S(1)} %bitcast.21, bf16[2,192,3584]{2,1,0:T(8,128)(2,1)S(1)} %shard_map.101.weights, f32[96,4]{1,0:T(8,128)S(1)} %copy.26.vectors), custom_call_target="tpu_custom_call" | custom-call | flops 3000000000 | bytes 1048576 | tf_op jit(solution)/shard_map/pallas_call | solution.py:489
  20.1 4.1 %collective-permute-start.5 = (bf16[3,9,48,128]{3,2,1,0:T(8,128)(2,1)S(1)}, bf16[3,9,48,128]{3,2,1,0:T(8,128)(2,1)S(1)}, u32[]{:S(2)}, u32[]{:S(2)}) collective-permute-start(bf16[3,9,48,128]{3,2,1,0:T(8,128)(2,1)S(1)} %pad_maximum_fusion), channel_id=1, source_target_pairs={{0,64},{4,196},{8,72},{12,204},{16,80},{20,212},{24,88},{28,220},{... | collective-permute-start | bytes 995336 | tf_op jit(solution)/shard_map/ppermute | solution.py:431
  24.2 4.3 %shard_map.104.second._.second_own = bf16[37,96,128]{2,1,0:T(8,128)(2,1)S(1)} custom-call(s32[594]{0:T(1024)S(1)} %copy-done.4, bf16[2,16,96,128]{3,2,1,0:T(8,128)(2,1)} %collective-permute-done.prev, f32[8,192,256]{2,1,0:T(8,128)S(1)} %shard_map.102.partial, bf16[2,192,3584]{2,1,0:T(8,128)(2,1)S(1)} %shard_map.101.weights, f32[96,4]{1,0:T(8,128)S(1)} %copy.26.vectors, ...), custom_call_target="tpu_custom_call" | custom-call | flops 8000000000 | bytes 1048576 | tf_op jit(solution)/shard_map/pallas_call | solution.py:492
  28.5 1.3 %collective-permute-start.3 = (bf16[37,96,128]{2,1,0:T(8,128)(2,1)S(1)}, bf16[37,96,128]{2,1,0:T(8,128)(2,1)S(1)}, u32[]{:S(2)}, u32[]{:S(2)}) collective-permute-start(bf16[37,96,128]{2,1,0:T(8,128)(2,1)S(1)} %shard_map.104.second._.second_own), channel_id=1, source_target_pairs={{0,1},{1,2},{2,3},{3,0},{4,5},{5,6},{6,7},{7,4},{8,9},{9,10},{10,1... | collective-permute-start | bytes 2727944 | tf_op jit(solution)/shard_map/ppermute | solution.py:435
  29.8 1.4 %collective-permute-done.5.t3 = bf16[3,9,48,128]{3,2,1,0:T(8,128)(2,1)S(1)} collective-permute-done((bf16[3,9,48,128]{3,2,1,0:T(8,128)(2,1)S(1)}, bf16[3,9,48,128]{3,2,1,0:T(8,128)(2,1)S(1)}, u32[]{:S(2)}, u32[]{:S(2)}) %collective-permute-start.5) | collective-permute-done | bytes 331808 | tf_op jit(solution)/shard_map/ppermute | solution.py:431
  31.2 1.7 %shard_map.106 = (bf16[4,5,96,128]{3,2,1,0:T(8,128)(2,1)S(1)}, bf16[4,5,96,128]{3,2,1,0:T(8,128)(2,1)S(1)}) custom-call(s32[48]{0:T(128)S(1)} %copy-done.6, bf16[2,9,48,128]{3,2,1,0:T(8,128)(2,1)S(1)} %copy-done.1, bf16[2,9,48,128]{3,2,1,0:T(8,128)(2,1)S(1)} %collective-permute-done.2._.t1, bf16[2,9,48,128]{3,2,1,0:T(8,128)(2,1)S(1)} %collective-permute-done.4.t2, ...), custom_call_target="tpu_custom_call" | custom-call | bytes 1048576 | tf_op jit(solution)/shard_map/pallas_call | solution.py:452
  33.0 1.9 %collective-permute-done.6.arrived = bf16[4,5,96,128]{3,2,1,0:T(8,128)(2,1)S(1)} collective-permute-done((bf16[4,5,96,128]{3,2,1,0:T(8,128)(2,1)S(1)}, bf16[4,5,96,128]{3,2,1,0:T(8,128)(2,1)S(1)}, u32[]{:S(2)}, u32[]{:S(2)}) %collective-permute-start.6) | collective-permute-done | bytes 491552 | tf_op jit(solution)/shard_map/ppermute | solution.py:431
  34.8 0.7 %shard_map.107 = (bf16[5,96,128]{2,1,0:T(8,128)(2,1)S(1)}, bf16[5,96,128]{2,1,0:T(8,128)(2,1)S(1)}, bf16[5,96,128]{2,1,0:T(8,128)(2,1)S(1)}, bf16[5,96,128]{2,1,0:T(8,128)(2,1)S(1)}) custom-call(s32[594]{0:T(1024)S(1)} %copy-done.4, bf16[4,5,96,128]{3,2,1,0:T(8,128)(2,1)S(1)} %get-tuple-element.14.mine, ...), custom_call_target="tpu_custom_call" | custom-call | bytes 1048576 | tf_op jit(solution)/shard_map/pallas_call | solution.py:454
  35.5 3.1 %collective-permute-start.7 = (bf16[5,96,128]{2,1,0:T(8,128)(2,1)S(1)}, bf16[5,96,128]{2,1,0:T(8,128)(2,1)S(1)}, u32[]{:S(2)}, u32[]{:S(2)}) collective-permute-start(bf16[5,96,128]{2,1,0:T(8,128)(2,1)S(1)} %get-tuple-element.17), channel_id=1, source_target_pairs={{0,16},{4,20},{8,24},{12,28},{16,0},{20,4},{24,8},{28,12},{32,48},... | collective-permute-start | bytes 368648 | tf_op jit(solution)/shard_map/ppermute | solution.py:431
  38.6 0.3 collective-permute-start.8
  38.9 2.3 %collective-permute-start.9 = (bf16[5,96,128]{2,1,0:T(8,128)(2,1)S(1)}, bf16[5,96,128]{2,1,0:T(8,128)(2,1)S(1)}, u32[]{:S(2)}, u32[]{:S(2)}) collective-permute-start(bf16[5,96,128]{2,1,0:T(8,128)(2,1)S(1)} %get-tuple-element.19), channel_id=1, source_target_pairs={{0,24},{4,28},{8,0},{12,4},{16,8},{20,12},{24,16},{28,20},{32,56},... | collective-permute-start | bytes 368648 | tf_op jit(solution)/shard_map/ppermute | solution.py:431
  41.3 1.8 %shard_map.105.partial = f32[2,16,96,128]{3,2,1,0:T(8,128)S(1)} custom-call(bf16[2,16,96,128]{3,2,1,0:T(8,128)(2,1)S(1)} %bitcast.22, bf16[37,96,128]{2,1,0:T(8,128)(2,1)S(1)} %shard_map.104.second._.second_own, bf16[2,192,3584]{2,1,0:T(8,128)(2,1)S(1)} %shard_map.101.weights, f32[96,4]{1,0:T(8,128)S(1)} %copy.26.vectors), custom_call_target="tpu_custom_call" | custom-call | flops 1000000000 | bytes 1048576 | tf_op jit(solution)/shard_map/pallas_call | solution.py:496
  43.1 1.7 %collective-permute-done.8 = bf16[5,96,128]{2,1,0:T(8,128)(2,1)S(1)} collective-permute-done((bf16[5,96,128]{2,1,0:T(8,128)(2,1)S(1)}, bf16[5,96,128]{2,1,0:T(8,128)(2,1)S(1)}, u32[]{:S(2)}, u32[]{:S(2)}) %collective-permute-start.8) | collective-permute-done | bytes 122912 | tf_op jit(solution)/shard_map/ppermute | solution.py:431
  44.8 0.1 collective-permute-done.9
  45.0 1.3 %collective-permute-start.10 = (bf16[5,96,128]{2,1,0:T(8,128)(2,1)S(1)}, bf16[5,96,128]{2,1,0:T(8,128)(2,1)S(1)}, u32[]{:S(2)}, u32[]{:S(2)}) collective-permute-start(bf16[5,96,128]{2,1,0:T(8,128)(2,1)S(1)} %add_convert_fusion._.halo0), channel_id=1, source_target_pairs={{0,1},{1,2},{2,3},{3,0},{4,5},{5,6},{6,7},{7,4},{8,9},{9,10},{10,1... | collective-permute-start | bytes 368648 | tf_op jit(solution)/shard_map/ppermute | solution.py:435
  46.2 1.6 %collective-permute-start.11 = (bf16[5,96,128]{2,1,0:T(8,128)(2,1)S(1)}, bf16[5,96,128]{2,1,0:T(8,128)(2,1)S(1)}, u32[]{:S(2)}, u32[]{:S(2)}) collective-permute-start(bf16[5,96,128]{2,1,0:T(8,128)(2,1)S(1)} %add_convert_fusion._.halo0), channel_id=1, source_target_pairs={{0,2},{1,3},{2,0},{3,1},{4,6},{5,7},{6,4},{7,5},{8,10},{9,11},{10,... | collective-permute-start | bytes 368648 | tf_op jit(solution)/shard_map/ppermute | solution.py:435
  47.8 4.2 %collective-permute-done.3.second_prev = bf16[37,96,128]{2,1,0:T(8,128)(2,1)S(1)} collective-permute-done((bf16[37,96,128]{2,1,0:T(8,128)(2,1)S(1)}, bf16[37,96,128]{2,1,0:T(8,128)(2,1)S(1)}, u32[]{:S(2)}, u32[]{:S(2)}) %collective-permute-start.3) | collective-permute-done | bytes 909344 | tf_op jit(solution)/shard_map/ppermute | solution.py:435
  52.0 2.4 %shard_map.108.inner = f32[2,16,96,128]{3,2,1,0:T(8,128)S(1)} custom-call(s32[594]{0:T(1024)S(1)} %copy-done.4, f32[2,16,96,128]{3,2,1,0:T(8,128)S(1)} %shard_map.105.partial, bf16[37,96,128]{2,1,0:T(8,128)(2,1)S(1)} %collective-permute-done.3.second_prev, bf16[2,192,3584]{2,1,0:T(8,128)(2,1)S(1)} %shard_map.101.weights, ...), custom_call_target="tpu_custom_call" | custom-call | flops 12000000000 | bytes 1048576 | tf_op jit(solution)/shard_map/pallas_call | solution.py:500
  54.3 0.3 collective-permute-done.10.halo1
  54.6 2.1 %collective-permute-done.11.halo2 = bf16[5,96,128]{2,1,0:T(8,128)(2,1)S(1)} collective-permute-done((bf16[5,96,128]{2,1,0:T(8,128)(2,1)S(1)}, bf16[5,96,128]{2,1,0:T(8,128)(2,1)S(1)}, u32[]{:S(2)}, u32[]{:S(2)}) %collective-permute-start.11) | collective-permute-done | bytes 122912 | tf_op jit(solution)/shard_map/ppermute | solution.py:435
  56.7 5.3 %shard_map.109 = bf16[2,16,96,128]{3,2,1,0:T(8,128)(2,1)S(1)} custom-call(s32[594]{0:T(1024)S(1)} %copy-done.4, f32[2,16,96,128]{3,2,1,0:T(8,128)S(1)} %shard_map.108.inner, bf16[5,96,128]{2,1,0:T(8,128)(2,1)S(1)} %get-tuple-element.20.record0, bf16[37,96,128]{2,1,0:T(8,128)(2,1)S(1)} %shard_map.104.second._.second_own, ...), custom_call_target="tpu_custom_call" | custom-call | flops 4000000000 | bytes 1048576 | tf_op jit(solution)/shard_map/pallas_call | solution.py:503
  62.0 1.2 %copy.30 = bf16[1,2,96,16,128]{4,3,2,1,0:T(8,128)(2,1)} copy(bf16[1,2,96,16,128]{4,2,3,1,0:T(8,128)(2,1)S(1)} %bitcast.23) | data formatting | bytes 1572864 | tf_op jit(solution)/shard_map/broadcast_in_dim | solution.py:516
  (40 shorter events, 0.7 us)
Async XLA Ops:
  0.0 3.7 %copy-start.5 = (s32[64,8]{0,1:T(8,128)S(1)}, s32[64,8]{0,1:T(8,128)}, u32[]{:S(2)}) copy-start(s32[64,8]{0,1:T(8,128)} %param.12) | copy-start | bytes 6148
  0.0 3.7 %copy-start.7 = (s32[64]{0:T(128)S(1)}, s32[64]{0:T(128)}, u32[]{:S(2)}) copy-start(s32[64]{0:T(128)} %tiles.1) | copy-start | bytes 772
  0.0 6.1 %copy-start.12 = (f32[96]{0:T(128)S(1)}, f32[96]{0:T(128)}, u32[]{:S(2)}) copy-start(f32[96]{0:T(128)} %param.16) | copy-start | bytes 1156
  0.0 6.1 %copy-start.11 = (f32[96]{0:T(128)S(1)}, f32[96]{0:T(128)}, u32[]{:S(2)}) copy-start(f32[96]{0:T(128)} %param.14) | copy-start | bytes 1156
  0.0 6.1 %copy-start.10 = (f32[96]{0:T(128)S(1)}, f32[96]{0:T(128)}, u32[]{:S(2)}) copy-start(f32[96]{0:T(128)} %param.17) | copy-start | bytes 1156
  0.0 6.1 %copy-start.9 = (f32[96]{0:T(128)S(1)}, f32[96]{0:T(128)}, u32[]{:S(2)}) copy-start(f32[96]{0:T(128)} %param.19) | copy-start | bytes 1156
  0.0 6.3 %copy-start.8 = (s32[16]{0:T(128)S(1)}, s32[16]{0:T(128)}, u32[]{:S(2)}) copy-start(s32[16]{0:T(128)} %param.13) | copy-start | bytes 196
  0.0 16.0 %copy-start.2 = (bf16[3,3,3,96,96]{4,3,2,1,0:T(8,128)(2,1)S(1)}, bf16[3,3,3,96,96]{4,3,2,1,0:T(8,128)(2,1)}, u32[]{:S(2)}) copy-start(bf16[3,3,3,96,96]{4,3,2,1,0:T(8,128)(2,1)} %param.15) | copy-start | bytes 1492996
  0.1 16.0 %copy-start.3 = (bf16[3,3,3,96,96]{4,3,2,1,0:T(8,128)(2,1)S(1)}, bf16[3,3,3,96,96]{4,3,2,1,0:T(8,128)(2,1)}, u32[]{:S(2)}) copy-start(bf16[3,3,3,96,96]{4,3,2,1,0:T(8,128)(2,1)} %param.18) | copy-start | bytes 1492996
  1.5 22.7 %collective-permute-start = (bf16[2,16,96,128]{3,2,1,0:T(8,128)(2,1)S(1)}, bf16[2,16,96,128]{3,2,1,0:T(8,128)(2,1)}, u32[]{:S(2)}, u32[]{:S(2)}) collective-permute-start(bf16[2,16,96,128]{3,2,1,0:T(8,128)(2,1)S(1)} %bitcast.19), channel_id=1, source_target_pairs={{0,1},{1,2},{2,3},{3,0},{4,5},{5,6},{6,7},{7,4},{8,9},{9,10},{10,1... | collective-permute-start | bytes 2359304 | tf_op jit(solution)/shard_map/ppermute | solution.py:435
  4.7 2.3 %collective-permute-start.1 = (bf16[9,48,128]{2,1,0:T(8,128)(2,1)S(1)}, bf16[9,48,128]{2,1,0:T(8,128)(2,1)S(1)}, u32[]{:S(2)}, u32[]{:S(2)}) collective-permute-start(bf16[9,48,128]{2,1,0:T(8,128)(2,1)S(1)} %get-tuple-element.13), channel_id=1, source_target_pairs={{0,4},{4,0},{8,12},{12,8},{16,20},{20,16},{24,28},{28,24},{32,36},... | collective-permute-start | bytes 331784 | tf_op jit(solution)/shard_map/ppermute | solution.py:431
  7.0 6.6 %copy-start = (bf16[2,9,48,128]{3,2,1,0:T(8,128)(2,1)}, bf16[2,9,48,128]{3,2,1,0:T(8,128)(2,1)S(1)}, u32[]{:S(2)}) copy-start(bf16[2,9,48,128]{3,2,1,0:T(8,128)(2,1)S(1)} %pad_maximum_fusion.1._.t0) | copy-start | bytes 663556
  7.0 13.0 %collective-permute-start.2 = (bf16[2,9,48,128]{3,2,1,0:T(8,128)(2,1)S(1)}, bf16[2,9,48,128]{3,2,1,0:T(8,128)(2,1)S(1)}, u32[]{:S(2)}, u32[]{:S(2)}) collective-permute-start(bf16[2,9,48,128]{3,2,1,0:T(8,128)(2,1)S(1)} %pad_maximum_fusion.1._.t0), channel_id=1, source_target_pairs={{0,32},{4,228},{8,40},{12,236},{16,48},{20,244},{24,56},{28,252},{... | collective-permute-start | bytes 663560 | tf_op jit(solution)/shard_map/ppermute | solution.py:431
  12.4 7.6 %collective-permute-start.4 = (bf16[2,9,48,128]{3,2,1,0:T(8,128)(2,1)S(1)}, bf16[2,9,48,128]{3,2,1,0:T(8,128)(2,1)S(1)}, u32[]{:S(2)}, u32[]{:S(2)}) collective-permute-start(bf16[2,9,48,128]{3,2,1,0:T(8,128)(2,1)S(1)} %pad_maximum_fusion.1._.t0), channel_id=1, source_target_pairs={{0,64},{4,196},{8,72},{12,204},{16,80},{20,212},{24,88},{28,220},{... | collective-permute-start | bytes 663560 | tf_op jit(solution)/shard_map/ppermute | solution.py:431
  16.1 0.9 %copy-start.1 = (bf16[2,9,48,128]{3,2,1,0:T(8,128)(2,1)S(1)}, bf16[2,9,48,128]{3,2,1,0:T(8,128)(2,1)}, u32[]{:S(2)}) copy-start(bf16[2,9,48,128]{3,2,1,0:T(8,128)(2,1)} %copy-done) | copy-start | bytes 663556
  17.6 6.6 %copy-start.4 = (s32[594]{0:T(1024)S(1)}, s32[594]{0:T(1024)}, u32[]{:S(2)}) copy-start(s32[594]{0:T(1024)} %concatenate.7.table) | copy-start | bytes 7132
  17.6 6.6 %copy-start.6 = (s32[48]{0:T(128)S(1)}, s32[48]{0:T(128)}, u32[]{:S(2)}) copy-start(s32[48]{0:T(128)} %shard_map.103._plan.plan) | copy-start | bytes 580
  20.1 11.1 %collective-permute-start.5 = (bf16[3,9,48,128]{3,2,1,0:T(8,128)(2,1)S(1)}, bf16[3,9,48,128]{3,2,1,0:T(8,128)(2,1)S(1)}, u32[]{:S(2)}, u32[]{:S(2)}) collective-permute-start(bf16[3,9,48,128]{3,2,1,0:T(8,128)(2,1)S(1)} %pad_maximum_fusion), channel_id=1, source_target_pairs={{0,64},{4,196},{8,72},{12,204},{16,80},{20,212},{24,88},{28,220},{... | collective-permute-start | bytes 995336 | tf_op jit(solution)/shard_map/ppermute | solution.py:431
  28.5 23.5 %collective-permute-start.3 = (bf16[37,96,128]{2,1,0:T(8,128)(2,1)S(1)}, bf16[37,96,128]{2,1,0:T(8,128)(2,1)S(1)}, u32[]{:S(2)}, u32[]{:S(2)}) collective-permute-start(bf16[37,96,128]{2,1,0:T(8,128)(2,1)S(1)} %shard_map.104.second._.second_own), channel_id=1, source_target_pairs={{0,1},{1,2},{2,3},{3,0},{4,5},{5,6},{6,7},{7,4},{8,9},{9,10},{10,1... | collective-permute-start | bytes 2727944 | tf_op jit(solution)/shard_map/ppermute | solution.py:435
  32.9 2.0 %collective-permute-start.6 = (bf16[4,5,96,128]{3,2,1,0:T(8,128)(2,1)S(1)}, bf16[4,5,96,128]{3,2,1,0:T(8,128)(2,1)S(1)}, u32[]{:S(2)}, u32[]{:S(2)}) collective-permute-start(bf16[4,5,96,128]{3,2,1,0:T(8,128)(2,1)S(1)} %get-tuple-element.15), channel_id=1, source_target_pairs={{0,4},{4,0},{8,12},{12,8},{16,20},{20,16},{24,28},{28,24},{32,36},... | collective-permute-start | bytes 1474568 | tf_op jit(solution)/shard_map/ppermute | solution.py:431
  35.5 7.5 %collective-permute-start.7 = (bf16[5,96,128]{2,1,0:T(8,128)(2,1)S(1)}, bf16[5,96,128]{2,1,0:T(8,128)(2,1)S(1)}, u32[]{:S(2)}, u32[]{:S(2)}) collective-permute-start(bf16[5,96,128]{2,1,0:T(8,128)(2,1)S(1)} %get-tuple-element.17), channel_id=1, source_target_pairs={{0,16},{4,20},{8,24},{12,28},{16,0},{20,4},{24,8},{28,12},{32,48},... | collective-permute-start | bytes 368648 | tf_op jit(solution)/shard_map/ppermute | solution.py:431
  38.6 6.2 %collective-permute-start.8 = (bf16[5,96,128]{2,1,0:T(8,128)(2,1)S(1)}, bf16[5,96,128]{2,1,0:T(8,128)(2,1)S(1)}, u32[]{:S(2)}, u32[]{:S(2)}) collective-permute-start(bf16[5,96,128]{2,1,0:T(8,128)(2,1)S(1)} %get-tuple-element.18), channel_id=1, source_target_pairs={{0,8},{4,12},{8,16},{12,20},{16,24},{20,28},{24,0},{28,4},{32,40},... | collective-permute-start | bytes 368648 | tf_op jit(solution)/shard_map/ppermute | solution.py:431
  38.9 5.9 %collective-permute-start.9 = (bf16[5,96,128]{2,1,0:T(8,128)(2,1)S(1)}, bf16[5,96,128]{2,1,0:T(8,128)(2,1)S(1)}, u32[]{:S(2)}, u32[]{:S(2)}) collective-permute-start(bf16[5,96,128]{2,1,0:T(8,128)(2,1)S(1)} %get-tuple-element.19), channel_id=1, source_target_pairs={{0,24},{4,28},{8,0},{12,4},{16,8},{20,12},{24,16},{28,20},{32,56},... | collective-permute-start | bytes 368648 | tf_op jit(solution)/shard_map/ppermute | solution.py:431
  45.0 9.7 %collective-permute-start.10 = (bf16[5,96,128]{2,1,0:T(8,128)(2,1)S(1)}, bf16[5,96,128]{2,1,0:T(8,128)(2,1)S(1)}, u32[]{:S(2)}, u32[]{:S(2)}) collective-permute-start(bf16[5,96,128]{2,1,0:T(8,128)(2,1)S(1)} %add_convert_fusion._.halo0), channel_id=1, source_target_pairs={{0,1},{1,2},{2,3},{3,0},{4,5},{5,6},{6,7},{7,4},{8,9},{9,10},{10,1... | collective-permute-start | bytes 368648 | tf_op jit(solution)/shard_map/ppermute | solution.py:435
  46.2 10.4 %collective-permute-start.11 = (bf16[5,96,128]{2,1,0:T(8,128)(2,1)S(1)}, bf16[5,96,128]{2,1,0:T(8,128)(2,1)S(1)}, u32[]{:S(2)}, u32[]{:S(2)}) collective-permute-start(bf16[5,96,128]{2,1,0:T(8,128)(2,1)S(1)} %add_convert_fusion._.halo0), channel_id=1, source_target_pairs={{0,2},{1,3},{2,0},{3,1},{4,6},{5,7},{6,4},{7,5},{8,10},{9,11},{10,... | collective-permute-start | bytes 368648 | tf_op jit(solution)/shard_map/ppermute | solution.py:435

commit v5 on v4

--- a/solution.py
+++ b/solution.py
@@ -128,13 +128,12 @@
     return jnp.concatenate(both, axis=0).astype(BF)
 
 
-def select_kernel(plan, t0, t1, t2, t3, _, mine, other):
+def select_kernel(first, plan, t0, t1, t2, t3, _, out):
     held = (t0, t1, t2, t3)
-    mine[...] = jnp.zeros_like(mine)
-    other[...] = jnp.zeros_like(other)
+    out[...] = jnp.zeros_like(out)
     low = lanes(C) < 64
-    for n in range(2 * NY):
-        out, yd = (mine, other)[n // NY], n % NY
+    for yd in range(NY):
+        n = first + yd
         for k, ref in enumerate(held):
 
             @pl.when(plan[6 * n] == k)
@@ -449,8 +448,9 @@
 
 
 def deliver(table, plan, held, after):
-    mine, other = call(select_kernel, [shape(NY, REC, C, W)] * 2, "svvvv-")(plan, *held, after)
+    other = call(functools.partial(select_kernel, NY), shape(NY, REC, C, W), "svvvv-")(plan, *held, after)
     arrived = send(other, swap)
+    mine = call(functools.partial(select_kernel, 0), shape(NY, REC, C, W), "svvvv-")(plan, *held, other)
     own, one, two, three = call(combine_kernel, [shape(REC, C, W)] * 4, "svv")(table, mine, arrived)
     total = own.astype(F32)
     for by, part in ((2, two), (1, one), (3, three)):

time: 63.3 us -> 63.3 us (level)
    ppermute x8, waiting for transfers between devices: 5.15 us -> 4.17 us  [send(): return lax.ppermute(array, 'tile', pairs(move))]
    pallas_call x1 -> x2, Pallas kernels: 1.66 us -> 2.02 us  [the longest x1 1.01 us: deliver(): call(functools.partial(select_kernel, NY), shape(NY, REC, C, W), 'svvvv-')]
  transfers between devices with their start and end apart: 12 -> 12, of which waited for: 8 -> 8; matrix products, arithmetic and copies ran while one was open for 2% -> 2% of each run, Pallas kernels for 27% -> 28%
where the time goes in v5:
time: 63.3 us; the launch traced here: 63.1 us
  starting transfers between devices  24.2 us (38%)
  Pallas kernels  22.8 us (36%)
  waiting for transfers between devices  11.2 us (18%)
  local copies, waits for them, and re-layouts  4.57 us (7%)
    ppermute x8, starting transfers between devices, send(): return lax.ppermute(array, 'tile', pairs(move))  17.9 us
    ppermute x4, waiting for transfers between devices, later(): return lax.ppermute(array, 'group', [(i, (i + by) % NX) for i in range(NX)])  6.98 us
    ppermute x4, starting transfers between devices, later(): return lax.ppermute(array, 'group', [(i, (i + by) % NX) for i in range(NX)])  6.26 us
    pallas_call x1, Pallas kernels, per_device(): call(outer_kernel, shape(F, H, C, W), 's' + 'v' * 9, [pltpu.VMEM((3 * F,...  5.26 us
    pallas_call x1, Pallas kernels, per_device(): call(inner_first_kernel, shape(F * H + REC, C, W), 'svvvv-s', scratch, 16...  4.26 us
    ppermute x8, waiting for transfers between devices, send(): return lax.ppermute(array, 'tile', pairs(move))  4.17 us
    unnamed x28, local copies, waits for them, and re-layouts  2.51 us
    pallas_call x1, Pallas kernels, per_device(): pl.pallas_call(plan_kernel, out_shape=jax.ShapeDtypeStruct((12 * NY,), jn...  2.44 us
  transfers between devices with their start and end apart: 12, of which 8 were waited for; matrix products, arithmetic and copies ran while one was open for 2% of the time, Pallas kernels for 28%

profile of v5, /device:TPU:1, one launch (start us, length us, event | category | flops | bytes accessed | tf_op | source)
XLA Modules:
  0.0 63.1 jit_solution(9292589547757975991)
XLA Ops:
  0.1 1.4 %copy.32 = bf16[1,2,96,16,128]{4,2,3,1,0:T(8,128)(2,1)S(1)} copy(bf16[1,2,96,16,128]{4,3,2,1,0:T(8,128)(2,1)} %param.10) | data formatting | bytes 1572864 | tf_op args[0]
  1.5 2.1 %collective-permute-start = (bf16[2,16,96,128]{3,2,1,0:T(8,128)(2,1)S(1)}, bf16[2,16,96,128]{3,2,1,0:T(8,128)(2,1)}, u32[]{:S(2)}, u32[]{:S(2)}) collective-permute-start(bf16[2,16,96,128]{3,2,1,0:T(8,128)(2,1)S(1)} %bitcast.19), channel_id=1, source_target_pairs={{0,1},{1,2},{2,3},{3,0},{4,5},{5,6},{6,7},{7,4},{8,9},{9,10},{10,1... | collective-permute-start | bytes 2359304 | tf_op jit(solution)/shard_map/ppermute | solution.py:434
  3.7 1.0 %shard_map.100 = (bf16[5,96,128]{2,1,0:T(8,128)(2,1)S(1)}, bf16[9,48,128]{2,1,0:T(8,128)(2,1)S(1)}) custom-call(s32[2]{0:T(128)S(1)} %pad_add_fusion.ids, s32[64]{0:T(128)S(1)} %copy-done.7, s32[8,64]{1,0:T(8,128)S(1)} %bitcast.27, bf16[2,16,96,128]{3,2,1,0:T(8,128)(2,1)S(1)} %bitcast.20), custom_call_target="tpu_custom_call" | custom-call | bytes 1048576 | tf_op jit(solution)/shard_map/pallas_call | solution.py:476
  4.7 1.3 %collective-permute-start.1 = (bf16[9,48,128]{2,1,0:T(8,128)(2,1)S(1)}, bf16[9,48,128]{2,1,0:T(8,128)(2,1)S(1)}, u32[]{:S(2)}, u32[]{:S(2)}) collective-permute-start(bf16[9,48,128]{2,1,0:T(8,128)(2,1)S(1)} %get-tuple-element.11), channel_id=1, source_target_pairs={{0,4},{4,0},{8,12},{12,8},{16,20},{20,16},{24,28},{28,24},{32,36},... | collective-permute-start | bytes 331784 | tf_op jit(solution)/shard_map/ppermute | solution.py:430
  6.3 0.7 %concatenate.7.table = s32[594]{0:T(1024)} concatenate(s32[1]{0:T(128)} %bitcast, s32[1]{0:T(128)} %bitcast.1, s32[64]{0:T(128)S(1)} %copy-done.7, s32[512]{0:T(512)S(1)} %reshape.9, s32[16]{0:T(128)S(1)} %copy-done.8), dimensions={0} | concatenate | bytes 4752 | tf_op jit(solution)/shard_map/concatenate | solution.py:465
  7.0 5.4 %collective-permute-start.2 = (bf16[2,9,48,128]{3,2,1,0:T(8,128)(2,1)S(1)}, bf16[2,9,48,128]{3,2,1,0:T(8,128)(2,1)S(1)}, u32[]{:S(2)}, u32[]{:S(2)}) collective-permute-start(bf16[2,9,48,128]{3,2,1,0:T(8,128)(2,1)S(1)} %pad_maximum_fusion.1._.t0), channel_id=1, source_target_pairs={{0,32},{4,228},{8,40},{12,236},{16,48},{20,244},{24,56},{28,252},{... | collective-permute-start | bytes 663560 | tf_op jit(solution)/shard_map/ppermute | solution.py:430
  12.4 1.2 %collective-permute-start.4 = (bf16[2,9,48,128]{3,2,1,0:T(8,128)(2,1)S(1)}, bf16[2,9,48,128]{3,2,1,0:T(8,128)(2,1)S(1)}, u32[]{:S(2)}, u32[]{:S(2)}) collective-permute-start(bf16[2,9,48,128]{3,2,1,0:T(8,128)(2,1)S(1)} %pad_maximum_fusion.1._.t0), channel_id=1, source_target_pairs={{0,64},{4,196},{8,72},{12,204},{16,80},{20,212},{24,88},{28,220},{... | collective-permute-start | bytes 663560 | tf_op jit(solution)/shard_map/ppermute | solution.py:430
  13.6 2.4 %shard_map.103._plan.plan = s32[48]{0:T(128)} custom-call(s32[594]{0:T(1024)} %concatenate.7.table, bf16[2,9,48,128]{3,2,1,0:T(8,128)(2,1)} %copy-done), custom_call_target="tpu_custom_call" | custom-call | tf_op jit(solution)/shard_map/pallas_call | solution.py:481
  16.1 0.9 %copy-done.1 = bf16[2,9,48,128]{3,2,1,0:T(8,128)(2,1)S(1)} copy-done((bf16[2,9,48,128]{3,2,1,0:T(8,128)(2,1)S(1)}, bf16[2,9,48,128]{3,2,1,0:T(8,128)(2,1)}, u32[]{:S(2)}) %copy-start.1) | copy-done | bytes 221208
  17.0 0.6 shard_map.101.weights
  17.6 2.4 %shard_map.102.partial = f32[8,192,256]{2,1,0:T(8,128)S(1)} custom-call(bf16[2,16,96,128]{3,2,1,0:T(8,128)(2,1)S(1)} %bitcast.21, bf16[2,192,3584]{2,1,0:T(8,128)(2,1)S(1)} %shard_map.101.weights, f32[96,4]{1,0:T(8,128)S(1)} %copy.26.vectors), custom_call_target="tpu_custom_call" | custom-call | flops 3000000000 | bytes 1048576 | tf_op jit(solution)/shard_map/pallas_call | solution.py:489
  20.1 4.1 %collective-permute-start.5 = (bf16[3,9,48,128]{3,2,1,0:T(8,128)(2,1)S(1)}, bf16[3,9,48,128]{3,2,1,0:T(8,128)(2,1)S(1)}, u32[]{:S(2)}, u32[]{:S(2)}) collective-permute-start(bf16[3,9,48,128]{3,2,1,0:T(8,128)(2,1)S(1)} %pad_maximum_fusion), channel_id=1, source_target_pairs={{0,64},{4,196},{8,72},{12,204},{16,80},{20,212},{24,88},{28,220},{... | collective-permute-start | bytes 995336 | tf_op jit(solution)/shard_map/ppermute | solution.py:430
  24.2 4.3 %shard_map.104.second._.second_own = bf16[37,96,128]{2,1,0:T(8,128)(2,1)S(1)} custom-call(s32[594]{0:T(1024)S(1)} %copy-done.4, bf16[2,16,96,128]{3,2,1,0:T(8,128)(2,1)} %collective-permute-done.prev, f32[8,192,256]{2,1,0:T(8,128)S(1)} %shard_map.102.partial, bf16[2,192,3584]{2,1,0:T(8,128)(2,1)S(1)} %shard_map.101.weights, f32[96,4]{1,0:T(8,128)S(1)} %copy.26.vectors, ...), custom_call_target="tpu_custom_call" | custom-call | flops 8000000000 | bytes 1048576 | tf_op jit(solution)/shard_map/pallas_call | solution.py:492
  28.5 1.3 %collective-permute-start.3 = (bf16[37,96,128]{2,1,0:T(8,128)(2,1)S(1)}, bf16[37,96,128]{2,1,0:T(8,128)(2,1)S(1)}, u32[]{:S(2)}, u32[]{:S(2)}) collective-permute-start(bf16[37,96,128]{2,1,0:T(8,128)(2,1)S(1)} %shard_map.104.second._.second_own), channel_id=1, source_target_pairs={{0,1},{1,2},{2,3},{3,0},{4,5},{5,6},{6,7},{7,4},{8,9},{9,10},{10,1... | collective-permute-start | bytes 2727944 | tf_op jit(solution)/shard_map/ppermute | solution.py:434
  29.8 1.4 %collective-permute-done.5.t3 = bf16[3,9,48,128]{3,2,1,0:T(8,128)(2,1)S(1)} collective-permute-done((bf16[3,9,48,128]{3,2,1,0:T(8,128)(2,1)S(1)}, bf16[3,9,48,128]{3,2,1,0:T(8,128)(2,1)S(1)}, u32[]{:S(2)}, u32[]{:S(2)}) %collective-permute-start.5) | collective-permute-done | bytes 331808 | tf_op jit(solution)/shard_map/ppermute | solution.py:430
  31.2 1.0 %shard_map.106._ = bf16[4,5,96,128]{3,2,1,0:T(8,128)(2,1)S(1)} custom-call(s32[48]{0:T(128)S(1)} %copy-done.6, bf16[2,9,48,128]{3,2,1,0:T(8,128)(2,1)S(1)} %copy-done.1, bf16[2,9,48,128]{3,2,1,0:T(8,128)(2,1)S(1)} %collective-permute-done.2._.t1, bf16[2,9,48,128]{3,2,1,0:T(8,128)(2,1)S(1)} %collective-permute-done.4.t2, ...), custom_call_target="tpu_custom_call" | custom-call | bytes 1048576 | tf_op jit(solution)/shard_map/pallas_call | solution.py:451
  32.2 0.3 collective-permute-start.6
  32.5 1.0 %shard_map.107.mine = bf16[4,5,96,128]{3,2,1,0:T(8,128)(2,1)S(1)} custom-call(s32[48]{0:T(128)S(1)} %copy-done.6, bf16[2,9,48,128]{3,2,1,0:T(8,128)(2,1)S(1)} %copy-done.1, bf16[2,9,48,128]{3,2,1,0:T(8,128)(2,1)S(1)} %collective-permute-done.2._.t1, bf16[2,9,48,128]{3,2,1,0:T(8,128)(2,1)S(1)} %collective-permute-done.4.t2, ...), custom_call_target="tpu_custom_call" | custom-call | bytes 1048576 | tf_op jit(solution)/shard_map/pallas_call | solution.py:453
  33.5 0.8 %collective-permute-done.6.arrived = bf16[4,5,96,128]{3,2,1,0:T(8,128)(2,1)S(1)} collective-permute-done((bf16[4,5,96,128]{3,2,1,0:T(8,128)(2,1)S(1)}, bf16[4,5,96,128]{3,2,1,0:T(8,128)(2,1)S(1)}, u32[]{:S(2)}, u32[]{:S(2)}) %collective-permute-start.6) | collective-permute-done | bytes 491552 | tf_op jit(solution)/shard_map/ppermute | solution.py:430
  34.3 0.7 %shard_map.108 = (bf16[5,96,128]{2,1,0:T(8,128)(2,1)S(1)}, bf16[5,96,128]{2,1,0:T(8,128)(2,1)S(1)}, bf16[5,96,128]{2,1,0:T(8,128)(2,1)S(1)}, bf16[5,96,128]{2,1,0:T(8,128)(2,1)S(1)}) custom-call(s32[594]{0:T(1024)S(1)} %copy-done.4, bf16[4,5,96,128]{3,2,1,0:T(8,128)(2,1)S(1)} %shard_map.107.mine, bf16[4,5,96,128]{3,2,1,0:T(8,128)(2,1)S(1)} %collective-permute-done.6.arrived), custom_call_target="tpu_custom_call" | custom-call | bytes 1048576 | tf_op jit(solution)/shard_map/pallas_call | solution.py:454
  35.0 3.0 %collective-permute-start.7 = (bf16[5,96,128]{2,1,0:T(8,128)(2,1)S(1)}, bf16[5,96,128]{2,1,0:T(8,128)(2,1)S(1)}, u32[]{:S(2)}, u32[]{:S(2)}) collective-permute-start(bf16[5,96,128]{2,1,0:T(8,128)(2,1)S(1)} %get-tuple-element.13), channel_id=1, source_target_pairs={{0,16},{4,20},{8,24},{12,28},{16,0},{20,4},{24,8},{28,12},{32,48},... | collective-permute-start | bytes 368648 | tf_op jit(solution)/shard_map/ppermute | solution.py:430
  38.1 0.4 collective-permute-start.8
  38.5 2.3 %collective-permute-start.9 = (bf16[5,96,128]{2,1,0:T(8,128)(2,1)S(1)}, bf16[5,96,128]{2,1,0:T(8,128)(2,1)S(1)}, u32[]{:S(2)}, u32[]{:S(2)}) collective-permute-start(bf16[5,96,128]{2,1,0:T(8,128)(2,1)S(1)} %get-tuple-element.15), channel_id=1, source_target_pairs={{0,24},{4,28},{8,0},{12,4},{16,8},{20,12},{24,16},{28,20},{32,56},... | collective-permute-start | bytes 368648 | tf_op jit(solution)/shard_map/ppermute | solution.py:430
  40.7 1.8 %shard_map.105.partial = f32[2,16,96,128]{3,2,1,0:T(8,128)S(1)} custom-call(bf16[2,16,96,128]{3,2,1,0:T(8,128)(2,1)S(1)} %bitcast.22, bf16[37,96,128]{2,1,0:T(8,128)(2,1)S(1)} %shard_map.104.second._.second_own, bf16[2,192,3584]{2,1,0:T(8,128)(2,1)S(1)} %shard_map.101.weights, f32[96,4]{1,0:T(8,128)S(1)} %copy.26.vectors), custom_call_target="tpu_custom_call" | custom-call | flops 1000000000 | bytes 1048576 | tf_op jit(solution)/shard_map/pallas_call | solution.py:496
  42.5 1.7 %collective-permute-done.8 = bf16[5,96,128]{2,1,0:T(8,128)(2,1)S(1)} collective-permute-done((bf16[5,96,128]{2,1,0:T(8,128)(2,1)S(1)}, bf16[5,96,128]{2,1,0:T(8,128)(2,1)S(1)}, u32[]{:S(2)}, u32[]{:S(2)}) %collective-permute-start.8) | collective-permute-done | bytes 122912 | tf_op jit(solution)/shard_map/ppermute | solution.py:430
  44.5 1.3 %collective-permute-start.10 = (bf16[5,96,128]{2,1,0:T(8,128)(2,1)S(1)}, bf16[5,96,128]{2,1,0:T(8,128)(2,1)S(1)}, u32[]{:S(2)}, u32[]{:S(2)}) collective-permute-start(bf16[5,96,128]{2,1,0:T(8,128)(2,1)S(1)} %add_convert_fusion._.halo0), channel_id=1, source_target_pairs={{0,1},{1,2},{2,3},{3,0},{4,5},{5,6},{6,7},{7,4},{8,9},{9,10},{10,1... | collective-permute-start | bytes 368648 | tf_op jit(solution)/shard_map/ppermute | solution.py:434
  45.8 1.6 %collective-permute-start.11 = (bf16[5,96,128]{2,1,0:T(8,128)(2,1)S(1)}, bf16[5,96,128]{2,1,0:T(8,128)(2,1)S(1)}, u32[]{:S(2)}, u32[]{:S(2)}) collective-permute-start(bf16[5,96,128]{2,1,0:T(8,128)(2,1)S(1)} %add_convert_fusion._.halo0), channel_id=1, source_target_pairs={{0,2},{1,3},{2,0},{3,1},{4,6},{5,7},{6,4},{7,5},{8,10},{9,11},{10,... | collective-permute-start | bytes 368648 | tf_op jit(solution)/shard_map/ppermute | solution.py:434
  47.3 4.6 %collective-permute-done.3.second_prev = bf16[37,96,128]{2,1,0:T(8,128)(2,1)S(1)} collective-permute-done((bf16[37,96,128]{2,1,0:T(8,128)(2,1)S(1)}, bf16[37,96,128]{2,1,0:T(8,128)(2,1)S(1)}, u32[]{:S(2)}, u32[]{:S(2)}) %collective-permute-start.3) | collective-permute-done | bytes 909344 | tf_op jit(solution)/shard_map/ppermute | solution.py:434
  52.0 2.4 %shard_map.109.inner = f32[2,16,96,128]{3,2,1,0:T(8,128)S(1)} custom-call(s32[594]{0:T(1024)S(1)} %copy-done.4, f32[2,16,96,128]{3,2,1,0:T(8,128)S(1)} %shard_map.105.partial, bf16[37,96,128]{2,1,0:T(8,128)(2,1)S(1)} %collective-permute-done.3.second_prev, bf16[2,192,3584]{2,1,0:T(8,128)(2,1)S(1)} %shard_map.101.weights, ...), custom_call_target="tpu_custom_call" | custom-call | flops 12000000000 | bytes 1048576 | tf_op jit(solution)/shard_map/pallas_call | solution.py:500
  54.6 2.1 %collective-permute-done.11.halo2 = bf16[5,96,128]{2,1,0:T(8,128)(2,1)S(1)} collective-permute-done((bf16[5,96,128]{2,1,0:T(8,128)(2,1)S(1)}, bf16[5,96,128]{2,1,0:T(8,128)(2,1)S(1)}, u32[]{:S(2)}, u32[]{:S(2)}) %collective-permute-start.11) | collective-permute-done | bytes 122912 | tf_op jit(solution)/shard_map/ppermute | solution.py:434
  56.7 5.3 %shard_map.110 = bf16[2,16,96,128]{3,2,1,0:T(8,128)(2,1)S(1)} custom-call(s32[594]{0:T(1024)S(1)} %copy-done.4, f32[2,16,96,128]{3,2,1,0:T(8,128)S(1)} %shard_map.109.inner, bf16[5,96,128]{2,1,0:T(8,128)(2,1)S(1)} %get-tuple-element.16.record0, bf16[37,96,128]{2,1,0:T(8,128)(2,1)S(1)} %shard_map.104.second._.second_own, ...), custom_call_target="tpu_custom_call" | custom-call | flops 4000000000 | bytes 1048576 | tf_op jit(solution)/shard_map/pallas_call | solution.py:503
  62.0 1.2 %copy.30 = bf16[1,2,96,16,128]{4,3,2,1,0:T(8,128)(2,1)} copy(bf16[1,2,96,16,128]{4,2,3,1,0:T(8,128)(2,1)S(1)} %bitcast.23) | data formatting | bytes 1572864 | tf_op jit(solution)/shard_map/broadcast_in_dim | solution.py:516
  (41 shorter events, 1.0 us)
Async XLA Ops:
  0.0 3.7 %copy-start.5 = (s32[64,8]{0,1:T(8,128)S(1)}, s32[64,8]{0,1:T(8,128)}, u32[]{:S(2)}) copy-start(s32[64,8]{0,1:T(8,128)} %param.12) | copy-start | bytes 6148
  0.0 3.7 %copy-start.7 = (s32[64]{0:T(128)S(1)}, s32[64]{0:T(128)}, u32[]{:S(2)}) copy-start(s32[64]{0:T(128)} %tiles.1) | copy-start | bytes 772
  0.0 6.1 %copy-start.12 = (f32[96]{0:T(128)S(1)}, f32[96]{0:T(128)}, u32[]{:S(2)}) copy-start(f32[96]{0:T(128)} %param.16) | copy-start | bytes 1156
  0.0 6.1 %copy-start.11 = (f32[96]{0:T(128)S(1)}, f32[96]{0:T(128)}, u32[]{:S(2)}) copy-start(f32[96]{0:T(128)} %param.14) | copy-start | bytes 1156
  0.0 6.1 %copy-start.10 = (f32[96]{0:T(128)S(1)}, f32[96]{0:T(128)}, u32[]{:S(2)}) copy-start(f32[96]{0:T(128)} %param.17) | copy-start | bytes 1156
  0.0 6.1 %copy-start.9 = (f32[96]{0:T(128)S(1)}, f32[96]{0:T(128)}, u32[]{:S(2)}) copy-start(f32[96]{0:T(128)} %param.19) | copy-start | bytes 1156
  0.0 6.3 %copy-start.8 = (s32[16]{0:T(128)S(1)}, s32[16]{0:T(128)}, u32[]{:S(2)}) copy-start(s32[16]{0:T(128)} %param.13) | copy-start | bytes 196
  0.0 16.0 %copy-start.2 = (bf16[3,3,3,96,96]{4,3,2,1,0:T(8,128)(2,1)S(1)}, bf16[3,3,3,96,96]{4,3,2,1,0:T(8,128)(2,1)}, u32[]{:S(2)}) copy-start(bf16[3,3,3,96,96]{4,3,2,1,0:T(8,128)(2,1)} %param.15) | copy-start | bytes 1492996
  0.1 16.0 %copy-start.3 = (bf16[3,3,3,96,96]{4,3,2,1,0:T(8,128)(2,1)S(1)}, bf16[3,3,3,96,96]{4,3,2,1,0:T(8,128)(2,1)}, u32[]{:S(2)}) copy-start(bf16[3,3,3,96,96]{4,3,2,1,0:T(8,128)(2,1)} %param.18) | copy-start | bytes 1492996
  1.5 22.7 %collective-permute-start = (bf16[2,16,96,128]{3,2,1,0:T(8,128)(2,1)S(1)}, bf16[2,16,96,128]{3,2,1,0:T(8,128)(2,1)}, u32[]{:S(2)}, u32[]{:S(2)}) collective-permute-start(bf16[2,16,96,128]{3,2,1,0:T(8,128)(2,1)S(1)} %bitcast.19), channel_id=1, source_target_pairs={{0,1},{1,2},{2,3},{3,0},{4,5},{5,6},{6,7},{7,4},{8,9},{9,10},{10,1... | collective-permute-start | bytes 2359304 | tf_op jit(solution)/shard_map/ppermute | solution.py:434
  4.7 2.3 %collective-permute-start.1 = (bf16[9,48,128]{2,1,0:T(8,128)(2,1)S(1)}, bf16[9,48,128]{2,1,0:T(8,128)(2,1)S(1)}, u32[]{:S(2)}, u32[]{:S(2)}) collective-permute-start(bf16[9,48,128]{2,1,0:T(8,128)(2,1)S(1)} %get-tuple-element.11), channel_id=1, source_target_pairs={{0,4},{4,0},{8,12},{12,8},{16,20},{20,16},{24,28},{28,24},{32,36},... | collective-permute-start | bytes 331784 | tf_op jit(solution)/shard_map/ppermute | solution.py:430
  7.0 6.6 %copy-start = (bf16[2,9,48,128]{3,2,1,0:T(8,128)(2,1)}, bf16[2,9,48,128]{3,2,1,0:T(8,128)(2,1)S(1)}, u32[]{:S(2)}) copy-start(bf16[2,9,48,128]{3,2,1,0:T(8,128)(2,1)S(1)} %pad_maximum_fusion.1._.t0) | copy-start | bytes 663556
  7.0 13.0 %collective-permute-start.2 = (bf16[2,9,48,128]{3,2,1,0:T(8,128)(2,1)S(1)}, bf16[2,9,48,128]{3,2,1,0:T(8,128)(2,1)S(1)}, u32[]{:S(2)}, u32[]{:S(2)}) collective-permute-start(bf16[2,9,48,128]{3,2,1,0:T(8,128)(2,1)S(1)} %pad_maximum_fusion.1._.t0), channel_id=1, source_target_pairs={{0,32},{4,228},{8,40},{12,236},{16,48},{20,244},{24,56},{28,252},{... | collective-permute-start | bytes 663560 | tf_op jit(solution)/shard_map/ppermute | solution.py:430
  12.4 7.6 %collective-permute-start.4 = (bf16[2,9,48,128]{3,2,1,0:T(8,128)(2,1)S(1)}, bf16[2,9,48,128]{3,2,1,0:T(8,128)(2,1)S(1)}, u32[]{:S(2)}, u32[]{:S(2)}) collective-permute-start(bf16[2,9,48,128]{3,2,1,0:T(8,128)(2,1)S(1)} %pad_maximum_fusion.1._.t0), channel_id=1, source_target_pairs={{0,64},{4,196},{8,72},{12,204},{16,80},{20,212},{24,88},{28,220},{... | collective-permute-start | bytes 663560 | tf_op jit(solution)/shard_map/ppermute | solution.py:430
  16.1 0.9 %copy-start.1 = (bf16[2,9,48,128]{3,2,1,0:T(8,128)(2,1)S(1)}, bf16[2,9,48,128]{3,2,1,0:T(8,128)(2,1)}, u32[]{:S(2)}) copy-start(bf16[2,9,48,128]{3,2,1,0:T(8,128)(2,1)} %copy-done) | copy-start | bytes 663556
  17.6 6.6 %copy-start.4 = (s32[594]{0:T(1024)S(1)}, s32[594]{0:T(1024)}, u32[]{:S(2)}) copy-start(s32[594]{0:T(1024)} %concatenate.7.table) | copy-start | bytes 7132
  17.6 6.6 %copy-start.6 = (s32[48]{0:T(128)S(1)}, s32[48]{0:T(128)}, u32[]{:S(2)}) copy-start(s32[48]{0:T(128)} %shard_map.103._plan.plan) | copy-start | bytes 580
  20.1 11.1 %collective-permute-start.5 = (bf16[3,9,48,128]{3,2,1,0:T(8,128)(2,1)S(1)}, bf16[3,9,48,128]{3,2,1,0:T(8,128)(2,1)S(1)}, u32[]{:S(2)}, u32[]{:S(2)}) collective-permute-start(bf16[3,9,48,128]{3,2,1,0:T(8,128)(2,1)S(1)} %pad_maximum_fusion), channel_id=1, source_target_pairs={{0,64},{4,196},{8,72},{12,204},{16,80},{20,212},{24,88},{28,220},{... | collective-permute-start | bytes 995336 | tf_op jit(solution)/shard_map/ppermute | solution.py:430
  28.5 23.5 %collective-permute-start.3 = (bf16[37,96,128]{2,1,0:T(8,128)(2,1)S(1)}, bf16[37,96,128]{2,1,0:T(8,128)(2,1)S(1)}, u32[]{:S(2)}, u32[]{:S(2)}) collective-permute-start(bf16[37,96,128]{2,1,0:T(8,128)(2,1)S(1)} %shard_map.104.second._.second_own), channel_id=1, source_target_pairs={{0,1},{1,2},{2,3},{3,0},{4,5},{5,6},{6,7},{7,4},{8,9},{9,10},{10,1... | collective-permute-start | bytes 2727944 | tf_op jit(solution)/shard_map/ppermute | solution.py:434
  32.2 2.1 %collective-permute-start.6 = (bf16[4,5,96,128]{3,2,1,0:T(8,128)(2,1)S(1)}, bf16[4,5,96,128]{3,2,1,0:T(8,128)(2,1)S(1)}, u32[]{:S(2)}, u32[]{:S(2)}) collective-permute-start(bf16[4,5,96,128]{3,2,1,0:T(8,128)(2,1)S(1)} %shard_map.106._), channel_id=1, source_target_pairs={{0,4},{4,0},{8,12},{12,8},{16,20},{20,16},{24,28},{28,24},{32,36},... | collective-permute-start | bytes 1474568 | tf_op jit(solution)/shard_map/ppermute | solution.py:430
  35.0 7.5 %collective-permute-start.7 = (bf16[5,96,128]{2,1,0:T(8,128)(2,1)S(1)}, bf16[5,96,128]{2,1,0:T(8,128)(2,1)S(1)}, u32[]{:S(2)}, u32[]{:S(2)}) collective-permute-start(bf16[5,96,128]{2,1,0:T(8,128)(2,1)S(1)} %get-tuple-element.13), channel_id=1, source_target_pairs={{0,16},{4,20},{8,24},{12,28},{16,0},{20,4},{24,8},{28,12},{32,48},... | collective-permute-start | bytes 368648 | tf_op jit(solution)/shard_map/ppermute | solution.py:430
  38.1 6.2 %collective-permute-start.8 = (bf16[5,96,128]{2,1,0:T(8,128)(2,1)S(1)}, bf16[5,96,128]{2,1,0:T(8,128)(2,1)S(1)}, u32[]{:S(2)}, u32[]{:S(2)}) collective-permute-start(bf16[5,96,128]{2,1,0:T(8,128)(2,1)S(1)} %get-tuple-element.14), channel_id=1, source_target_pairs={{0,8},{4,12},{8,16},{12,20},{16,24},{20,28},{24,0},{28,4},{32,40},... | collective-permute-start | bytes 368648 | tf_op jit(solution)/shard_map/ppermute | solution.py:430
  38.5 5.9 %collective-permute-start.9 = (bf16[5,96,128]{2,1,0:T(8,128)(2,1)S(1)}, bf16[5,96,128]{2,1,0:T(8,128)(2,1)S(1)}, u32[]{:S(2)}, u32[]{:S(2)}) collective-permute-start(bf16[5,96,128]{2,1,0:T(8,128)(2,1)S(1)} %get-tuple-element.15), channel_id=1, source_target_pairs={{0,24},{4,28},{8,0},{12,4},{16,8},{20,12},{24,16},{28,20},{32,56},... | collective-permute-start | bytes 368648 | tf_op jit(solution)/shard_map/ppermute | solution.py:430
  44.5 10.1 %collective-permute-start.10 = (bf16[5,96,128]{2,1,0:T(8,128)(2,1)S(1)}, bf16[5,96,128]{2,1,0:T(8,128)(2,1)S(1)}, u32[]{:S(2)}, u32[]{:S(2)}) collective-permute-start(bf16[5,96,128]{2,1,0:T(8,128)(2,1)S(1)} %add_convert_fusion._.halo0), channel_id=1, source_target_pairs={{0,1},{1,2},{2,3},{3,0},{4,5},{5,6},{6,7},{7,4},{8,9},{9,10},{10,1... | collective-permute-start | bytes 368648 | tf_op jit(solution)/shard_map/ppermute | solution.py:434
  45.8 10.9 %collective-permute-start.11 = (bf16[5,96,128]{2,1,0:T(8,128)(2,1)S(1)}, bf16[5,96,128]{2,1,0:T(8,128)(2,1)S(1)}, u32[]{:S(2)}, u32[]{:S(2)}) collective-permute-start(bf16[5,96,128]{2,1,0:T(8,128)(2,1)S(1)} %add_convert_fusion._.halo0), channel_id=1, source_target_pairs={{0,2},{1,3},{2,0},{3,1},{4,6},{5,7},{6,4},{7,5},{8,10},{9,11},{10,... | collective-permute-start | bytes 368648 | tf_op jit(solution)/shard_map/ppermute | solution.py:434

commit v6 on v5

--- a/solution.py
+++ b/solution.py
@@ -293,14 +293,14 @@
             windows[fr, yy] = jnp.zeros((3 * C, W), BF)
 
 
-def band_parts(band, columns, base):
-    parts = row_parts([(band, base + fr) for fr in range(2 * F)], 0, 2)
-    for fr in range(2 * F):
+def band_parts(frames):
+    parts = row_parts([(band, f) for band, _, f in frames], 0, 2)
+    for n, (_, columns, f) in enumerate(frames):
         beside = [
-            jnp.concatenate([columns[base + fr, j + dx, dy] for dy in range(3) for dx in range(3)], axis=0)
+            jnp.concatenate([columns[f, j + dx, dy] for dy in range(3) for dx in range(3)], axis=0)
             for j in range(2)
         ]
-        parts[fr] = jnp.concatenate([parts[fr]] + beside, axis=1)
+        parts[n] = jnp.concatenate([parts[n]] + beside, axis=1)
     return parts
 
 
@@ -310,15 +310,9 @@
     columns[fr, k, 2] = rotate(value, W - 1).astype(BF)
 
 
-def outer_kernel(
-    table, inner, record0, second_own, second_prev, halo0, halo1, halo2, weights, vectors,
-    out, band1, columns1, band2, columns2
-):
+def border_windows(table, vectors, record, base, halo, exists, band, columns):
     up, left = sides(table)
-    bias1, gain1, gain2 = vectors[:, 0:1], vectors[:, 1:2], vectors[:, 2:3]
-    sources = ((second_prev, F * H, halo2), (second_own, F * H, halo1), (record0, 0, halo0))
-    lane = lanes(C)
-
+    gain = vectors[:, 1:2]
     src = lax.broadcasted_iota(jnp.int32, (W, 2 * W), 0)
     dst2 = lax.broadcasted_iota(jnp.int32, (W, 2 * W), 1)
     dst, col = dst2 % W, dst2 // W
@@ -329,37 +323,50 @@
     corner = jnp.where(up, above, below)
     past = jnp.where(up, 0, H + 2)
     first_col = jnp.where(left, 0, W - 2)
-    for fr in range(3 * F):
-        f = fr % F
-        record, base, halo = sources[fr // F]
-        exists = table[1] >= 2 - fr // F
+    for f in range(F):
         pick = (src == jnp.maximum(body, corner) + f * 32 + col).astype(F32).astype(BF)
         theirs = jnp.dot(halo[4], pick, preferred_element_type=F32)
-        theirs = norm_silu(jnp.where(exists, theirs, 0.0), gain1)
+        theirs = norm_silu(jnp.where(exists, theirs, 0.0), gain)
         picks = [(src == body + f * 32 + col).astype(F32).astype(BF)]
         for r in range(2):
             picks.append(((src == first_col + col) & (dst == past + r)).astype(F32).astype(BF))
         mine = jnp.concatenate([record[base + 4], halo[2 * f], halo[2 * f + 1]], axis=1)
         ours = jnp.dot(mine, jnp.concatenate(picks, axis=0), preferred_element_type=F32)
-        ours = norm_silu(jnp.where(exists, ours, 0.0), gain1)
+        ours = norm_silu(jnp.where(exists, ours, 0.0), gain)
         low, high = jnp.where(left, theirs, ours), jnp.where(left, ours, theirs)
         for k in range(4):
-            put_column(columns1, fr, k, (low if k < 2 else high)[:, (k % 2) * W : (k % 2 + 1) * W])
+            put_column(columns, f, k, (low if k < 2 else high)[:, (k % 2) * W : (k % 2 + 1) * W])
         near = jnp.where(left, theirs[:, W:], theirs[:, :W])
         for r in range(4):
             other, self = halo[2 * f + r % 2], record[base + 2 * f + r % 2]
             raw = jnp.where(up, other if r < 2 else self, self if r < 2 else other)
             at = jnp.where(up, r, H + r)
             moved = rotate(near, jnp.where(left, (W - at) % W, W - 1 - at))
-            center = norm_silu(jnp.where(exists, raw.astype(F32), 0.0), gain1)
+            center = norm_silu(jnp.where(exists, raw.astype(F32), 0.0), gain)
             put_window(
-                band1, (fr, r), three_shifts(center, jnp.where(left, moved, 0.0), jnp.where(left, 0.0, moved))
+                band, (f, r), three_shifts(center, jnp.where(left, moved, 0.0), jnp.where(left, 0.0, moved))
             )
+
+def own_border_kernel(table, record, halo, vectors, _, band, columns):
+    border_windows(table, vectors, record, 0, halo, True, band, columns)
+
+
+def outer_kernel(
+    table, inner, band0, columns0, second_own, second_prev, halo1, halo2, weights, vectors,
+    out, band1, columns1, bandp, columnsp, band2, columns2
+):
+    up, left = sides(table)
+    bias1, gain2 = vectors[:, 0:1], vectors[:, 2:3]
+    lane = lanes(C)
+    first_col = jnp.where(left, 0, W - 2)
+    border_windows(table, vectors, second_own, F * H, halo1, table[1] >= 1, band1, columns1)
+    border_windows(table, vectors, second_prev, F * H, halo2, table[1] >= 2, bandp, columnsp)
+    frames = [(b, c, f) for b, c in ((bandp, columnsp), (band1, columns1), (band0, columns0)) for f in range(F)]
 
     inside = (lane >= jnp.where(up, 3, 2)) & (lane < jnp.where(up, H + 2, H + 1))
     row_at, col_at = jnp.where(up, 0, 2), jnp.where(left, 0, 2)
     for p in range(2):
-        acc = product(weights.at[0], band_parts(band1, columns1, F * p))
+        acc = product(weights.at[0], band_parts(frames[F * p : F * p + 2 * F]))
         for f in range(F):
             s = F * p + f
             value = norm_silu(acc[f * C : (f + 1) * C] + bias1, gain2)
@@ -382,7 +389,7 @@
 
     length = table[T_CLIP + table[T_LIST + table[0]] // TPC]
     start = table[1] * F
-    acc = product(weights.at[1], band_parts(band2, columns2, 0))
+    acc = product(weights.at[1], band_parts([(band2, columns2, s) for s in range(2 * F)]))
     for f in range(F):
         value = acc[f * C : (f + 1) * C]
         for y in range(H):
@@ -500,19 +507,17 @@
     inner = call(inner_second_kernel, whole, "svvv-", scratch, 16, 12 * 10**9)(
         table, own_two, second_prev, weights, halo
     )
+    edges = [shape(F, 4, 3 * C, W), shape(F, 4, 3, C, W)]
+    border0 = call(own_border_kernel, edges, "svvv-")(table, record, halo, vectors, inner)
     out = call(
         outer_kernel,
         shape(F, H, C, W),
         "s" + "v" * 9,
-        [
-            pltpu.VMEM((3 * F, 4, 3 * C, W), BF),
-            pltpu.VMEM((3 * F, 4, 3, C, W), BF),
-            pltpu.VMEM((2 * F, 4, 3 * C, W), BF),
-            pltpu.VMEM((2 * F, 4, 3, C, W), BF),
-        ],
+        [pltpu.VMEM(edge.shape, BF) for edge in edges] * 2
+        + [pltpu.VMEM((2 * F, 4, 3 * C, W), BF), pltpu.VMEM((2 * F, 4, 3, C, W), BF)],
         24,
         4 * 10**9,
-    )(table, inner, record, second, second_prev, halo, halo1, halo2, weights, vectors)
+    )(table, inner, *border0, second, second_prev, halo1, halo2, weights, vectors)
     return out.transpose(0, 2, 1, 3)[None]
 
 

time: 63.3 us -> 63.4 us (level)
  the two profiles are of different devices: /device:TPU:1 before, /device:TPU:48 now
where the time goes in v6:
time: 63.4 us; the launch traced here: 63.2 us
  Pallas kernels  23.8 us (38%)
  starting transfers between devices  19.3 us (30%)
  waiting for transfers between devices  14.9 us (24%)
  local copies, waits for them, and re-layouts  4.58 us (7%)
    ppermute x8, starting transfers between devices, send(): return lax.ppermute(array, 'tile', pairs(move))  13.4 us
    ppermute x4, waiting for transfers between devices, later(): return lax.ppermute(array, 'group', [(i, (i + by) % NX) for i in range(NX)])  8.07 us
    ppermute x8, waiting for transfers between devices, send(): return lax.ppermute(array, 'tile', pairs(move))  6.86 us
    ppermute x4, starting transfers between devices, later(): return lax.ppermute(array, 'group', [(i, (i + by) % NX) for i in range(NX)])  5.94 us
    pallas_call x1, Pallas kernels, per_device(): call(outer_kernel, shape(F, H, C, W), 's' + 'v' * 9, [pltpu.VMEM(edge.sha...  4.91 us
    pallas_call x1, Pallas kernels, per_device(): call(inner_first_kernel, shape(F * H + REC, C, W), 'svvvv-s', scratch, 16...  4.31 us
    unnamed x28, local copies, waits for them, and re-layouts  2.51 us
    pallas_call x1, Pallas kernels, per_device(): pl.pallas_call(plan_kernel, out_shape=jax.ShapeDtypeStruct((12 * NY,), jn...  2.44 us
  transfers between devices with their start and end apart: 12, of which 6 were waited for; matrix products, arithmetic and copies ran while one was open for 2% of the time, Pallas kernels for 30%

profile of v6, /device:TPU:48, one launch (start us, length us, event | category | flops | bytes accessed | tf_op | source)
XLA Modules:
  0.0 63.2 jit_solution(10442635478334731449)
XLA Ops:
  0.1 1.4 %copy.33 = bf16[1,2,96,16,128]{4,2,3,1,0:T(8,128)(2,1)S(1)} copy(bf16[1,2,96,16,128]{4,3,2,1,0:T(8,128)(2,1)} %param.10) | data formatting | bytes 1572864 | tf_op args[0]
  1.5 1.6 %collective-permute-start = (bf16[2,16,96,128]{3,2,1,0:T(8,128)(2,1)S(1)}, bf16[2,16,96,128]{3,2,1,0:T(8,128)(2,1)}, u32[]{:S(2)}, u32[]{:S(2)}) collective-permute-start(bf16[2,16,96,128]{3,2,1,0:T(8,128)(2,1)S(1)} %bitcast.19), channel_id=1, source_target_pairs={{0,1},{1,2},{2,3},{3,0},{4,5},{5,6},{6,7},{7,4},{8,9},{9,10},{10,1... | collective-permute-start | bytes 2359304 | tf_op jit(solution)/shard_map/ppermute | solution.py:441
  3.2 1.0 %shard_map.100 = (bf16[5,96,128]{2,1,0:T(8,128)(2,1)S(1)}, bf16[9,48,128]{2,1,0:T(8,128)(2,1)S(1)}) custom-call(s32[2]{0:T(128)S(1)} %pad_add_fusion.ids, s32[64]{0:T(128)S(1)} %copy-done.7, s32[8,64]{1,0:T(8,128)S(1)} %bitcast.27, bf16[2,16,96,128]{3,2,1,0:T(8,128)(2,1)S(1)} %bitcast.20), custom_call_target="tpu_custom_call" | custom-call | bytes 1048576 | tf_op jit(solution)/shard_map/pallas_call | solution.py:483
  4.6 0.7 %concatenate.7.table = s32[594]{0:T(1024)} concatenate(s32[1]{0:T(128)} %bitcast, s32[1]{0:T(128)} %bitcast.1, s32[64]{0:T(128)S(1)} %copy-done.7, s32[512]{0:T(512)S(1)} %reshape.9, s32[16]{0:T(128)S(1)} %copy-done.8), dimensions={0} | concatenate | bytes 4752 | tf_op jit(solution)/shard_map/concatenate | solution.py:472
  5.3 0.3 collective-permute-done.1
  5.6 3.3 %collective-permute-start.4 = (bf16[2,9,48,128]{3,2,1,0:T(8,128)(2,1)S(1)}, bf16[2,9,48,128]{3,2,1,0:T(8,128)(2,1)S(1)}, u32[]{:S(2)}, u32[]{:S(2)}) collective-permute-start(bf16[2,9,48,128]{3,2,1,0:T(8,128)(2,1)S(1)} %pad_maximum_fusion.1._.t0), channel_id=1, source_target_pairs={{0,64},{4,196},{8,72},{12,204},{16,80},{20,212},{24,88},{28,220},{... | collective-permute-start | bytes 663560 | tf_op jit(solution)/shard_map/ppermute | solution.py:437
  8.9 3.1 %collective-permute-start.2 = (bf16[2,9,48,128]{3,2,1,0:T(8,128)(2,1)S(1)}, bf16[2,9,48,128]{3,2,1,0:T(8,128)(2,1)S(1)}, u32[]{:S(2)}, u32[]{:S(2)}) collective-permute-start(bf16[2,9,48,128]{3,2,1,0:T(8,128)(2,1)S(1)} %pad_maximum_fusion.1._.t0), channel_id=1, source_target_pairs={{0,32},{4,228},{8,40},{12,236},{16,48},{20,244},{24,56},{28,252},{... | collective-permute-start | bytes 663560 | tf_op jit(solution)/shard_map/ppermute | solution.py:437
  12.1 2.4 %shard_map.103._plan.plan = s32[48]{0:T(128)} custom-call(s32[594]{0:T(1024)} %concatenate.7.table, bf16[2,9,48,128]{3,2,1,0:T(8,128)(2,1)} %copy-done), custom_call_target="tpu_custom_call" | custom-call | tf_op jit(solution)/shard_map/pallas_call | solution.py:488
  14.5 0.9 %copy-done.1 = bf16[2,9,48,128]{3,2,1,0:T(8,128)(2,1)S(1)} copy-done((bf16[2,9,48,128]{3,2,1,0:T(8,128)(2,1)S(1)}, bf16[2,9,48,128]{3,2,1,0:T(8,128)(2,1)}, u32[]{:S(2)}) %copy-start.1) | copy-done | bytes 221208
  15.5 0.6 shard_map.101.weights
  16.1 2.4 %shard_map.102.partial = f32[8,192,256]{2,1,0:T(8,128)S(1)} custom-call(bf16[2,16,96,128]{3,2,1,0:T(8,128)(2,1)S(1)} %bitcast.21, bf16[2,192,3584]{2,1,0:T(8,128)(2,1)S(1)} %shard_map.101.weights, f32[96,4]{1,0:T(8,128)S(1)} %copy.26.vectors), custom_call_target="tpu_custom_call" | custom-call | flops 3000000000 | bytes 1048576 | tf_op jit(solution)/shard_map/pallas_call | solution.py:496
  18.5 3.7 %collective-permute-start.5 = (bf16[3,9,48,128]{3,2,1,0:T(8,128)(2,1)S(1)}, bf16[3,9,48,128]{3,2,1,0:T(8,128)(2,1)S(1)}, u32[]{:S(2)}, u32[]{:S(2)}) collective-permute-start(bf16[3,9,48,128]{3,2,1,0:T(8,128)(2,1)S(1)} %pad_maximum_fusion), channel_id=1, source_target_pairs={{0,64},{4,196},{8,72},{12,204},{16,80},{20,212},{24,88},{28,220},{... | collective-permute-start | bytes 995336 | tf_op jit(solution)/shard_map/ppermute | solution.py:437
  22.2 4.3 %shard_map.104.second._.second_own = bf16[37,96,128]{2,1,0:T(8,128)(2,1)S(1)} custom-call(s32[594]{0:T(1024)S(1)} %copy-done.4, bf16[2,16,96,128]{3,2,1,0:T(8,128)(2,1)} %collective-permute-done.prev, f32[8,192,256]{2,1,0:T(8,128)S(1)} %shard_map.102.partial, bf16[2,192,3584]{2,1,0:T(8,128)(2,1)S(1)} %shard_map.101.weights, f32[96,4]{1,0:T(8,128)S(1)} %copy.26.vectors, ...), custom_call_target="tpu_custom_call" | custom-call | flops 8000000000 | bytes 1048576 | tf_op jit(solution)/shard_map/pallas_call | solution.py:499
  26.6 1.6 %collective-permute-start.3 = (bf16[37,96,128]{2,1,0:T(8,128)(2,1)S(1)}, bf16[37,96,128]{2,1,0:T(8,128)(2,1)S(1)}, u32[]{:S(2)}, u32[]{:S(2)}) collective-permute-start(bf16[37,96,128]{2,1,0:T(8,128)(2,1)S(1)} %shard_map.104.second._.second_own), channel_id=1, source_target_pairs={{0,1},{1,2},{2,3},{3,0},{4,5},{5,6},{6,7},{7,4},{8,9},{9,10},{10,1... | collective-permute-start | bytes 2727944 | tf_op jit(solution)/shard_map/ppermute | solution.py:441
  28.1 1.6 %collective-permute-done.5.t3 = bf16[3,9,48,128]{3,2,1,0:T(8,128)(2,1)S(1)} collective-permute-done((bf16[3,9,48,128]{3,2,1,0:T(8,128)(2,1)S(1)}, bf16[3,9,48,128]{3,2,1,0:T(8,128)(2,1)S(1)}, u32[]{:S(2)}, u32[]{:S(2)}) %collective-permute-start.5) | collective-permute-done | bytes 331808 | tf_op jit(solution)/shard_map/ppermute | solution.py:437
  29.7 1.1 %shard_map.106._ = bf16[4,5,96,128]{3,2,1,0:T(8,128)(2,1)S(1)} custom-call(s32[48]{0:T(128)S(1)} %copy-done.6, bf16[2,9,48,128]{3,2,1,0:T(8,128)(2,1)S(1)} %copy-done.1, bf16[2,9,48,128]{3,2,1,0:T(8,128)(2,1)S(1)} %collective-permute-done.2._.t1, bf16[2,9,48,128]{3,2,1,0:T(8,128)(2,1)S(1)} %collective-permute-done.4.t2, ...), custom_call_target="tpu_custom_call" | custom-call | bytes 1048576 | tf_op jit(solution)/shard_map/pallas_call | solution.py:458
  30.8 0.3 collective-permute-start.6
  31.0 1.1 %shard_map.107.mine = bf16[4,5,96,128]{3,2,1,0:T(8,128)(2,1)S(1)} custom-call(s32[48]{0:T(128)S(1)} %copy-done.6, bf16[2,9,48,128]{3,2,1,0:T(8,128)(2,1)S(1)} %copy-done.1, bf16[2,9,48,128]{3,2,1,0:T(8,128)(2,1)S(1)} %collective-permute-done.2._.t1, bf16[2,9,48,128]{3,2,1,0:T(8,128)(2,1)S(1)} %collective-permute-done.4.t2, ...), custom_call_target="tpu_custom_call" | custom-call | bytes 1048576 | tf_op jit(solution)/shard_map/pallas_call | solution.py:460
  32.1 0.8 %collective-permute-done.6.arrived = bf16[4,5,96,128]{3,2,1,0:T(8,128)(2,1)S(1)} collective-permute-done((bf16[4,5,96,128]{3,2,1,0:T(8,128)(2,1)S(1)}, bf16[4,5,96,128]{3,2,1,0:T(8,128)(2,1)S(1)}, u32[]{:S(2)}, u32[]{:S(2)}) %collective-permute-start.6) | collective-permute-done | bytes 491552 | tf_op jit(solution)/shard_map/ppermute | solution.py:437
  32.9 0.7 %shard_map.108 = (bf16[5,96,128]{2,1,0:T(8,128)(2,1)S(1)}, bf16[5,96,128]{2,1,0:T(8,128)(2,1)S(1)}, bf16[5,96,128]{2,1,0:T(8,128)(2,1)S(1)}, bf16[5,96,128]{2,1,0:T(8,128)(2,1)S(1)}) custom-call(s32[594]{0:T(1024)S(1)} %copy-done.4, bf16[4,5,96,128]{3,2,1,0:T(8,128)(2,1)S(1)} %shard_map.107.mine, bf16[4,5,96,128]{3,2,1,0:T(8,128)(2,1)S(1)} %collective-permute-done.6.arrived), custom_call_target="tpu_custom_call" | custom-call | bytes 1048576 | tf_op jit(solution)/shard_map/pallas_call | solution.py:461
  33.6 0.4 collective-permute-start.7
  34.0 2.2 %collective-permute-start.8 = (bf16[5,96,128]{2,1,0:T(8,128)(2,1)S(1)}, bf16[5,96,128]{2,1,0:T(8,128)(2,1)S(1)}, u32[]{:S(2)}, u32[]{:S(2)}) collective-permute-start(bf16[5,96,128]{2,1,0:T(8,128)(2,1)S(1)} %get-tuple-element.16), channel_id=1, source_target_pairs={{0,8},{4,12},{8,16},{12,20},{16,24},{20,28},{24,0},{28,4},{32,40},... | collective-permute-start | bytes 368648 | tf_op jit(solution)/shard_map/ppermute | solution.py:437
  36.2 0.3 collective-permute-start.9
  36.5 1.8 %shard_map.105.partial = f32[2,16,96,128]{3,2,1,0:T(8,128)S(1)} custom-call(bf16[2,16,96,128]{3,2,1,0:T(8,128)(2,1)S(1)} %bitcast.22, bf16[37,96,128]{2,1,0:T(8,128)(2,1)S(1)} %shard_map.104.second._.second_own, bf16[2,192,3584]{2,1,0:T(8,128)(2,1)S(1)} %shard_map.101.weights, f32[96,4]{1,0:T(8,128)S(1)} %copy.26.vectors), custom_call_target="tpu_custom_call" | custom-call | flops 1000000000 | bytes 1048576 | tf_op jit(solution)/shard_map/pallas_call | solution.py:503
  38.3 3.1 %collective-permute-done.7 = bf16[5,96,128]{2,1,0:T(8,128)(2,1)S(1)} collective-permute-done((bf16[5,96,128]{2,1,0:T(8,128)(2,1)S(1)}, bf16[5,96,128]{2,1,0:T(8,128)(2,1)S(1)}, u32[]{:S(2)}, u32[]{:S(2)}) %collective-permute-start.7) | collective-permute-done | bytes 122912 | tf_op jit(solution)/shard_map/ppermute | solution.py:437
  41.4 1.0 %collective-permute-done.8 = bf16[5,96,128]{2,1,0:T(8,128)(2,1)S(1)} collective-permute-done((bf16[5,96,128]{2,1,0:T(8,128)(2,1)S(1)}, bf16[5,96,128]{2,1,0:T(8,128)(2,1)S(1)}, u32[]{:S(2)}, u32[]{:S(2)}) %collective-permute-start.8) | collective-permute-done | bytes 122912 | tf_op jit(solution)/shard_map/ppermute | solution.py:437
  42.5 2.8 %collective-permute-start.11 = (bf16[5,96,128]{2,1,0:T(8,128)(2,1)S(1)}, bf16[5,96,128]{2,1,0:T(8,128)(2,1)S(1)}, u32[]{:S(2)}, u32[]{:S(2)}) collective-permute-start(bf16[5,96,128]{2,1,0:T(8,128)(2,1)S(1)} %add_convert_fusion._.halo), channel_id=1, source_target_pairs={{0,2},{1,3},{2,0},{3,1},{4,6},{5,7},{6,4},{7,5},{8,10},{9,11},{10,... | collective-permute-start | bytes 368648 | tf_op jit(solution)/shard_map/ppermute | solution.py:441
  45.4 8.1 %collective-permute-done.3.second_prev = bf16[37,96,128]{2,1,0:T(8,128)(2,1)S(1)} collective-permute-done((bf16[37,96,128]{2,1,0:T(8,128)(2,1)S(1)}, bf16[37,96,128]{2,1,0:T(8,128)(2,1)S(1)}, u32[]{:S(2)}, u32[]{:S(2)}) %collective-permute-start.3) | collective-permute-done | bytes 909344 | tf_op jit(solution)/shard_map/ppermute | solution.py:441
  53.4 2.4 %shard_map.109._.inner = f32[2,16,96,128]{3,2,1,0:T(8,128)S(1)} custom-call(s32[594]{0:T(1024)S(1)} %copy-done.4, f32[2,16,96,128]{3,2,1,0:T(8,128)S(1)} %shard_map.105.partial, bf16[37,96,128]{2,1,0:T(8,128)(2,1)S(1)} %collective-permute-done.3.second_prev, bf16[2,192,3584]{2,1,0:T(8,128)(2,1)S(1)} %shard_map.101.weights, ...), custom_call_target="tpu_custom_call" | custom-call | flops 12000000000 | bytes 1048576 | tf_op jit(solution)/shard_map/pallas_call | solution.py:507
  55.8 1.3 %shard_map.110 = (bf16[2,4,288,128]{3,2,1,0:T(8,128)(2,1)S(1)}, bf16[2,4,3,96,128]{4,3,2,1,0:T(8,128)(2,1)S(1)}) custom-call(s32[594]{0:T(1024)S(1)} %copy-done.4, bf16[5,96,128]{2,1,0:T(8,128)(2,1)S(1)} %get-tuple-element.18.record, bf16[5,96,128]{2,1,0:T(8,128)(2,1)S(1)} %add_convert_fusion._.halo, f32[96,4]{1,0:T(8,128)S(1)} %copy.26.vectors, ...), custom_call_target="tpu_custom_call" | custom-call | bytes 1048576 | tf_op jit(solution)/shard_map/pallas_call | solution.py:511
  57.1 4.9 %shard_map.111 = bf16[2,16,96,128]{3,2,1,0:T(8,128)(2,1)S(1)} custom-call(s32[594]{0:T(1024)S(1)} %copy-done.4, f32[2,16,96,128]{3,2,1,0:T(8,128)S(1)} %shard_map.109._.inner, bf16[2,4,288,128]{3,2,1,0:T(8,128)(2,1)S(1)} %get-tuple-element.19.band0, bf16[2,4,3,96,128]{4,3,2,1,0:T(8,128)(2,1)S(1)} %get-tuple-element.20.columns0, ...), custom_call_target="tpu_custom_call" | custom-call | flops 4000000000 | bytes 1048576 | tf_op jit(solution)/shard_map/pallas_call | solution.py:512
  62.0 1.2 %copy.31 = bf16[1,2,96,16,128]{4,3,2,1,0:T(8,128)(2,1)} copy(bf16[1,2,96,16,128]{4,2,3,1,0:T(8,128)(2,1)S(1)} %bitcast.23) | data formatting | bytes 1572864 | tf_op jit(solution)/shard_map/broadcast_in_dim | solution.py:521
  (42 shorter events, 0.7 us)
Async XLA Ops:
  0.0 3.2 %copy-start.7 = (s32[64]{0:T(128)S(1)}, s32[64]{0:T(128)}, u32[]{:S(2)}) copy-start(s32[64]{0:T(128)} %tiles.1) | copy-start | bytes 772
  0.0 3.2 %copy-start.5 = (s32[64,8]{0,1:T(8,128)S(1)}, s32[64,8]{0,1:T(8,128)}, u32[]{:S(2)}) copy-start(s32[64,8]{0,1:T(8,128)} %param.12) | copy-start | bytes 6148
  0.0 4.4 %copy-start.9 = (f32[96]{0:T(128)S(1)}, f32[96]{0:T(128)}, u32[]{:S(2)}) copy-start(f32[96]{0:T(128)} %param.19) | copy-start | bytes 1156
  0.0 4.4 %copy-start.10 = (f32[96]{0:T(128)S(1)}, f32[96]{0:T(128)}, u32[]{:S(2)}) copy-start(f32[96]{0:T(128)} %param.17) | copy-start | bytes 1156
  0.0 4.4 %copy-start.12 = (f32[96]{0:T(128)S(1)}, f32[96]{0:T(128)}, u32[]{:S(2)}) copy-start(f32[96]{0:T(128)} %param.16) | copy-start | bytes 1156
  0.0 4.4 %copy-start.11 = (f32[96]{0:T(128)S(1)}, f32[96]{0:T(128)}, u32[]{:S(2)}) copy-start(f32[96]{0:T(128)} %param.14) | copy-start | bytes 1156
  0.0 4.5 %copy-start.8 = (s32[16]{0:T(128)S(1)}, s32[16]{0:T(128)}, u32[]{:S(2)}) copy-start(s32[16]{0:T(128)} %param.13) | copy-start | bytes 196
  0.0 14.5 %copy-start.3 = (bf16[3,3,3,96,96]{4,3,2,1,0:T(8,128)(2,1)S(1)}, bf16[3,3,3,96,96]{4,3,2,1,0:T(8,128)(2,1)}, u32[]{:S(2)}) copy-start(bf16[3,3,3,96,96]{4,3,2,1,0:T(8,128)(2,1)} %param.18) | copy-start | bytes 1492996
  0.1 14.5 %copy-start.2 = (bf16[3,3,3,96,96]{4,3,2,1,0:T(8,128)(2,1)S(1)}, bf16[3,3,3,96,96]{4,3,2,1,0:T(8,128)(2,1)}, u32[]{:S(2)}) copy-start(bf16[3,3,3,96,96]{4,3,2,1,0:T(8,128)(2,1)} %param.15) | copy-start | bytes 1492996
  1.5 20.7 %collective-permute-start = (bf16[2,16,96,128]{3,2,1,0:T(8,128)(2,1)S(1)}, bf16[2,16,96,128]{3,2,1,0:T(8,128)(2,1)}, u32[]{:S(2)}, u32[]{:S(2)}) collective-permute-start(bf16[2,16,96,128]{3,2,1,0:T(8,128)(2,1)S(1)} %bitcast.19), channel_id=1, source_target_pairs={{0,1},{1,2},{2,3},{3,0},{4,5},{5,6},{6,7},{7,4},{8,9},{9,10},{10,1... | collective-permute-start | bytes 2359304 | tf_op jit(solution)/shard_map/ppermute | solution.py:441
  4.1 1.4 %collective-permute-start.1 = (bf16[9,48,128]{2,1,0:T(8,128)(2,1)S(1)}, bf16[9,48,128]{2,1,0:T(8,128)(2,1)S(1)}, u32[]{:S(2)}, u32[]{:S(2)}) collective-permute-start(bf16[9,48,128]{2,1,0:T(8,128)(2,1)S(1)} %get-tuple-element.13), channel_id=1, source_target_pairs={{0,4},{4,0},{8,12},{12,8},{16,20},{20,16},{24,28},{28,24},{32,36},... | collective-permute-start | bytes 331784 | tf_op jit(solution)/shard_map/ppermute | solution.py:437
  5.6 6.5 %copy-start = (bf16[2,9,48,128]{3,2,1,0:T(8,128)(2,1)}, bf16[2,9,48,128]{3,2,1,0:T(8,128)(2,1)S(1)}, u32[]{:S(2)}) copy-start(bf16[2,9,48,128]{3,2,1,0:T(8,128)(2,1)S(1)} %pad_maximum_fusion.1._.t0) | copy-start | bytes 663556
  5.6 12.9 %collective-permute-start.4 = (bf16[2,9,48,128]{3,2,1,0:T(8,128)(2,1)S(1)}, bf16[2,9,48,128]{3,2,1,0:T(8,128)(2,1)S(1)}, u32[]{:S(2)}, u32[]{:S(2)}) collective-permute-start(bf16[2,9,48,128]{3,2,1,0:T(8,128)(2,1)S(1)} %pad_maximum_fusion.1._.t0), channel_id=1, source_target_pairs={{0,64},{4,196},{8,72},{12,204},{16,80},{20,212},{24,88},{28,220},{... | collective-permute-start | bytes 663560 | tf_op jit(solution)/shard_map/ppermute | solution.py:437
  8.9 9.5 %collective-permute-start.2 = (bf16[2,9,48,128]{3,2,1,0:T(8,128)(2,1)S(1)}, bf16[2,9,48,128]{3,2,1,0:T(8,128)(2,1)S(1)}, u32[]{:S(2)}, u32[]{:S(2)}) collective-permute-start(bf16[2,9,48,128]{3,2,1,0:T(8,128)(2,1)S(1)} %pad_maximum_fusion.1._.t0), channel_id=1, source_target_pairs={{0,32},{4,228},{8,40},{12,236},{16,48},{20,244},{24,56},{28,252},{... | collective-permute-start | bytes 663560 | tf_op jit(solution)/shard_map/ppermute | solution.py:437
  14.5 0.9 %copy-start.1 = (bf16[2,9,48,128]{3,2,1,0:T(8,128)(2,1)S(1)}, bf16[2,9,48,128]{3,2,1,0:T(8,128)(2,1)}, u32[]{:S(2)}) copy-start(bf16[2,9,48,128]{3,2,1,0:T(8,128)(2,1)} %copy-done) | copy-start | bytes 663556
  16.0 6.2 %copy-start.4 = (s32[594]{0:T(1024)S(1)}, s32[594]{0:T(1024)}, u32[]{:S(2)}) copy-start(s32[594]{0:T(1024)} %concatenate.7.table) | copy-start | bytes 7132
  16.0 6.2 %copy-start.6 = (s32[48]{0:T(128)S(1)}, s32[48]{0:T(128)}, u32[]{:S(2)}) copy-start(s32[48]{0:T(128)} %shard_map.103._plan.plan) | copy-start | bytes 580
  18.5 11.2 %collective-permute-start.5 = (bf16[3,9,48,128]{3,2,1,0:T(8,128)(2,1)S(1)}, bf16[3,9,48,128]{3,2,1,0:T(8,128)(2,1)S(1)}, u32[]{:S(2)}, u32[]{:S(2)}) collective-permute-start(bf16[3,9,48,128]{3,2,1,0:T(8,128)(2,1)S(1)} %pad_maximum_fusion), channel_id=1, source_target_pairs={{0,64},{4,196},{8,72},{12,204},{16,80},{20,212},{24,88},{28,220},{... | collective-permute-start | bytes 995336 | tf_op jit(solution)/shard_map/ppermute | solution.py:437
  26.6 26.9 %collective-permute-start.3 = (bf16[37,96,128]{2,1,0:T(8,128)(2,1)S(1)}, bf16[37,96,128]{2,1,0:T(8,128)(2,1)S(1)}, u32[]{:S(2)}, u32[]{:S(2)}) collective-permute-start(bf16[37,96,128]{2,1,0:T(8,128)(2,1)S(1)} %shard_map.104.second._.second_own), channel_id=1, source_target_pairs={{0,1},{1,2},{2,3},{3,0},{4,5},{5,6},{6,7},{7,4},{8,9},{9,10},{10,1... | collective-permute-start | bytes 2727944 | tf_op jit(solution)/shard_map/ppermute | solution.py:441
  30.8 2.1 %collective-permute-start.6 = (bf16[4,5,96,128]{3,2,1,0:T(8,128)(2,1)S(1)}, bf16[4,5,96,128]{3,2,1,0:T(8,128)(2,1)S(1)}, u32[]{:S(2)}, u32[]{:S(2)}) collective-permute-start(bf16[4,5,96,128]{3,2,1,0:T(8,128)(2,1)S(1)} %shard_map.106._), channel_id=1, source_target_pairs={{0,4},{4,0},{8,12},{12,8},{16,20},{20,16},{24,28},{28,24},{32,36},... | collective-permute-start | bytes 1474568 | tf_op jit(solution)/shard_map/ppermute | solution.py:437
  33.6 7.8 %collective-permute-start.7 = (bf16[5,96,128]{2,1,0:T(8,128)(2,1)S(1)}, bf16[5,96,128]{2,1,0:T(8,128)(2,1)S(1)}, u32[]{:S(2)}, u32[]{:S(2)}) collective-permute-start(bf16[5,96,128]{2,1,0:T(8,128)(2,1)S(1)} %get-tuple-element.15), channel_id=1, source_target_pairs={{0,16},{4,20},{8,24},{12,28},{16,0},{20,4},{24,8},{28,12},{32,48},... | collective-permute-start | bytes 368648 | tf_op jit(solution)/shard_map/ppermute | solution.py:437
  34.0 8.4 %collective-permute-start.8 = (bf16[5,96,128]{2,1,0:T(8,128)(2,1)S(1)}, bf16[5,96,128]{2,1,0:T(8,128)(2,1)S(1)}, u32[]{:S(2)}, u32[]{:S(2)}) collective-permute-start(bf16[5,96,128]{2,1,0:T(8,128)(2,1)S(1)} %get-tuple-element.16), channel_id=1, source_target_pairs={{0,8},{4,12},{8,16},{12,20},{16,24},{20,28},{24,0},{28,4},{32,40},... | collective-permute-start | bytes 368648 | tf_op jit(solution)/shard_map/ppermute | solution.py:437
  36.2 6.2 %collective-permute-start.9 = (bf16[5,96,128]{2,1,0:T(8,128)(2,1)S(1)}, bf16[5,96,128]{2,1,0:T(8,128)(2,1)S(1)}, u32[]{:S(2)}, u32[]{:S(2)}) collective-permute-start(bf16[5,96,128]{2,1,0:T(8,128)(2,1)S(1)} %get-tuple-element.17), channel_id=1, source_target_pairs={{0,24},{4,28},{8,0},{12,4},{16,8},{20,12},{24,16},{28,20},{32,56},... | collective-permute-start | bytes 368648 | tf_op jit(solution)/shard_map/ppermute | solution.py:437
  42.5 14.5 %collective-permute-start.11 = (bf16[5,96,128]{2,1,0:T(8,128)(2,1)S(1)}, bf16[5,96,128]{2,1,0:T(8,128)(2,1)S(1)}, u32[]{:S(2)}, u32[]{:S(2)}) collective-permute-start(bf16[5,96,128]{2,1,0:T(8,128)(2,1)S(1)} %add_convert_fusion._.halo), channel_id=1, source_target_pairs={{0,2},{1,3},{2,0},{3,1},{4,6},{5,7},{6,4},{7,5},{8,10},{9,11},{10,... | collective-permute-start | bytes 368648 | tf_op jit(solution)/shard_map/ppermute | solution.py:441
  45.3 11.7 %collective-permute-start.10 = (bf16[5,96,128]{2,1,0:T(8,128)(2,1)S(1)}, bf16[5,96,128]{2,1,0:T(8,128)(2,1)S(1)}, u32[]{:S(2)}, u32[]{:S(2)}) collective-permute-start(bf16[5,96,128]{2,1,0:T(8,128)(2,1)S(1)} %add_convert_fusion._.halo), channel_id=1, source_target_pairs={{0,1},{1,2},{2,3},{3,0},{4,5},{5,6},{6,7},{7,4},{8,9},{9,10},{10,1... | collective-permute-start | bytes 368648 | tf_op jit(solution)/shard_map/ppermute | solution.py:441

commit v7 on v6

--- a/solution.py
+++ b/solution.py
@@ -352,7 +352,7 @@
 
 
 def outer_kernel(
-    table, inner, band0, columns0, second_own, second_prev, halo1, halo2, weights, vectors,
+    table, inner, band0, columns0, second_own, second_prev, halo2, halo1, weights, vectors,
     out, band1, columns1, bandp, columnsp, band2, columns2
 ):
     up, left = sides(table)
@@ -517,7 +517,7 @@
         + [pltpu.VMEM((2 * F, 4, 3 * C, W), BF), pltpu.VMEM((2 * F, 4, 3, C, W), BF)],
         24,
         4 * 10**9,
-    )(table, inner, *border0, second, second_prev, halo1, halo2, weights, vectors)
+    )(table, inner, *border0, second, second_prev, halo2, halo1, weights, vectors)
     return out.transpose(0, 2, 1, 3)[None]
 
 

time: 63.4 us -> 61.9 us (0.976)
  the two profiles are of different devices: /device:TPU:48 before, /device:TPU:1 now
where the time goes in v7:
time: 61.9 us; the launch traced here: 61.5 us
  starting transfers between devices  25.4 us (41%)
  Pallas kernels  23.8 us (38%)
  waiting for transfers between devices  7.28 us (12%)
  local copies, waits for them, and re-layouts  4.58 us (7%)
    ppermute x8, starting transfers between devices, send(): return lax.ppermute(array, 'tile', pairs(move))  19.1 us
    ppermute x4, starting transfers between devices, later(): return lax.ppermute(array, 'group', [(i, (i + by) % NX) for i in range(NX)])  6.26 us
    ppermute x8, waiting for transfers between devices, send(): return lax.ppermute(array, 'tile', pairs(move))  5.02 us
    pallas_call x1, Pallas kernels, per_device(): call(outer_kernel, shape(F, H, C, W), 's' + 'v' * 9, [pltpu.VMEM(edge.sha...  4.9 us
    pallas_call x1, Pallas kernels, per_device(): call(inner_first_kernel, shape(F * H + REC, C, W), 'svvvv-s', scratch, 16...  4.3 us
    unnamed x28, local copies, waits for them, and re-layouts  2.51 us
    pallas_call x1, Pallas kernels, per_device(): pl.pallas_call(plan_kernel, out_shape=jax.ShapeDtypeStruct((12 * NY,), jn...  2.44 us
    pallas_call x1, Pallas kernels, per_device(): call(own_first_kernel, jax.ShapeDtypeStruct((H // 2, 2 * C, 2 * W), F32),...  2.37 us
  transfers between devices with their start and end apart: 12, of which 6 were waited for; matrix products, arithmetic and copies ran while one was open for 2% of the time, Pallas kernels for 31%

profile of v7, /device:TPU:1, one launch (start us, length us, event | category | flops | bytes accessed | tf_op | source)
XLA Modules:
  0.0 61.5 jit_solution(15381932950697435668)
XLA Ops:
  0.1 1.4 %copy.33 = bf16[1,2,96,16,128]{4,2,3,1,0:T(8,128)(2,1)S(1)} copy(bf16[1,2,96,16,128]{4,3,2,1,0:T(8,128)(2,1)} %param.10) | data formatting | bytes 1572864 | tf_op args[0]
  1.5 2.1 %collective-permute-start = (bf16[2,16,96,128]{3,2,1,0:T(8,128)(2,1)S(1)}, bf16[2,16,96,128]{3,2,1,0:T(8,128)(2,1)}, u32[]{:S(2)}, u32[]{:S(2)}) collective-permute-start(bf16[2,16,96,128]{3,2,1,0:T(8,128)(2,1)S(1)} %bitcast.19), channel_id=1, source_target_pairs={{0,1},{1,2},{2,3},{3,0},{4,5},{5,6},{6,7},{7,4},{8,9},{9,10},{10,1... | collective-permute-start | bytes 2359304 | tf_op jit(solution)/shard_map/ppermute | solution.py:441
  3.7 1.0 %shard_map.100 = (bf16[5,96,128]{2,1,0:T(8,128)(2,1)S(1)}, bf16[9,48,128]{2,1,0:T(8,128)(2,1)S(1)}) custom-call(s32[2]{0:T(128)S(1)} %pad_add_fusion.ids, s32[64]{0:T(128)S(1)} %copy-done.7, s32[8,64]{1,0:T(8,128)S(1)} %bitcast.27, bf16[2,16,96,128]{3,2,1,0:T(8,128)(2,1)S(1)} %bitcast.20), custom_call_target="tpu_custom_call" | custom-call | bytes 1048576 | tf_op jit(solution)/shard_map/pallas_call | solution.py:483
  4.7 1.3 %collective-permute-start.1 = (bf16[9,48,128]{2,1,0:T(8,128)(2,1)S(1)}, bf16[9,48,128]{2,1,0:T(8,128)(2,1)S(1)}, u32[]{:S(2)}, u32[]{:S(2)}) collective-permute-start(bf16[9,48,128]{2,1,0:T(8,128)(2,1)S(1)} %get-tuple-element.13), channel_id=1, source_target_pairs={{0,4},{4,0},{8,12},{12,8},{16,20},{20,16},{24,28},{28,24},{32,36},... | collective-permute-start | bytes 331784 | tf_op jit(solution)/shard_map/ppermute | solution.py:437
  6.3 0.7 %concatenate.7.table = s32[594]{0:T(1024)} concatenate(s32[1]{0:T(128)} %bitcast, s32[1]{0:T(128)} %bitcast.1, s32[64]{0:T(128)S(1)} %copy-done.7, s32[512]{0:T(512)S(1)} %reshape.9, s32[16]{0:T(128)S(1)} %copy-done.8), dimensions={0} | concatenate | bytes 4752 | tf_op jit(solution)/shard_map/concatenate | solution.py:472
  7.0 5.8 %collective-permute-start.4 = (bf16[2,9,48,128]{3,2,1,0:T(8,128)(2,1)S(1)}, bf16[2,9,48,128]{3,2,1,0:T(8,128)(2,1)S(1)}, u32[]{:S(2)}, u32[]{:S(2)}) collective-permute-start(bf16[2,9,48,128]{3,2,1,0:T(8,128)(2,1)S(1)} %pad_maximum_fusion.1._.t0), channel_id=1, source_target_pairs={{0,64},{4,196},{8,72},{12,204},{16,80},{20,212},{24,88},{28,220},{... | collective-permute-start | bytes 663560 | tf_op jit(solution)/shard_map/ppermute | solution.py:437
  12.9 0.7 %collective-permute-start.2 = (bf16[2,9,48,128]{3,2,1,0:T(8,128)(2,1)S(1)}, bf16[2,9,48,128]{3,2,1,0:T(8,128)(2,1)S(1)}, u32[]{:S(2)}, u32[]{:S(2)}) collective-permute-start(bf16[2,9,48,128]{3,2,1,0:T(8,128)(2,1)S(1)} %pad_maximum_fusion.1._.t0), channel_id=1, source_target_pairs={{0,32},{4,228},{8,40},{12,236},{16,48},{20,244},{24,56},{28,252},{... | collective-permute-start | bytes 663560 | tf_op jit(solution)/shard_map/ppermute | solution.py:437
  13.6 2.4 %shard_map.103._plan.plan = s32[48]{0:T(128)} custom-call(s32[594]{0:T(1024)} %concatenate.7.table, bf16[2,9,48,128]{3,2,1,0:T(8,128)(2,1)} %copy-done), custom_call_target="tpu_custom_call" | custom-call | tf_op jit(solution)/shard_map/pallas_call | solution.py:488
  16.1 0.9 %copy-done.1 = bf16[2,9,48,128]{3,2,1,0:T(8,128)(2,1)S(1)} copy-done((bf16[2,9,48,128]{3,2,1,0:T(8,128)(2,1)S(1)}, bf16[2,9,48,128]{3,2,1,0:T(8,128)(2,1)}, u32[]{:S(2)}) %copy-start.1) | copy-done | bytes 221208
  17.0 0.6 shard_map.101.weights
  17.6 2.4 %shard_map.102.partial = f32[8,192,256]{2,1,0:T(8,128)S(1)} custom-call(bf16[2,16,96,128]{3,2,1,0:T(8,128)(2,1)S(1)} %bitcast.21, bf16[2,192,3584]{2,1,0:T(8,128)(2,1)S(1)} %shard_map.101.weights, f32[96,4]{1,0:T(8,128)S(1)} %copy.26.vectors), custom_call_target="tpu_custom_call" | custom-call | flops 3000000000 | bytes 1048576 | tf_op jit(solution)/shard_map/pallas_call | solution.py:496
  20.0 0.6 collective-permute-done.2._.t1
  20.7 2.7 %collective-permute-start.5 = (bf16[3,9,48,128]{3,2,1,0:T(8,128)(2,1)S(1)}, bf16[3,9,48,128]{3,2,1,0:T(8,128)(2,1)S(1)}, u32[]{:S(2)}, u32[]{:S(2)}) collective-permute-start(bf16[3,9,48,128]{3,2,1,0:T(8,128)(2,1)S(1)} %pad_maximum_fusion), channel_id=1, source_target_pairs={{0,64},{4,196},{8,72},{12,204},{16,80},{20,212},{24,88},{28,220},{... | collective-permute-start | bytes 995336 | tf_op jit(solution)/shard_map/ppermute | solution.py:437
  23.4 4.3 %shard_map.104.second._.second_own = bf16[37,96,128]{2,1,0:T(8,128)(2,1)S(1)} custom-call(s32[594]{0:T(1024)S(1)} %copy-done.4, bf16[2,16,96,128]{3,2,1,0:T(8,128)(2,1)} %collective-permute-done.prev, f32[8,192,256]{2,1,0:T(8,128)S(1)} %shard_map.102.partial, bf16[2,192,3584]{2,1,0:T(8,128)(2,1)S(1)} %shard_map.101.weights, f32[96,4]{1,0:T(8,128)S(1)} %copy.26.vectors, ...), custom_call_target="tpu_custom_call" | custom-call | flops 8000000000 | bytes 1048576 | tf_op jit(solution)/shard_map/pallas_call | solution.py:499
  27.7 1.3 %collective-permute-start.3 = (bf16[37,96,128]{2,1,0:T(8,128)(2,1)S(1)}, bf16[37,96,128]{2,1,0:T(8,128)(2,1)S(1)}, u32[]{:S(2)}, u32[]{:S(2)}) collective-permute-start(bf16[37,96,128]{2,1,0:T(8,128)(2,1)S(1)} %shard_map.104.second._.second_own), channel_id=1, source_target_pairs={{0,1},{1,2},{2,3},{3,0},{4,5},{5,6},{6,7},{7,4},{8,9},{9,10},{10,1... | collective-permute-start | bytes 2727944 | tf_op jit(solution)/shard_map/ppermute | solution.py:441
  29.0 2.3 %collective-permute-done.5.t3 = bf16[3,9,48,128]{3,2,1,0:T(8,128)(2,1)S(1)} collective-permute-done((bf16[3,9,48,128]{3,2,1,0:T(8,128)(2,1)S(1)}, bf16[3,9,48,128]{3,2,1,0:T(8,128)(2,1)S(1)}, u32[]{:S(2)}, u32[]{:S(2)}) %collective-permute-start.5) | collective-permute-done | bytes 331808 | tf_op jit(solution)/shard_map/ppermute | solution.py:437
  31.3 1.0 %shard_map.106._ = bf16[4,5,96,128]{3,2,1,0:T(8,128)(2,1)S(1)} custom-call(s32[48]{0:T(128)S(1)} %copy-done.6, bf16[2,9,48,128]{3,2,1,0:T(8,128)(2,1)S(1)} %copy-done.1, bf16[2,9,48,128]{3,2,1,0:T(8,128)(2,1)S(1)} %collective-permute-done.2._.t1, bf16[2,9,48,128]{3,2,1,0:T(8,128)(2,1)S(1)} %collective-permute-done.4.t2, ...), custom_call_target="tpu_custom_call" | custom-call | bytes 1048576 | tf_op jit(solution)/shard_map/pallas_call | solution.py:458
  32.4 2.8 %collective-permute-start.6 = (bf16[4,5,96,128]{3,2,1,0:T(8,128)(2,1)S(1)}, bf16[4,5,96,128]{3,2,1,0:T(8,128)(2,1)S(1)}, u32[]{:S(2)}, u32[]{:S(2)}) collective-permute-start(bf16[4,5,96,128]{3,2,1,0:T(8,128)(2,1)S(1)} %shard_map.106._), channel_id=1, source_target_pairs={{0,4},{4,0},{8,12},{12,8},{16,20},{20,16},{24,28},{28,24},{32,36},... | collective-permute-start | bytes 1474568 | tf_op jit(solution)/shard_map/ppermute | solution.py:437
  35.2 1.1 %shard_map.107.mine = bf16[4,5,96,128]{3,2,1,0:T(8,128)(2,1)S(1)} custom-call(s32[48]{0:T(128)S(1)} %copy-done.6, bf16[2,9,48,128]{3,2,1,0:T(8,128)(2,1)S(1)} %copy-done.1, bf16[2,9,48,128]{3,2,1,0:T(8,128)(2,1)S(1)} %collective-permute-done.2._.t1, bf16[2,9,48,128]{3,2,1,0:T(8,128)(2,1)S(1)} %collective-permute-done.4.t2, ...), custom_call_target="tpu_custom_call" | custom-call | bytes 1048576 | tf_op jit(solution)/shard_map/pallas_call | solution.py:460
  36.7 0.7 %shard_map.108 = (bf16[5,96,128]{2,1,0:T(8,128)(2,1)S(1)}, bf16[5,96,128]{2,1,0:T(8,128)(2,1)S(1)}, bf16[5,96,128]{2,1,0:T(8,128)(2,1)S(1)}, bf16[5,96,128]{2,1,0:T(8,128)(2,1)S(1)}) custom-call(s32[594]{0:T(1024)S(1)} %copy-done.4, bf16[4,5,96,128]{3,2,1,0:T(8,128)(2,1)S(1)} %shard_map.107.mine, bf16[4,5,96,128]{3,2,1,0:T(8,128)(2,1)S(1)} %collective-permute-done.6.arrived), custom_call_target="tpu_custom_call" | custom-call | bytes 1048576 | tf_op jit(solution)/shard_map/pallas_call | solution.py:461
  37.4 3.0 %collective-permute-start.7 = (bf16[5,96,128]{2,1,0:T(8,128)(2,1)S(1)}, bf16[5,96,128]{2,1,0:T(8,128)(2,1)S(1)}, u32[]{:S(2)}, u32[]{:S(2)}) collective-permute-start(bf16[5,96,128]{2,1,0:T(8,128)(2,1)S(1)} %get-tuple-element.15), channel_id=1, source_target_pairs={{0,16},{4,20},{8,24},{12,28},{16,0},{20,4},{24,8},{28,12},{32,48},... | collective-permute-start | bytes 368648 | tf_op jit(solution)/shard_map/ppermute | solution.py:437
  40.8 2.3 %collective-permute-start.9 = (bf16[5,96,128]{2,1,0:T(8,128)(2,1)S(1)}, bf16[5,96,128]{2,1,0:T(8,128)(2,1)S(1)}, u32[]{:S(2)}, u32[]{:S(2)}) collective-permute-start(bf16[5,96,128]{2,1,0:T(8,128)(2,1)S(1)} %get-tuple-element.17), channel_id=1, source_target_pairs={{0,24},{4,28},{8,0},{12,4},{16,8},{20,12},{24,16},{28,20},{32,56},... | collective-permute-start | bytes 368648 | tf_op jit(solution)/shard_map/ppermute | solution.py:437
  43.1 1.8 %shard_map.105.partial = f32[2,16,96,128]{3,2,1,0:T(8,128)S(1)} custom-call(bf16[2,16,96,128]{3,2,1,0:T(8,128)(2,1)S(1)} %bitcast.22, bf16[37,96,128]{2,1,0:T(8,128)(2,1)S(1)} %shard_map.104.second._.second_own, bf16[2,192,3584]{2,1,0:T(8,128)(2,1)S(1)} %shard_map.101.weights, f32[96,4]{1,0:T(8,128)S(1)} %copy.26.vectors), custom_call_target="tpu_custom_call" | custom-call | flops 1000000000 | bytes 1048576 | tf_op jit(solution)/shard_map/pallas_call | solution.py:503
  44.9 1.7 %collective-permute-done.8 = bf16[5,96,128]{2,1,0:T(8,128)(2,1)S(1)} collective-permute-done((bf16[5,96,128]{2,1,0:T(8,128)(2,1)S(1)}, bf16[5,96,128]{2,1,0:T(8,128)(2,1)S(1)}, u32[]{:S(2)}, u32[]{:S(2)}) %collective-permute-start.8) | collective-permute-done | bytes 122912 | tf_op jit(solution)/shard_map/ppermute | solution.py:437
  46.6 1.3 %collective-permute-start.11 = (bf16[5,96,128]{2,1,0:T(8,128)(2,1)S(1)}, bf16[5,96,128]{2,1,0:T(8,128)(2,1)S(1)}, u32[]{:S(2)}, u32[]{:S(2)}) collective-permute-start(bf16[5,96,128]{2,1,0:T(8,128)(2,1)S(1)} %add_convert_fusion._.halo), channel_id=1, source_target_pairs={{0,1},{1,2},{2,3},{3,0},{4,5},{5,6},{6,7},{7,4},{8,9},{9,10},{10,1... | collective-permute-start | bytes 368648 | tf_op jit(solution)/shard_map/ppermute | solution.py:441
  47.9 1.6 %collective-permute-start.10 = (bf16[5,96,128]{2,1,0:T(8,128)(2,1)S(1)}, bf16[5,96,128]{2,1,0:T(8,128)(2,1)S(1)}, u32[]{:S(2)}, u32[]{:S(2)}) collective-permute-start(bf16[5,96,128]{2,1,0:T(8,128)(2,1)S(1)} %add_convert_fusion._.halo), channel_id=1, source_target_pairs={{0,2},{1,3},{2,0},{3,1},{4,6},{5,7},{6,4},{7,5},{8,10},{9,11},{10,... | collective-permute-start | bytes 368648 | tf_op jit(solution)/shard_map/ppermute | solution.py:441
  49.5 1.3 %collective-permute-done.3.second_prev = bf16[37,96,128]{2,1,0:T(8,128)(2,1)S(1)} collective-permute-done((bf16[37,96,128]{2,1,0:T(8,128)(2,1)S(1)}, bf16[37,96,128]{2,1,0:T(8,128)(2,1)S(1)}, u32[]{:S(2)}, u32[]{:S(2)}) %collective-permute-start.3) | collective-permute-done | bytes 909344 | tf_op jit(solution)/shard_map/ppermute | solution.py:441
  50.8 2.4 %shard_map.109._.inner = f32[2,16,96,128]{3,2,1,0:T(8,128)S(1)} custom-call(s32[594]{0:T(1024)S(1)} %copy-done.4, f32[2,16,96,128]{3,2,1,0:T(8,128)S(1)} %shard_map.105.partial, bf16[37,96,128]{2,1,0:T(8,128)(2,1)S(1)} %collective-permute-done.3.second_prev, bf16[2,192,3584]{2,1,0:T(8,128)(2,1)S(1)} %shard_map.101.weights, ...), custom_call_target="tpu_custom_call" | custom-call | flops 12000000000 | bytes 1048576 | tf_op jit(solution)/shard_map/pallas_call | solution.py:507
  53.1 1.3 %shard_map.110 = (bf16[2,4,288,128]{3,2,1,0:T(8,128)(2,1)S(1)}, bf16[2,4,3,96,128]{4,3,2,1,0:T(8,128)(2,1)S(1)}) custom-call(s32[594]{0:T(1024)S(1)} %copy-done.4, bf16[5,96,128]{2,1,0:T(8,128)(2,1)S(1)} %get-tuple-element.18.record, bf16[5,96,128]{2,1,0:T(8,128)(2,1)S(1)} %add_convert_fusion._.halo, f32[96,4]{1,0:T(8,128)S(1)} %copy.26.vectors, ...), custom_call_target="tpu_custom_call" | custom-call | bytes 1048576 | tf_op jit(solution)/shard_map/pallas_call | solution.py:511
  54.4 1.0 %collective-permute-done.10.halo2 = bf16[5,96,128]{2,1,0:T(8,128)(2,1)S(1)} collective-permute-done((bf16[5,96,128]{2,1,0:T(8,128)(2,1)S(1)}, bf16[5,96,128]{2,1,0:T(8,128)(2,1)S(1)}, u32[]{:S(2)}, u32[]{:S(2)}) %collective-permute-start.10) | collective-permute-done | bytes 122912 | tf_op jit(solution)/shard_map/ppermute | solution.py:441
  55.4 4.9 %shard_map.111 = bf16[2,16,96,128]{3,2,1,0:T(8,128)(2,1)S(1)} custom-call(s32[594]{0:T(1024)S(1)} %copy-done.4, f32[2,16,96,128]{3,2,1,0:T(8,128)S(1)} %shard_map.109._.inner, bf16[2,4,288,128]{3,2,1,0:T(8,128)(2,1)S(1)} %get-tuple-element.19.band0, bf16[2,4,3,96,128]{4,3,2,1,0:T(8,128)(2,1)S(1)} %get-tuple-element.20.columns0, ...), custom_call_target="tpu_custom_call" | custom-call | flops 4000000000 | bytes 1048576 | tf_op jit(solution)/shard_map/pallas_call | solution.py:512
  60.3 1.2 %copy.31 = bf16[1,2,96,16,128]{4,3,2,1,0:T(8,128)(2,1)} copy(bf16[1,2,96,16,128]{4,2,3,1,0:T(8,128)(2,1)S(1)} %bitcast.23) | data formatting | bytes 1572864 | tf_op jit(solution)/shard_map/broadcast_in_dim | solution.py:521
  (42 shorter events, 1.4 us)
Async XLA Ops:
  0.0 3.7 %copy-start.7 = (s32[64]{0:T(128)S(1)}, s32[64]{0:T(128)}, u32[]{:S(2)}) copy-start(s32[64]{0:T(128)} %tiles.1) | copy-start | bytes 772
  0.0 3.7 %copy-start.5 = (s32[64,8]{0,1:T(8,128)S(1)}, s32[64,8]{0,1:T(8,128)}, u32[]{:S(2)}) copy-start(s32[64,8]{0,1:T(8,128)} %param.12) | copy-start | bytes 6148
  0.0 6.2 %copy-start.9 = (f32[96]{0:T(128)S(1)}, f32[96]{0:T(128)}, u32[]{:S(2)}) copy-start(f32[96]{0:T(128)} %param.19) | copy-start | bytes 1156
  0.0 6.2 %copy-start.10 = (f32[96]{0:T(128)S(1)}, f32[96]{0:T(128)}, u32[]{:S(2)}) copy-start(f32[96]{0:T(128)} %param.17) | copy-start | bytes 1156
  0.0 6.2 %copy-start.12 = (f32[96]{0:T(128)S(1)}, f32[96]{0:T(128)}, u32[]{:S(2)}) copy-start(f32[96]{0:T(128)} %param.16) | copy-start | bytes 1156
  0.0 6.2 %copy-start.11 = (f32[96]{0:T(128)S(1)}, f32[96]{0:T(128)}, u32[]{:S(2)}) copy-start(f32[96]{0:T(128)} %param.14) | copy-start | bytes 1156
  0.0 6.3 %copy-start.8 = (s32[16]{0:T(128)S(1)}, s32[16]{0:T(128)}, u32[]{:S(2)}) copy-start(s32[16]{0:T(128)} %param.13) | copy-start | bytes 196
  0.0 16.0 %copy-start.3 = (bf16[3,3,3,96,96]{4,3,2,1,0:T(8,128)(2,1)S(1)}, bf16[3,3,3,96,96]{4,3,2,1,0:T(8,128)(2,1)}, u32[]{:S(2)}) copy-start(bf16[3,3,3,96,96]{4,3,2,1,0:T(8,128)(2,1)} %param.18) | copy-start | bytes 1492996
  0.1 16.0 %copy-start.2 = (bf16[3,3,3,96,96]{4,3,2,1,0:T(8,128)(2,1)S(1)}, bf16[3,3,3,96,96]{4,3,2,1,0:T(8,128)(2,1)}, u32[]{:S(2)}) copy-start(bf16[3,3,3,96,96]{4,3,2,1,0:T(8,128)(2,1)} %param.15) | copy-start | bytes 1492996
  1.5 21.9 %collective-permute-start = (bf16[2,16,96,128]{3,2,1,0:T(8,128)(2,1)S(1)}, bf16[2,16,96,128]{3,2,1,0:T(8,128)(2,1)}, u32[]{:S(2)}, u32[]{:S(2)}) collective-permute-start(bf16[2,16,96,128]{3,2,1,0:T(8,128)(2,1)S(1)} %bitcast.19), channel_id=1, source_target_pairs={{0,1},{1,2},{2,3},{3,0},{4,5},{5,6},{6,7},{7,4},{8,9},{9,10},{10,1... | collective-permute-start | bytes 2359304 | tf_op jit(solution)/shard_map/ppermute | solution.py:441
  4.7 2.3 %collective-permute-start.1 = (bf16[9,48,128]{2,1,0:T(8,128)(2,1)S(1)}, bf16[9,48,128]{2,1,0:T(8,128)(2,1)S(1)}, u32[]{:S(2)}, u32[]{:S(2)}) collective-permute-start(bf16[9,48,128]{2,1,0:T(8,128)(2,1)S(1)} %get-tuple-element.13), channel_id=1, source_target_pairs={{0,4},{4,0},{8,12},{12,8},{16,20},{20,16},{24,28},{28,24},{32,36},... | collective-permute-start | bytes 331784 | tf_op jit(solution)/shard_map/ppermute | solution.py:437
  7.0 6.6 %copy-start = (bf16[2,9,48,128]{3,2,1,0:T(8,128)(2,1)}, bf16[2,9,48,128]{3,2,1,0:T(8,128)(2,1)S(1)}, u32[]{:S(2)}) copy-start(bf16[2,9,48,128]{3,2,1,0:T(8,128)(2,1)S(1)} %pad_maximum_fusion.1._.t0) | copy-start | bytes 663556
  7.0 13.0 %collective-permute-start.4 = (bf16[2,9,48,128]{3,2,1,0:T(8,128)(2,1)S(1)}, bf16[2,9,48,128]{3,2,1,0:T(8,128)(2,1)S(1)}, u32[]{:S(2)}, u32[]{:S(2)}) collective-permute-start(bf16[2,9,48,128]{3,2,1,0:T(8,128)(2,1)S(1)} %pad_maximum_fusion.1._.t0), channel_id=1, source_target_pairs={{0,64},{4,196},{8,72},{12,204},{16,80},{20,212},{24,88},{28,220},{... | collective-permute-start | bytes 663560 | tf_op jit(solution)/shard_map/ppermute | solution.py:437
  12.9 7.7 %collective-permute-start.2 = (bf16[2,9,48,128]{3,2,1,0:T(8,128)(2,1)S(1)}, bf16[2,9,48,128]{3,2,1,0:T(8,128)(2,1)S(1)}, u32[]{:S(2)}, u32[]{:S(2)}) collective-permute-start(bf16[2,9,48,128]{3,2,1,0:T(8,128)(2,1)S(1)} %pad_maximum_fusion.1._.t0), channel_id=1, source_target_pairs={{0,32},{4,228},{8,40},{12,236},{16,48},{20,244},{24,56},{28,252},{... | collective-permute-start | bytes 663560 | tf_op jit(solution)/shard_map/ppermute | solution.py:437
  16.1 0.9 %copy-start.1 = (bf16[2,9,48,128]{3,2,1,0:T(8,128)(2,1)S(1)}, bf16[2,9,48,128]{3,2,1,0:T(8,128)(2,1)}, u32[]{:S(2)}) copy-start(bf16[2,9,48,128]{3,2,1,0:T(8,128)(2,1)} %copy-done) | copy-start | bytes 663556
  17.6 5.8 %copy-start.4 = (s32[594]{0:T(1024)S(1)}, s32[594]{0:T(1024)}, u32[]{:S(2)}) copy-start(s32[594]{0:T(1024)} %concatenate.7.table) | copy-start | bytes 7132
  17.6 5.8 %copy-start.6 = (s32[48]{0:T(128)S(1)}, s32[48]{0:T(128)}, u32[]{:S(2)}) copy-start(s32[48]{0:T(128)} %shard_map.103._plan.plan) | copy-start | bytes 580
  20.7 10.7 %collective-permute-start.5 = (bf16[3,9,48,128]{3,2,1,0:T(8,128)(2,1)S(1)}, bf16[3,9,48,128]{3,2,1,0:T(8,128)(2,1)S(1)}, u32[]{:S(2)}, u32[]{:S(2)}) collective-permute-start(bf16[3,9,48,128]{3,2,1,0:T(8,128)(2,1)S(1)} %pad_maximum_fusion), channel_id=1, source_target_pairs={{0,64},{4,196},{8,72},{12,204},{16,80},{20,212},{24,88},{28,220},{... | collective-permute-start | bytes 995336 | tf_op jit(solution)/shard_map/ppermute | solution.py:437
  27.7 23.0 %collective-permute-start.3 = (bf16[37,96,128]{2,1,0:T(8,128)(2,1)S(1)}, bf16[37,96,128]{2,1,0:T(8,128)(2,1)S(1)}, u32[]{:S(2)}, u32[]{:S(2)}) collective-permute-start(bf16[37,96,128]{2,1,0:T(8,128)(2,1)S(1)} %shard_map.104.second._.second_own), channel_id=1, source_target_pairs={{0,1},{1,2},{2,3},{3,0},{4,5},{5,6},{6,7},{7,4},{8,9},{9,10},{10,1... | collective-permute-start | bytes 2727944 | tf_op jit(solution)/shard_map/ppermute | solution.py:441
  32.4 4.3 %collective-permute-start.6 = (bf16[4,5,96,128]{3,2,1,0:T(8,128)(2,1)S(1)}, bf16[4,5,96,128]{3,2,1,0:T(8,128)(2,1)S(1)}, u32[]{:S(2)}, u32[]{:S(2)}) collective-permute-start(bf16[4,5,96,128]{3,2,1,0:T(8,128)(2,1)S(1)} %shard_map.106._), channel_id=1, source_target_pairs={{0,4},{4,0},{8,12},{12,8},{16,20},{20,16},{24,28},{28,24},{32,36},... | collective-permute-start | bytes 1474568 | tf_op jit(solution)/shard_map/ppermute | solution.py:437
  37.4 7.5 %collective-permute-start.7 = (bf16[5,96,128]{2,1,0:T(8,128)(2,1)S(1)}, bf16[5,96,128]{2,1,0:T(8,128)(2,1)S(1)}, u32[]{:S(2)}, u32[]{:S(2)}) collective-permute-start(bf16[5,96,128]{2,1,0:T(8,128)(2,1)S(1)} %get-tuple-element.15), channel_id=1, source_target_pairs={{0,16},{4,20},{8,24},{12,28},{16,0},{20,4},{24,8},{28,12},{32,48},... | collective-permute-start | bytes 368648 | tf_op jit(solution)/shard_map/ppermute | solution.py:437
  40.4 6.1 %collective-permute-start.8 = (bf16[5,96,128]{2,1,0:T(8,128)(2,1)S(1)}, bf16[5,96,128]{2,1,0:T(8,128)(2,1)S(1)}, u32[]{:S(2)}, u32[]{:S(2)}) collective-permute-start(bf16[5,96,128]{2,1,0:T(8,128)(2,1)S(1)} %get-tuple-element.16), channel_id=1, source_target_pairs={{0,8},{4,12},{8,16},{12,20},{16,24},{20,28},{24,0},{28,4},{32,40},... | collective-permute-start | bytes 368648 | tf_op jit(solution)/shard_map/ppermute | solution.py:437
  40.8 5.8 %collective-permute-start.9 = (bf16[5,96,128]{2,1,0:T(8,128)(2,1)S(1)}, bf16[5,96,128]{2,1,0:T(8,128)(2,1)S(1)}, u32[]{:S(2)}, u32[]{:S(2)}) collective-permute-start(bf16[5,96,128]{2,1,0:T(8,128)(2,1)S(1)} %get-tuple-element.17), channel_id=1, source_target_pairs={{0,24},{4,28},{8,0},{12,4},{16,8},{20,12},{24,16},{28,20},{32,56},... | collective-permute-start | bytes 368648 | tf_op jit(solution)/shard_map/ppermute | solution.py:437
  46.6 7.8 %collective-permute-start.11 = (bf16[5,96,128]{2,1,0:T(8,128)(2,1)S(1)}, bf16[5,96,128]{2,1,0:T(8,128)(2,1)S(1)}, u32[]{:S(2)}, u32[]{:S(2)}) collective-permute-start(bf16[5,96,128]{2,1,0:T(8,128)(2,1)S(1)} %add_convert_fusion._.halo), channel_id=1, source_target_pairs={{0,1},{1,2},{2,3},{3,0},{4,5},{5,6},{6,7},{7,4},{8,9},{9,10},{10,1... | collective-permute-start | bytes 368648 | tf_op jit(solution)/shard_map/ppermute | solution.py:441
  47.9 7.5 %collective-permute-start.10 = (bf16[5,96,128]{2,1,0:T(8,128)(2,1)S(1)}, bf16[5,96,128]{2,1,0:T(8,128)(2,1)S(1)}, u32[]{:S(2)}, u32[]{:S(2)}) collective-permute-start(bf16[5,96,128]{2,1,0:T(8,128)(2,1)S(1)} %add_convert_fusion._.halo), channel_id=1, source_target_pairs={{0,2},{1,3},{2,0},{3,1},{4,6},{5,7},{6,4},{7,5},{8,10},{9,11},{10,... | collective-permute-start | bytes 368648 | tf_op jit(solution)/shard_map/ppermute | solution.py:441
